TPU v7x, 32 devices: a whole 2x2x4 slice. The times are simulated.
32 devices in a mesh: dp: 4 (over y, x), fsdp: 8 (over z, core).
Axes of the slice: x: 2, y: 2, z: 4, core: 2. Of those that a mesh axis runs over, the one named last changes fastest.
Arguments:
- tok_ids: int32 [64, 512], P(('dp', 'fsdp')), may hold values from 0 to 30591
- segments: int32 [64, 512], P(('dp', 'fsdp')), may hold values from 0 to 1, as said below
- seq_len: int32 [64], P(('dp', 'fsdp')), may hold values from 0 to 512, as said below
- label_pos: int32 [64, 64], P(('dp', 'fsdp')), may hold values from 1 to 511, as said below
- label_ids: int32 [64, 64], P(('dp', 'fsdp')), may hold values from 0 to 30591
- table: float32 [30592, 768], P(('dp', 'fsdp')), may hold values from -0.4375 to 0.4375
- w_qkv: float32 [768, 2304], P(('dp', 'fsdp')), may hold values from -0.21875 to 0.21875
- w_out: float32 [768, 768], P(('dp', 'fsdp')), may hold values from -0.875 to 0.875
- w_up: float32 [768, 3072], P(('dp', 'fsdp')), may hold values from -0.21875 to 0.21875
- w_down: float32 [3072, 768], P(('dp', 'fsdp')), may hold values from -0.109375 to 0.109375
- small: float32 [16, 768], P(None, ('dp', 'fsdp'))
- position: float32 [512, 768], P(None, ('dp', 'fsdp')), may hold values from -0.4375 to 0.4375
- t_table: bfloat16 [30592, 768], P(('dp', 'fsdp')), may hold values from -0.4375 to 0.4375
- t_qkv: bfloat16 [768, 2304], P(('dp', 'fsdp')), may hold values from -0.21875 to 0.21875
- t_out: bfloat16 [768, 768], P(('dp', 'fsdp')), may hold values from -0.875 to 0.875
- t_up: bfloat16 [768, 3072], P(('dp', 'fsdp')), may hold values from -0.21875 to 0.21875
- t_down: bfloat16 [3072, 768], P(('dp', 'fsdp')), may hold values from -0.109375 to 0.109375
- t_small: bfloat16 [16, 768], P(None, ('dp', 'fsdp'))
- t_position: bfloat16 [512, 768], P(None, ('dp', 'fsdp')), may hold values from -0.4375 to 0.4375
- mom_table: float32 [30592, 768], P(('dp', 'fsdp')), may hold values from -2.0861626e-07 to 2.0861626e-07
- mom_qkv: float32 [768, 2304], P(('dp', 'fsdp')), may hold values from -2.0861626e-07 to 2.0861626e-07
- mom_out: float32 [768, 768], P(('dp', 'fsdp')), may hold values from -2.0861626e-07 to 2.0861626e-07
- mom_up: float32 [768, 3072], P(('dp', 'fsdp')), may hold values from -2.0861626e-07 to 2.0861626e-07
- mom_down: float32 [3072, 768], P(('dp', 'fsdp')), may hold values from -2.0861626e-07 to 2.0861626e-07
- mom_small: float32 [16, 768], P(None, ('dp', 'fsdp')), may hold values from -2.0861626e-07 to 2.0861626e-07
- mom_position: float32 [512, 768], P(None, ('dp', 'fsdp')), may hold values from -2.0861626e-07 to 2.0861626e-07
- avg_table: float32 [30592, 768], P(('dp', 'fsdp')), may hold values from -0.4375 to 0.4375
- avg_qkv: float32 [768, 2304], P(('dp', 'fsdp')), may hold values from -0.21875 to 0.21875
- avg_out: float32 [768, 768], P(('dp', 'fsdp')), may hold values from -0.875 to 0.875
- avg_up: float32 [768, 3072], P(('dp', 'fsdp')), may hold values from -0.21875 to 0.21875
- avg_down: float32 [3072, 768], P(('dp', 'fsdp')), may hold values from -0.109375 to 0.109375
- avg_small: float32 [16, 768], P(None, ('dp', 'fsdp'))
- avg_position: float32 [512, 768], P(None, ('dp', 'fsdp')), may hold values from -0.4375 to 0.4375
Outputs:
- new_table: float32 [30592, 768], P(('dp', 'fsdp'))
- new_qkv: float32 [768, 2304], P(('dp', 'fsdp'))
- new_out: float32 [768, 768], P(('dp', 'fsdp'))
- new_up: float32 [768, 3072], P(('dp', 'fsdp'))
- new_down: float32 [3072, 768], P(('dp', 'fsdp'))
- new_small: float32 [16, 768], P(None, ('dp', 'fsdp'))
- new_position: float32 [512, 768], P(None, ('dp', 'fsdp'))
- moment_table: float32 [30592, 768], P(('dp', 'fsdp'))
- moment_qkv: float32 [768, 2304], P(('dp', 'fsdp'))
- moment_out: float32 [768, 768], P(('dp', 'fsdp'))
- moment_up: float32 [768, 3072], P(('dp', 'fsdp'))
- moment_down: float32 [3072, 768], P(('dp', 'fsdp'))
- moment_small: float32 [16, 768], P(None, ('dp', 'fsdp'))
- moment_position: float32 [512, 768], P(None, ('dp', 'fsdp'))
- average_table: float32 [30592, 768], P(('dp', 'fsdp'))
- average_qkv: float32 [768, 2304], P(('dp', 'fsdp'))
- average_out: float32 [768, 768], P(('dp', 'fsdp'))
- average_up: float32 [768, 3072], P(('dp', 'fsdp'))
- average_down: float32 [3072, 768], P(('dp', 'fsdp'))
- average_small: float32 [16, 768], P(None, ('dp', 'fsdp'))
- average_position: float32 [512, 768], P(None, ('dp', 'fsdp'))
- grad_norm: float32 [], replicated
- loss_value: float32 [], replicated
Inputs may be any that keep to these rules, and one draw needn't show every extreme that they name: `seq_len`: A length of 0 marks an empty slot; the first of each device's 2 slots is never empty; some sequence has 512 tokens; live lengths are at least 256. `label_pos`: each labeled position lies from 1 to its slot's length minus one (is 1 in an empty slot). `segments`: each row is 0 up to some position from 1 to 511 and 1 from there on.
All inputs are finite; a program needn't handle non-finite values.
Results may differ from a plain program's by a relative error of at most 0.011.
Values may be sent and summed in bfloat16 or wider, within the bound.
A program may use at most 384 MiB of HBM per device.

v0:
```python
import math

import jax
import jax.numpy as jnp
from jax import lax
from jax.sharding import PartitionSpec as P

HD = 64
NPARAM = 30978048


SOFTMAX_HEAT = 2.0
SOFT_FRACTION = 0.5
PKD_WEIGHT = 10.0
MOMENTUM = 0.9
AVERAGE = 0.75
CLIP = 0.002
RATE_SCALE = 20.0
EPSILON = 1e-12
NEGATIVE = -1e30


def merged_2(shard, axis, combine):
    everything = jax.tree.map(lambda part: lax.all_gather(part, axis), shard)
    leading = jax.tree.map(lambda part: part[0], everything)

    def turn(k, so_far):
        return combine(so_far, jax.tree.map(lambda part: part[k], everything))

    return lax.fori_loop(1, lax.axis_size(axis), turn, leading)


def product_of(form, left, right):
    return jnp.einsum(form, left, right, preferred_element_type=jnp.float32)


def owned(ids, share, groups, own):
    block = ids // share
    inside = block % groups == own
    local = block // groups * share + ids % share
    return (inside, jnp.where(inside, local, 0))


def layer_norm_keep(value, gain, shift):
    mean = jnp.mean(value, axis=-1, keepdims=True)
    centred = value - mean
    inverse = lax.rsqrt(jnp.mean(centred * centred, axis=-1, keepdims=True) + EPSILON)
    normed = centred * inverse
    return (normed * gain + shift, normed, inverse)


def layer_norm_back(grad, normed, inverse, gain):
    gain_grad = jnp.sum(grad * normed, axis=0)
    shift_grad = jnp.sum(grad, axis=0)
    scaled = grad * gain
    centred = scaled - jnp.mean(scaled, axis=-1, keepdims=True)
    return (
        inverse * (centred - normed * jnp.mean(scaled * normed, axis=-1, keepdims=True)),
        gain_grad,
        shift_grad,
    )


def gelu_parts(upward):
    normal_cdf = 0.5 * (1.0 + lax.erf(upward * 0.7071067811865476))
    density = jnp.exp(-0.5 * upward * upward) * 0.3989422804014327
    return (upward * normal_cdf, normal_cdf + upward * density)


def label_valid(lengths, labels, span):
    needed = (lengths * labels + span - 1) // span
    return (jnp.arange(labels)[None, :] < needed[:, None]).astype(jnp.float32)


def masked_scores(queries, keys, length):
    raw = product_of("qhd,khd->hqk", queries, keys)
    keep = jnp.arange(keys.shape[0]) < jnp.maximum(length, 1)
    return jnp.where(keep[None, None, :], raw * 0.125, NEGATIVE)


def gather_layer(weights):
    return (
        lax.all_gather(weights[0], ("dp", "fsdp"), axis=0, tiled=True),
        lax.all_gather(weights[1], ("dp", "fsdp"), axis=0, tiled=True),
        lax.all_gather(weights[2], ("dp", "fsdp"), axis=0, tiled=True),
        lax.all_gather(weights[3], ("dp", "fsdp"), axis=0, tiled=True),
        lax.all_gather(weights[4], ("dp", "fsdp"), axis=1, tiled=True),
        lax.all_gather(weights[5], ("dp", "fsdp"), axis=1, tiled=True),
    )


def reduce_layer(grads):
    return (
        lax.psum_scatter(grads[0], ("dp", "fsdp"), scatter_dimension=0, tiled=True),
        lax.psum_scatter(grads[1], ("dp", "fsdp"), scatter_dimension=0, tiled=True),
        lax.psum_scatter(grads[2], ("dp", "fsdp"), scatter_dimension=0, tiled=True),
        lax.psum_scatter(grads[3], ("dp", "fsdp"), scatter_dimension=0, tiled=True),
        lax.psum_scatter(grads[4], ("dp", "fsdp"), scatter_dimension=1, tiled=True),
        lax.psum_scatter(grads[5], ("dp", "fsdp"), scatter_dimension=1, tiled=True),
    )


def embed_forward(token_rows, weights, segment_ids):
    small = weights[4].astype(jnp.float32)
    position = weights[5].astype(jnp.float32)
    segment_rows = jnp.where(segment_ids[:, None] == 0, small[14], small[15])
    return layer_norm_keep(token_rows + position + segment_rows, small[12], small[13])


def layer_forward(value, weights, length):
    w_qkv, w_out, w_up, w_down, small_low = weights[:5]
    small = small_low.astype(jnp.float32)
    rows, width = value.shape
    heads = width // HD
    value_low = value.astype(jnp.bfloat16)
    bias = jnp.concatenate([small[0], jnp.zeros_like(small[0]), small[1]])
    joined = (jnp.dot(value_low, w_qkv, preferred_element_type=jnp.float32) + bias).astype(
        jnp.bfloat16
    )
    split = joined.reshape(rows, 3, heads, HD)
    scores = masked_scores(split[:, 0], split[:, 1], length)
    top = jnp.max(scores, axis=-1, keepdims=True)
    exponent = jnp.exp(scores - top)
    total = jnp.sum(exponent, axis=-1, keepdims=True)
    probs = (exponent / total).astype(jnp.bfloat16)
    logsum = top + jnp.log(total)
    context = (
        product_of("hqk,khd->qhd", probs, split[:, 2]).reshape(rows, width).astype(jnp.bfloat16)
    )
    attn = jnp.dot(context, w_out, preferred_element_type=jnp.float32) + small[2]
    first, normed_first, inverse_first = layer_norm_keep(value + attn, small[8], small[9])
    first_low = first.astype(jnp.bfloat16)
    upward = jnp.dot(first_low, w_up, preferred_element_type=jnp.float32) + small[3:7].reshape(-1)
    act, slope = gelu_parts(upward)
    act_low = act.astype(jnp.bfloat16)
    down = jnp.dot(act_low, w_down, preferred_element_type=jnp.float32) + small[7]
    out, normed_second, inverse_second = layer_norm_keep(first + down, small[10], small[11])
    return (
        out,
        (
            value_low,
            joined,
            logsum,
            context,
            normed_first,
            inverse_first,
            first_low,
            slope,
            act_low,
            normed_second,
            inverse_second,
        ),
    )


def layer_backward(grad, weights, kept, length):
    w_qkv, w_out, w_up, w_down, small_low = weights[:5]
    small = small_low.astype(jnp.float32)
    (
        value_low,
        joined,
        logsum,
        context,
        normed_first,
        inverse_first,
        first_low,
        slope,
        act_low,
        normed_second,
        inverse_second,
    ) = kept
    rows, width = value_low.shape
    heads = width // HD
    d_second, gain_second, shift_second = layer_norm_back(
        grad, normed_second, inverse_second, small[10]
    )
    d_down = d_second.astype(jnp.bfloat16)
    g_down = product_of("sf,sd->fd", act_low, d_down)
    d_up = (product_of("sd,fd->sf", d_down, w_down) * slope).astype(jnp.bfloat16)
    g_up = product_of("sd,sf->df", first_low, d_up)
    d_first = d_second + product_of("sf,df->sd", d_up, w_up)
    d_sum, gain_first, shift_first = layer_norm_back(d_first, normed_first, inverse_first, small[8])
    d_attn = d_sum.astype(jnp.bfloat16)
    g_out = product_of("sc,sd->cd", context, d_attn)
    d_context = product_of("sd,cd->sc", d_attn, w_out).astype(jnp.bfloat16).reshape(rows, heads, HD)
    split = joined.reshape(rows, 3, heads, HD)
    probs = jnp.exp(masked_scores(split[:, 0], split[:, 1], length) - logsum)
    g_values = product_of("hqk,qhd->khd", probs.astype(jnp.bfloat16), d_context)
    d_probs = product_of("qhd,khd->hqk", d_context, split[:, 2])
    d_scores = (probs * (d_probs - jnp.sum(probs * d_probs, axis=-1, keepdims=True))).astype(
        jnp.bfloat16
    )
    g_queries = product_of("hqk,khd->qhd", d_scores, split[:, 1]) * 0.125
    g_keys = product_of("hqk,qhd->khd", d_scores, split[:, 0]) * 0.125
    d_joined = (
        jnp.stack([g_queries, g_keys, g_values], axis=1)
        .reshape(rows, 3 * width)
        .astype(jnp.bfloat16)
    )
    g_qkv = product_of("sd,sf->df", value_low, d_joined)
    d_value = d_sum + product_of("sf,df->sd", d_joined, w_qkv)
    joined_sum = jnp.sum(d_joined.astype(jnp.float32), axis=0)
    rows_grad = jnp.concatenate(
        [
            joined_sum[:width][None],
            joined_sum[2 * width :][None],
            jnp.sum(d_attn.astype(jnp.float32), axis=0)[None],
            jnp.sum(d_up.astype(jnp.float32), axis=0).reshape(-1, width),
            jnp.sum(d_down.astype(jnp.float32), axis=0)[None],
            gain_first[None],
            shift_first[None],
            gain_second[None],
            shift_second[None],
        ]
    )
    return ((g_qkv, g_out, g_up, g_down), rows_grad, d_value)


def merge_stats(first, second):
    result = []
    for start, count in ((0, 2), (2, 2), (4, 3)):
        top = jnp.maximum(first[start], second[start])
        scale_first = jnp.exp(first[start] - top)
        scale_second = jnp.exp(second[start] - top)
        result.append(top)
        for offset in range(1, count):
            result.append(
                first[start + offset] * scale_first + second[start + offset] * scale_second
            )
    result.append(first[7] + second[7])
    return tuple(result)


def label_head(
    student_out, teacher_out, places, tables, targets, valid_mask, own, share, groups, label_count
):
    table_student, table_teacher = tables
    vocab_rows = table_student.shape[0]
    labels = places.shape[0]
    rows_student = student_out[places].astype(jnp.bfloat16)
    rows_teacher = teacher_out[places].astype(jnp.bfloat16)
    all_student, all_teacher = (
        lax.all_gather(rows_student, "fsdp", axis=0, tiled=True),
        lax.all_gather(rows_teacher, "fsdp", axis=0, tiled=True),
    )
    student_scores = product_of("pd,vd->pv", all_student, table_student)
    teacher_scores = product_of("pd,vd->pv", all_teacher, table_teacher)
    student_scaled_logits = student_scores / SOFTMAX_HEAT
    teacher_scaled_logits = teacher_scores / SOFTMAX_HEAT
    top_plain = jnp.max(student_scores, axis=1)
    sum_plain = jnp.sum(jnp.exp(student_scores - top_plain[:, None]), axis=1)
    top_soft = jnp.max(student_scaled_logits, axis=1)
    sum_soft = jnp.sum(jnp.exp(student_scaled_logits - top_soft[:, None]), axis=1)
    top_teacher = jnp.max(teacher_scaled_logits, axis=1)
    teacher_exp = jnp.exp(teacher_scaled_logits - top_teacher[:, None])
    sum_teacher = jnp.sum(teacher_exp, axis=1)
    cross_teacher = jnp.sum(teacher_exp * (teacher_scaled_logits - student_scaled_logits), axis=1)
    inside, local_target = owned(targets, share, groups, own)
    picked = jnp.take_along_axis(student_scores, local_target[:, None], axis=1)[:, 0]
    target_logit = jnp.where(inside, picked, 0.0)
    merged = merged_2(
        (
            top_plain,
            sum_plain,
            top_soft,
            sum_soft,
            top_teacher,
            sum_teacher,
            cross_teacher,
            target_logit,
        ),
        "fsdp",
        merge_stats,
    )
    lse_plain = merged[0] + jnp.log(merged[1])
    lse_soft = merged[2] + jnp.log(merged[3])
    lse_teacher = merged[4] + jnp.log(merged[5])
    cross_entropy = lse_plain - merged[7]
    divergence_loss = merged[6] / merged[5] - lse_teacher + lse_soft
    share_lab = valid_mask / label_count
    onehot = ((jnp.arange(vocab_rows)[None, :] == local_target[:, None]) & inside[:, None]).astype(
        jnp.float32
    )
    hard_loss_part = jnp.exp(student_scores - lse_plain[:, None]) - onehot
    soft_loss_part = jnp.exp(student_scaled_logits - lse_soft[:, None]) - jnp.exp(
        teacher_scaled_logits - lse_teacher[:, None]
    )
    d_logits = (
        share_lab[:, None]
        * ((1.0 - SOFT_FRACTION) * hard_loss_part + SOFT_FRACTION * SOFTMAX_HEAT * soft_loss_part)
    ).astype(jnp.bfloat16)
    d_rows = lax.psum_scatter(
        product_of("pv,vd->pd", d_logits, table_student).astype(jnp.bfloat16),
        "fsdp",
        scatter_dimension=0,
        tiled=True,
    ).astype(jnp.float32)
    table_term = product_of("pv,pd->vd", d_logits, all_student)
    terms = share_lab * (
        (1.0 - SOFT_FRACTION) * cross_entropy
        + SOFT_FRACTION * SOFTMAX_HEAT * SOFTMAX_HEAT * divergence_loss
    )
    mine = lax.dynamic_slice_in_dim(terms, own * labels, labels)
    return (d_rows, table_term, jnp.sum(mine))


def on_device(
    tok_ids,
    segments,
    seq_len,
    label_pos,
    label_ids,
    table,
    w_qkv,
    w_out,
    w_up,
    w_down,
    small,
    position,
    t_table,
    t_qkv,
    t_out,
    t_up,
    t_down,
    t_small,
    t_position,
    mom_table,
    mom_qkv,
    mom_out,
    mom_up,
    mom_down,
    mom_small,
    mom_position,
    avg_table,
    avg_qkv,
    avg_out,
    avg_up,
    avg_down,
    avg_small,
    avg_position,
):
    micro, span = tok_ids.shape
    labels = label_pos.shape[1]
    share = table.shape[0]
    groups = lax.axis_size("fsdp")
    own = lax.axis_index("fsdp")
    valid_local = label_valid(seq_len, labels, span)
    label_count, count_seq = lax.psum(
        (jnp.sum(valid_local), jnp.sum((seq_len > 0).astype(jnp.float32))), ("dp", "fsdp")
    )
    tables = (
        lax.all_gather(table.astype(jnp.bfloat16), "dp", axis=0, tiled=True),
        lax.all_gather(t_table, "dp", axis=0, tiled=True),
    )
    vocab_rows, width = tables[0].shape
    ids_all, targets_all, lengths_all = (
        lax.all_gather(tok_ids, "fsdp", axis=0, tiled=True),
        lax.all_gather(label_ids, "fsdp", axis=0, tiled=True),
        lax.all_gather(seq_len, "fsdp", axis=0, tiled=True),
    )
    inside, safe_ids = owned(ids_all, share, groups, own)
    blank = jnp.zeros((), jnp.bfloat16)
    picked_student = jnp.where(inside[..., None], tables[0][safe_ids], blank)
    picked_teacher = jnp.where(inside[..., None], tables[1][safe_ids], blank)
    tokens_student, tokens_teacher = (
        lax.psum_scatter(picked_student, "fsdp", scatter_dimension=0, tiled=True).astype(
            jnp.float32
        ),
        lax.psum_scatter(picked_teacher, "fsdp", scatter_dimension=0, tiled=True).astype(
            jnp.float32
        ),
    )
    student = (w_qkv, w_out, w_up, w_down, small, position)
    student_low = tuple((weight.astype(jnp.bfloat16) for weight in student))
    teacher = gather_layer((t_qkv, t_out, t_up, t_down, t_small, t_position))
    targets_all = targets_all.reshape(groups, micro, labels)
    lengths_all = lengths_all.reshape(groups, micro)
    table_grad = jnp.zeros((vocab_rows, width), jnp.float32)
    loss_part = jnp.zeros((), jnp.float32)
    token_grads = []
    for index in range(micro):
        weights = gather_layer(student_low)
        start, normed_start, inverse_start = embed_forward(
            tokens_student[index], weights, segments[index]
        )
        teacher_start = embed_forward(tokens_teacher[index], teacher, segments[index])[0]
        student_out, kept = layer_forward(start, weights, seq_len[index])
        teacher_out = layer_forward(teacher_start, teacher, seq_len[index])[0]
        valid_group = label_valid(lengths_all[:, index], labels, span).reshape(-1)
        d_rows, table_term, label_loss = label_head(
            student_out,
            teacher_out,
            label_pos[index],
            tables,
            targets_all[:, index].reshape(-1),
            valid_group,
            own,
            share,
            groups,
            label_count,
        )
        cls_student = student_out[0]
        cls_teacher = teacher_out[0]
        scale_student = lax.rsqrt(jnp.sum(cls_student * cls_student) + 1e-06)
        unit_student = cls_student * scale_student
        unit_teacher = cls_teacher * lax.rsqrt(jnp.sum(cls_teacher * cls_teacher) + 1e-06)
        weight_pkd = PKD_WEIGHT * (seq_len[index] > 0).astype(jnp.float32) / count_seq
        gap = unit_student - unit_teacher
        d_unit = 2.0 * weight_pkd * gap
        d_cls = scale_student * d_unit - cls_student * scale_student**3 * jnp.sum(
            cls_student * d_unit
        )
        d_out = jnp.zeros_like(student_out).at[label_pos[index]].add(d_rows).at[0].add(d_cls)
        back = gather_layer(student_low)
        matrices, rows_grad, d_start = layer_backward(d_out, back, kept, seq_len[index])
        small_back = back[4].astype(jnp.float32)
        d_embed, gain_embed, shift_embed = layer_norm_back(
            d_start, normed_start, inverse_start, small_back[12]
        )
        token_grads.append(d_embed.astype(jnp.bfloat16))
        zero_segment = (segments[index] == 0).astype(jnp.float32)[:, None]
        small_grad = jnp.concatenate(
            [
                rows_grad,
                gain_embed[None],
                shift_embed[None],
                jnp.sum(d_embed * zero_segment, axis=0)[None],
                jnp.sum(d_embed * (1.0 - zero_segment), axis=0)[None],
            ]
        )
        step_grads = matrices + (small_grad, d_embed)
        accumulated = step_grads if index == 0 else jax.tree.map(jnp.add, accumulated, step_grads)
        table_grad = table_grad + table_term
        loss_part = loss_part + label_loss + weight_pkd * jnp.sum(gap * gap)
    accumulated = reduce_layer(accumulated)
    embed_grads = lax.all_gather(jnp.stack(token_grads), "fsdp", axis=0, tiled=True)
    flat = jnp.where(inside[..., None], embed_grads.astype(jnp.float32), 0.0).reshape(-1, width)
    table_grad = table_grad + jax.ops.segment_sum(
        flat, safe_ids.reshape(-1), num_segments=vocab_rows
    )
    table_shard = lax.psum_scatter(
        table_grad.astype(jnp.bfloat16), "dp", scatter_dimension=0, tiled=True
    ).astype(jnp.float32)
    grads = (table_shard,) + tuple(accumulated)
    squares = jnp.zeros((), jnp.float32)
    for grad in grads:
        squares = squares + jnp.sum(grad * grad)
    total_sq, loss_value = lax.psum((squares, loss_part), ("dp", "fsdp"))
    grad_norm = jnp.sqrt(total_sq)
    factor = CLIP / jnp.maximum(grad_norm, CLIP)
    rate = RATE_SCALE * math.sqrt(NPARAM)
    params = (table, w_qkv, w_out, w_up, w_down, small, position)
    moms = (mom_table, mom_qkv, mom_out, mom_up, mom_down, mom_small, mom_position)
    avgs = (avg_table, avg_qkv, avg_out, avg_up, avg_down, avg_small, avg_position)
    news, moments, averages = ([], [], [])
    for weight, grad, momentum, average in zip(params, grads, moms, avgs):
        clipped = grad * factor
        moment = MOMENTUM * momentum + clipped
        fresh = weight - rate * (clipped + MOMENTUM * moment)
        news.append(fresh)
        moments.append(moment)
        averages.append(AVERAGE * average + (1.0 - AVERAGE) * fresh)
    return tuple(news) + tuple(moments) + tuple(averages) + (grad_norm, loss_value)


def solution(mesh):
    placed = (
        P(("dp", "fsdp"), None),
        P(("dp", "fsdp"), None),
        P(("dp", "fsdp")),
        P(("dp", "fsdp"), None),
        P(("dp", "fsdp"), None),
        P(("dp", "fsdp"), None),
        P(("dp", "fsdp"), None),
        P(("dp", "fsdp"), None),
        P(("dp", "fsdp"), None),
        P(("dp", "fsdp"), None),
        P(None, ("dp", "fsdp")),
        P(None, ("dp", "fsdp")),
        P(("dp", "fsdp"), None),
        P(("dp", "fsdp"), None),
        P(("dp", "fsdp"), None),
        P(("dp", "fsdp"), None),
        P(("dp", "fsdp"), None),
        P(None, ("dp", "fsdp")),
        P(None, ("dp", "fsdp")),
        P(("dp", "fsdp"), None),
        P(("dp", "fsdp"), None),
        P(("dp", "fsdp"), None),
        P(("dp", "fsdp"), None),
        P(("dp", "fsdp"), None),
        P(None, ("dp", "fsdp")),
        P(None, ("dp", "fsdp")),
        P(("dp", "fsdp"), None),
        P(("dp", "fsdp"), None),
        P(("dp", "fsdp"), None),
        P(("dp", "fsdp"), None),
        P(("dp", "fsdp"), None),
        P(None, ("dp", "fsdp")),
        P(None, ("dp", "fsdp")),
    )
    return jax.shard_map(
        on_device,
        mesh=mesh,
        in_specs=placed,
        out_specs=(
            P(("dp", "fsdp"), None),
            P(("dp", "fsdp"), None),
            P(("dp", "fsdp"), None),
            P(("dp", "fsdp"), None),
            P(("dp", "fsdp"), None),
            P(None, ("dp", "fsdp")),
            P(None, ("dp", "fsdp")),
            P(("dp", "fsdp"), None),
            P(("dp", "fsdp"), None),
            P(("dp", "fsdp"), None),
            P(("dp", "fsdp"), None),
            P(("dp", "fsdp"), None),
            P(None, ("dp", "fsdp")),
            P(None, ("dp", "fsdp")),
            P(("dp", "fsdp"), None),
            P(("dp", "fsdp"), None),
            P(("dp", "fsdp"), None),
            P(("dp", "fsdp"), None),
            P(("dp", "fsdp"), None),
            P(None, ("dp", "fsdp")),
            P(None, ("dp", "fsdp")),
            P(),
            P(),
        ),
        check_vma=False,
    )
```

profile of v0, /device:TPU:0, one launch (start us, length us, event | category | flops | bytes accessed | tf_op | source)
XLA Modules:
  0.0 2236.4 jit_solution(2463154137222471869)
XLA Ops:
  28.6 52.3 %all-gather.66.cloned.1.call-done = bf16[4,956,768]{2,1,0:T(8,128)(2,1)} async-done(((bf16[1,956,768]{2,1,0:T(8,128)(2,1)}), bf16[4,956,768]{2,1,0:T(8,128)(2,1)}) %all-gather.66.cloned.1.call-update) | async-done | bytes 5873680 | tf_op jit(solution)/shard_map/all_gather | solution.py:352
  85.8 40.5 %gather_fusion = bf16[8192,768]{1,0:T(8,128)(2,1)} fusion(bf16[3824,768]{1,0:T(8,128)(2,1)} %reshape.1217, s32[8192]{0:T(1024)S(1)} %broadcast_clamp_fusion), kind=kCustom, calls=%fused_computation.2 | custom fusion | bytes 25198592 | tf_op jit(solution)/shard_map/gather | solution.py:363
  126.3 23.4 %all-gather.68.cloned.1.call-done = bf16[4,956,768]{2,1,0:T(8,128)(2,1)} async-done(((bf16[1,956,768]{2,1,0:T(8,128)(2,1)}), bf16[4,956,768]{2,1,0:T(8,128)(2,1)}) %all-gather.68.cloned.1.call-update) | async-done | bytes 5873680 | tf_op jit(solution)/shard_map/all_gather | solution.py:353
  154.6 40.5 %gather_fusion.2 = bf16[8192,768]{1,0:T(8,128)(2,1)} fusion(bf16[3824,768]{1,0:T(8,128)(2,1)} %reshape.1229, s32[8192]{0:T(1024)S(1)} %broadcast_clamp_fusion), kind=kCustom, calls=%fused_computation.4 | custom fusion | bytes 25198592 | tf_op jit(solution)/shard_map/gather | solution.py:364
  236.2 39.4 %all-gather.22 = bf16[32,24,16]{1,2,0:T(8,128)(2,1)S(1)} all-gather(bf16[1,24,16]{1,2,0:T(8,128)(2,1)S(1)} %bitcast.564), channel_id=1, replica_groups=mesh['dp'=4,'fsdp'=8] {'dp','fsdp'}, dimensions={0}, use_global_device_ids=true | all-gather | bytes 25344 | tf_op jit(solution)/shard_map/all_gather | solution.py:87
  276.3 40.7 %all-gather.16 = bf16[32,24,16]{1,2,0:T(8,128)(2,1)S(1)} all-gather(bf16[1,24,16]{1,2,0:T(8,128)(2,1)S(1)} %convert_bitcast_fusion.3), channel_id=1, replica_groups=mesh['dp'=4,'fsdp'=8] {'dp','fsdp'}, dimensions={0}, use_global_device_ids=true | all-gather | bytes 25344 | tf_op jit(solution)/shard_map/all_gather | solution.py:87
  326.4 41.8 %all-reduce.5 = (f32[]{:T(128)}, f32[]{:T(128)}) all-reduce(f32[]{:T(128)} %fusion.156, f32[]{:T(128)} %fusion.157), channel_id=1, replica_groups=mesh['dp'=4,'fsdp'=8] {'dp','fsdp'}, use_global_device_ids=true, to_apply=%region_1.2 | all-reduce | flops 2 | bytes 16 | tf_op jit(solution)/shard_map/psum | solution.py:348
  376.9 53.6 %all_gather.177 = bf16[512,768]{0,1:T(8,128)(2,1)S(1)} all-gather(bf16[512,24]{0,1:T(8,128)(2,1)S(1)} %convert_element_type.311), channel_id=1, replica_groups=mesh['dp'=4,'fsdp'=8] {'dp','fsdp'}, dimensions={1}, use_global_device_ids=true | all-gather | bytes 811008 | tf_op jit(solution)/shard_map/all_gather | solution.py:88
  431.7 47.8 %all_gather.193 = bf16[512,768]{0,1:T(8,128)(2,1)S(1)} all-gather(bf16[512,24]{0,1:T(8,128)(2,1)S(1)} %copy-done.121), channel_id=1, replica_groups=mesh['dp'=4,'fsdp'=8] {'dp','fsdp'}, dimensions={1}, use_global_device_ids=true | all-gather | bytes 811008 | tf_op jit(solution)/shard_map/all_gather | solution.py:88
  548.7 31.9 %all-gather.60.cloned.1.call-done = bf16[768,3072]{1,0:T(8,128)(2,1)} async-done(((bf16[24,3072]{1,0:T(8,128)(2,1)}), bf16[768,3072]{1,0:T(8,128)(2,1)}) %all-gather.60.cloned.1.call-update) | async-done | bytes 4718608 | tf_op jit(solution)/shard_map/all_gather | solution.py:85
  580.6 65.3 %all-gather.62.cloned.1.call-done = bf16[3072,768]{1,0:T(8,128)(2,1)} async-done(((bf16[96,768]{1,0:T(8,128)(2,1)}), bf16[3072,768]{1,0:T(8,128)(2,1)}) %all-gather.62.cloned.1.call-update) | async-done | bytes 4718608 | tf_op jit(solution)/shard_map/all_gather | solution.py:86
  851.0 49.7 %all-gather.54.cloned.1.call-done = bf16[3072,768]{1,0:T(8,128)(2,1)} async-done(((bf16[96,768]{1,0:T(8,128)(2,1)}), bf16[3072,768]{1,0:T(8,128)(2,1)}) %all-gather.54.cloned.1.call-update) | async-done | bytes 4718608 | tf_op jit(solution)/shard_map/all_gather | solution.py:86
  1109.5 18.7 gather_fusion.6
  1195.3 31.4 %while.61 = (s32[]{:T(128)}, f32[512]{0:T(512)S(1)}, f32[512]{0:T(512)S(1)}, f32[512]{0:T(512)S(1)}, f32[512]{0:T(512)S(1)}, /*index=5*/f32[512]{0:T(512)S(1)}, ...) while((s32[]{:T(128)}, f32[512]{0:T(512)S(1)}, ...), condition=%wide.region_53.55_spmd, body=%wide.region_52.54_spmd.sunk | while | flops 12293 | bytes 92399 | solution.py:30
  1242.4 26.2 %while.60 = (s32[]{:T(128)}, f32[512]{0:T(512)S(1)}, f32[512]{0:T(512)S(1)}, f32[512]{0:T(512)S(1)}, f32[512]{0:T(512)S(1)}, /*index=5*/f32[512]{0:T(512)S(1)}, ...) while((s32[]{:T(128)}, f32[512]{0:T(512)S(1)}, ...), condition=%wide.region_28.30_spmd, body=%wide.region_27.29_spmd.sunk | while | flops 12293 | bytes 92399 | solution.py:30
  1304.3 18.5 reduce-scatter.19.cloned.1.call-done
  1496.0 43.6 %all-reduce.2 = f32[16,768]{1,0:T(8,128)S(1)} all-reduce(f32[16,768]{1,0:T(8,128)S(1)} %add.1176), channel_id=25, replica_groups=mesh['dp'=4,'fsdp'=8] {'dp','fsdp'}, use_global_device_ids=true, to_apply=%region_115.117.clone | all-reduce | flops 12288 | bytes 98304
  1540.4 79.3 %reduce-scatter.31.cloned.1.call-done = f32[24,512]{1,0:T(8,128)} async-done(((f32[768,512]{1,0:T(8,128)}), f32[24,512]{1,0:T(8,128)}) %reduce-scatter.31.cloned.1.call-update) | async-done | bytes 49168
  1621.3 102.3 %reduce-scatter.25.cloned.1.call-done = f32[24,768]{1,0:T(8,128)} async-done(((f32[768,768]{1,0:T(8,128)}), f32[24,768]{1,0:T(8,128)}) %reduce-scatter.25.cloned.1.call-update) | async-done | bytes 73744 | tf_op jit(solution)/shard_map/reduce_scatter | solution.py:95
  1725.0 122.7 %reduce-scatter.23.cloned.1.call-done = f32[24,2304]{1,0:T(8,128)} async-done(((f32[768,2304]{1,0:T(8,128)}), f32[24,2304]{1,0:T(8,128)}) %reduce-scatter.23.cloned.1.call-update) | async-done | bytes 221200 | tf_op jit(solution)/shard_map/reduce_scatter | solution.py:94
  1849.3 139.1 %reduce-scatter.27.cloned.1.call-done = f32[24,3072]{1,0:T(8,128)} async-done(((f32[768,3072]{1,0:T(8,128)}), f32[24,3072]{1,0:T(8,128)}) %reduce-scatter.27.cloned.1.call-update) | async-done | bytes 294928 | tf_op jit(solution)/shard_map/reduce_scatter | solution.py:96
  2004.3 64.2 %scatter_fusion = f32[3824,768]{1,0:T(8,128)} fusion(f32[3824,768]{1,0:T(8,128)} %convolution_add_fusion, s32[8192]{0:T(1024)S(1)} %bitcast.508, f32[8192,768]{1,0:T(8,128)} %bitcast.444), kind=kCustom, calls=%fused_computation.10 | custom fusion | flops 6291456 | bytes 75530240 | tf_op jit(solution)/shard_map/scatter-add | solution.py:438
  2076.2 78.7 %fusion = bf16[960,768]{1,0:T(8,128)(2,1)S(1)} fusion(bf16[3824,768]{1,0:T(8,128)(2,1)} %convert_element_type.386), kind=kCustom, calls=%all-reduce-scatter | all-reduce-scatter fusion | flops 2949121 | bytes 7348736
  2172.9 40.3 %all-reduce.4 = (f32[]{:T(128)}, f32[]{:T(128)}) all-reduce(f32[]{:T(128)S(6)} %add.1179, f32[]{:T(128)S(6)} %add.1208), channel_id=1, replica_groups=mesh['dp'=4,'fsdp'=8] {'dp','fsdp'}, use_global_device_ids=true, to_apply=%region_119.121 | all-reduce | flops 2 | bytes 16 | tf_op jit(solution)/shard_map/psum | solution.py:448
  (993 shorter events, 964.8 us)
Async XLA Ops:
  8.0 72.9 %all-gather.66.cloned.1.call-start = ((), (), s32[]{:S(2)}) async-start(), calls=%async_computation.26 | async-start | bytes 7372800 | tf_op jit(solution)/shard_map/all_gather | solution.py:352
  11.2 138.5 %all-gather.68.cloned.1.call-start = ((), (), s32[]{:S(2)}) async-start(), calls=%async_computation.27 | async-start | bytes 7372800 | tf_op jit(solution)/shard_map/all_gather | solution.py:353
  11.9 470.0 %reduce-scatter.17.cloned.1.call-start = ((), (), s32[]{:S(2)}) async-start(), calls=%async_computation.14 | async-start | bytes 14155776 | tf_op jit(solution)/shard_map/reduce_scatter | solution.py:369
  212.5 288.0 %reduce-scatter.15.cloned.1.call-start = ((), (), s32[]{:S(2)}) async-start(), calls=%async_computation.9 | async-start | bytes 14155776 | tf_op jit(solution)/shard_map/reduce_scatter | solution.py:366
  213.1 292.4 %all-gather.56.cloned.1.call-start = ((), (), s32[]{:S(2)}) async-start(), calls=%async_computation.15 | async-start | bytes 3649536 | tf_op jit(solution)/shard_map/all_gather | solution.py:83
  213.7 330.6 %all-gather.58.cloned.1.call-start = ((), (), s32[]{:S(2)}) async-start(), calls=%async_computation.16 | async-start | bytes 1216512 | tf_op jit(solution)/shard_map/all_gather | solution.py:84
  214.3 366.3 %all-gather.60.cloned.1.call-start = ((), (), s32[]{:S(2)}) async-start(), calls=%async_computation.17 | async-start | bytes 4866048 | tf_op jit(solution)/shard_map/all_gather | solution.py:85
  214.9 431.0 %all-gather.62.cloned.1.call-start = ((), (), s32[]{:S(2)}) async-start(), calls=%async_computation.18 | async-start | bytes 4866048 | tf_op jit(solution)/shard_map/all_gather | solution.py:86
  215.6 558.9 %all-gather.48.cloned.1.call-start = ((), (), s32[]{:S(2)}) async-start(), calls=%async_computation.10 | async-start | bytes 3649536 | tf_op jit(solution)/shard_map/all_gather | solution.py:83
  216.3 591.2 %all-gather.50.cloned.1.call-start = ((), (), s32[]{:S(2)}) async-start(), calls=%async_computation.11 | async-start | bytes 1216512 | tf_op jit(solution)/shard_map/all_gather | solution.py:84
  217.1 617.9 %all-gather.52.cloned.1.call-start = ((), (), s32[]{:S(2)}) async-start(), calls=%async_computation.12 | async-start | bytes 4866048 | tf_op jit(solution)/shard_map/all_gather | solution.py:85
  217.9 682.8 %all-gather.54.cloned.1.call-start = ((), (), s32[]{:S(2)}) async-start(), calls=%async_computation.13 | async-start | bytes 4866048 | tf_op jit(solution)/shard_map/all_gather | solution.py:86
  218.6 1077.5 %reduce-scatter.21.cloned.1.call-start = ((), (), s32[]{:S(2)}) async-start(), calls=%async_computation.20 | async-start | bytes 884736 | tf_op jit(solution)/shard_map/reduce_scatter | solution.py:292
  318.2 504.7 %copy-start.109 = (f32[768]{0:T(1024)}, f32[768]{0:T(1024)S(1)}, u32[]{:S(2)}) copy-start(f32[768]{0:T(1024)S(1)} %get-tuple-element.1015) | copy-start | bytes 9220
  318.2 504.7 %copy-start.142 = (f32[768]{0:T(1024)}, f32[768]{0:T(1024)S(1)}, u32[]{:S(2)}) copy-start(f32[768]{0:T(1024)S(1)} %get-tuple-element.1014) | copy-start | bytes 9220
  1242.1 80.7 %reduce-scatter.19.cloned.1.call-start = ((), (), s32[]{:S(2)}) async-start(), calls=%async_computation.19 | async-start | bytes 884736 | tf_op jit(solution)/shard_map/reduce_scatter | solution.py:292
  1293.5 326.2 %reduce-scatter.31.cloned.1.call-start = ((), (), s32[]{:S(2)}) async-start(), calls=%async_computation.28 | async-start | bytes 1622016
  1433.8 289.7 %reduce-scatter.25.cloned.1.call-start = ((), (), s32[]{:S(2)}) async-start(), calls=%async_computation.23 | async-start | bytes 2433024 | tf_op jit(solution)/shard_map/reduce_scatter | solution.py:95
  1438.7 409.0 %reduce-scatter.23.cloned.1.call-start = ((), (), s32[]{:S(2)}) async-start(), calls=%async_computation.22 | async-start | bytes 7299072 | tf_op jit(solution)/shard_map/reduce_scatter | solution.py:94
  1448.7 539.7 %reduce-scatter.27.cloned.1.call-start = ((), (), s32[]{:S(2)}) async-start(), calls=%async_computation.24 | async-start | bytes 9732096 | tf_op jit(solution)/shard_map/reduce_scatter | solution.py:96
  1460.9 529.1 %all-gather.64.cloned.1.call-start = ((), (), s32[]{:S(2)}) async-start(), calls=%async_computation.21 | async-start | bytes 14155776 | tf_op jit(solution)/shard_map/all_gather | solution.py:436
  1464.5 693.8 %reduce-scatter.29.cloned.1.call-start = ((), (), s32[]{:S(2)}) async-start(), calls=%async_computation.25 | async-start | bytes 9732096 | tf_op jit(solution)/shard_map/reduce_scatter | solution.py:97
  1495.2 494.8 %copy-start.102 = (pred[16,512]{1,0:T(8,128)(4,1)S(1)}, pred[16,512]{1,0:T(8,128)(4,1)}, u32[]{:S(2)}) copy-start(pred[16,512]{1,0:T(8,128)(4,1)} %copy-done.101) | copy-start | bytes 24580
  2155.0 5.0 collective-permute-start
  (217 other events, 6601.9 us)
Sparse Core Ops, SparseCore 0:
  11.3 69.5 all-gather.65
  82.8 66.8 all-gather.67
  212.6 139.6 reduce-scatter.16
  354.4 145.9 reduce-scatter.14
  1242.2 29.5 reduce-scatter.20
  1293.6 29.1 reduce-scatter.18
  1464.6 118.8 all-gather.63
Sparse Core Ops, SparseCore 1:
  216.6 146.5 all-gather.55
  366.1 148.6 all-gather.57
  517.7 62.8 all-gather.59
  583.6 62.2 all-gather.61
  649.5 61.4 all-gather.47
  714.5 54.0 all-gather.49
  772.1 62.8 all-gather.51
  838.5 62.2 all-gather.53
  1433.9 185.7 reduce-scatter.30
  1625.5 97.9 reduce-scatter.24
  1730.0 117.6 reduce-scatter.22
  1853.6 134.7 reduce-scatter.26
  1995.2 143.8 reduce-scatter.28
where the time goes:
time: 2260 us; the launch traced here: 2240 us
  waiting for transfers between devices  714 us (32%)
  blocking collectives  692 us (31%)
  matrix products  284 us (13%)
  local copies, waits for them, and re-layouts  274 us (12%)
  other arithmetic  230 us (10%)
  between operations  37 us (2%)
    all_gather x16, blocking collectives, merged_2(): everything = jax.tree.map(lambda part: lax.all_gather(part, axis), shard)  206 us
    dot_general x38, matrix products, product_of(): return jnp.einsum(form, left, right, preferred_element_type=jnp.float32)  187 us
    reduce_scatter x1, waiting for transfers between devices, reduce_layer(): lax.psum_scatter(grads[2], ('dp', 'fsdp'), scatter_dimension=0, tiled=True)  139 us
    unnamed x3, blocking collectives  128 us
    reduce_scatter x1, waiting for transfers between devices, reduce_layer(): lax.psum_scatter(grads[0], ('dp', 'fsdp'), scatter_dimension=0, tiled=True)  123 us
    all_gather x2, waiting for transfers between devices, gather_layer(): lax.all_gather(weights[3], ('dp', 'fsdp'), axis=0, tiled=True)  115 us
    reduce_scatter x1, waiting for transfers between devices, reduce_layer(): lax.psum_scatter(grads[1], ('dp', 'fsdp'), scatter_dimension=0, tiled=True)  102 us
    all_gather x2, blocking collectives, gather_layer(): lax.all_gather(weights[5], ('dp', 'fsdp'), axis=1, tiled=True)  101 us
  transfers between devices with their start and end apart: 21, of which 12 were waited for; matrix products, arithmetic and copies ran while one was open for 23% of the time, Pallas kernels for 0%

commit v1 on v0

v1 whole, which is shorter than its diff:
```python
import math

import jax
import jax.numpy as jnp
from jax import lax
from jax.sharding import PartitionSpec as P

HD = 64
NPARAM = 30978048


SOFTMAX_HEAT = 2.0
SOFT_FRACTION = 0.5
PKD_WEIGHT = 10.0
MOMENTUM = 0.9
AVERAGE = 0.75
CLIP = 0.002
RATE_SCALE = 20.0
EPSILON = 1e-12
NEGATIVE = -1e30
BOTH = ("dp", "fsdp")
LOW = jnp.bfloat16


def product_of(form, left, right):
    return jnp.einsum(form, left, right, preferred_element_type=jnp.float32)


def owned(ids, share, padded, groups, own):
    block = ids // share
    inside = block % groups == own
    local = block // groups * padded + ids % share
    return (inside, jnp.where(inside, local, 0))


def layer_norm_keep(value, gain, shift):
    mean = jnp.mean(value, axis=-1, keepdims=True)
    centred = value - mean
    inverse = lax.rsqrt(jnp.mean(centred * centred, axis=-1, keepdims=True) + EPSILON)
    normed = centred * inverse
    return (normed * gain + shift, normed, inverse)


def layer_norm_back(grad, normed, inverse, gain):
    axes = tuple(range(grad.ndim - 1))
    gain_grad = jnp.sum(grad * normed, axis=axes)
    shift_grad = jnp.sum(grad, axis=axes)
    scaled = grad * gain
    centred = scaled - jnp.mean(scaled, axis=-1, keepdims=True)
    return (
        inverse * (centred - normed * jnp.mean(scaled * normed, axis=-1, keepdims=True)),
        gain_grad,
        shift_grad,
    )


def gelu_parts(upward):
    normal_cdf = 0.5 * (1.0 + lax.erf(upward * 0.7071067811865476))
    density = jnp.exp(-0.5 * upward * upward) * 0.3989422804014327
    return (upward * normal_cdf, normal_cdf + upward * density)


def label_valid(lengths, labels, span):
    needed = (lengths * labels + span - 1) // span
    return (jnp.arange(labels)[None, :] < needed[:, None]).astype(jnp.float32)


def masked_scores(queries, keys, lengths):
    raw = product_of("bqhd,bkhd->bhqk", queries, keys)
    keep = jnp.arange(keys.shape[1])[None, :] < jnp.maximum(lengths, 1)[:, None]
    return jnp.where(keep[:, None, None, :], raw * 0.125, NEGATIVE)


def pack_layer(weights, extra):
    w_qkv, w_out, w_up, w_down, small, position = (w.astype(LOW) for w in weights)
    rows = w_qkv.shape[0]
    parts = w_down.shape[0] // rows
    pieces = [w_qkv, w_out, w_up]
    pieces += [w_down[k * rows : (k + 1) * rows] for k in range(parts)]
    pieces += [position.T, small.T]
    filled = small.shape[0]
    if extra is not None:
        pieces.append(extra)
        filled += extra.shape[1]
    pieces.append(jnp.zeros((rows, -filled % 128), LOW))
    return jnp.concatenate(pieces, axis=1)


def unpack_layer(packed, devices, span, slots):
    width = packed.shape[0]
    ff = 4 * width
    edges = [3 * width, 4 * width, 4 * width + ff, 4 * width + 2 * ff]
    w_qkv = packed[:, : edges[0]]
    w_out = packed[:, edges[0] : edges[1]]
    w_up = packed[:, edges[1] : edges[2]]
    down = packed[:, edges[2] : edges[3]]
    w_down = (
        down.reshape(devices, width // devices, 4, width).transpose(0, 2, 1, 3).reshape(ff, width)
    )
    rest = packed[:, edges[3] :]
    position = rest[:, :span].T.astype(jnp.float32)
    small = rest[:, span : span + slots].T.astype(jnp.float32)
    return (w_qkv, w_out, w_up, w_down, small, position), rest[:, span + slots :]


def embed_forward(token_rows, weights, segment_ids):
    small, position = weights[4:]
    segment_rows = jnp.where(segment_ids[..., None] == 0, small[14], small[15])
    return layer_norm_keep(token_rows + position + segment_rows, small[12], small[13])


def layer_forward(value, weights, lengths):
    w_qkv, w_out, w_up, w_down, small = weights[:5]
    micro, span, width = value.shape
    heads = width // HD
    value_low = value.astype(LOW)
    bias = jnp.concatenate([small[0], jnp.zeros_like(small[0]), small[1]])
    joined = (product_of("bsd,df->bsf", value_low, w_qkv) + bias).astype(LOW)
    split = joined.reshape(micro, span, 3, heads, HD)
    scores = masked_scores(split[:, :, 0], split[:, :, 1], lengths)
    top = jnp.max(scores, axis=-1, keepdims=True)
    exponent = jnp.exp(scores - top)
    total = jnp.sum(exponent, axis=-1, keepdims=True)
    probs = (exponent / total).astype(LOW)
    logsum = top + jnp.log(total)
    context = (
        product_of("bhqk,bkhd->bqhd", probs, split[:, :, 2]).reshape(micro, span, width).astype(LOW)
    )
    attn = product_of("bsc,cd->bsd", context, w_out) + small[2]
    first, normed_first, inverse_first = layer_norm_keep(value + attn, small[8], small[9])
    first_low = first.astype(LOW)
    upward = product_of("bsd,df->bsf", first_low, w_up) + small[3:7].reshape(-1)
    act, slope = gelu_parts(upward)
    act_low = act.astype(LOW)
    down = product_of("bsf,fd->bsd", act_low, w_down) + small[7]
    out, normed_second, inverse_second = layer_norm_keep(first + down, small[10], small[11])
    return (
        out,
        (
            value_low,
            joined,
            logsum,
            context,
            normed_first,
            inverse_first,
            first_low,
            slope,
            act_low,
            normed_second,
            inverse_second,
        ),
    )


def layer_backward(grad, weights, kept, lengths):
    w_qkv, w_out, w_up, w_down, small = weights[:5]
    (
        value_low,
        joined,
        logsum,
        context,
        normed_first,
        inverse_first,
        first_low,
        slope,
        act_low,
        normed_second,
        inverse_second,
    ) = kept
    micro, span, width = value_low.shape
    heads = width // HD
    d_second, gain_second, shift_second = layer_norm_back(
        grad, normed_second, inverse_second, small[10]
    )
    d_down = d_second.astype(LOW)
    g_down = product_of("bsf,bsd->fd", act_low, d_down)
    d_up = (product_of("bsd,fd->bsf", d_down, w_down) * slope).astype(LOW)
    g_up = product_of("bsd,bsf->df", first_low, d_up)
    d_first = d_second + product_of("bsf,df->bsd", d_up, w_up)
    d_sum, gain_first, shift_first = layer_norm_back(d_first, normed_first, inverse_first, small[8])
    d_attn = d_sum.astype(LOW)
    g_out = product_of("bsc,bsd->cd", context, d_attn)
    d_context = (
        product_of("bsd,cd->bsc", d_attn, w_out).astype(LOW).reshape(micro, span, heads, HD)
    )
    split = joined.reshape(micro, span, 3, heads, HD)
    probs = jnp.exp(masked_scores(split[:, :, 0], split[:, :, 1], lengths) - logsum)
    g_values = product_of("bhqk,bqhd->bkhd", probs.astype(LOW), d_context)
    d_probs = product_of("bqhd,bkhd->bhqk", d_context, split[:, :, 2])
    d_scores = (probs * (d_probs - jnp.sum(probs * d_probs, axis=-1, keepdims=True))).astype(LOW)
    g_queries = product_of("bhqk,bkhd->bqhd", d_scores, split[:, :, 1]) * 0.125
    g_keys = product_of("bhqk,bqhd->bkhd", d_scores, split[:, :, 0]) * 0.125
    d_joined = (
        jnp.stack([g_queries, g_keys, g_values], axis=2)
        .reshape(micro, span, 3 * width)
        .astype(LOW)
    )
    g_qkv = product_of("bsd,bsf->df", value_low, d_joined)
    d_value = d_sum + product_of("bsf,df->bsd", d_joined, w_qkv)

    def column_sum(value):
        return jnp.sum(value.astype(jnp.float32), axis=(0, 1))

    joined_sum = column_sum(d_joined)
    rows_grad = jnp.concatenate(
        [
            joined_sum[:width][None],
            joined_sum[2 * width :][None],
            column_sum(d_attn)[None],
            column_sum(d_up).reshape(-1, width),
            column_sum(d_down)[None],
            gain_first[None],
            shift_first[None],
            gain_second[None],
            shift_second[None],
        ]
    )
    return ((g_qkv, g_out, g_up, g_down), rows_grad, d_value)


def label_head(
    student_out, teacher_out, places, tables, targets, valid_mask, own, share, padded, groups, count
):
    table_student, table_teacher = tables
    vocab_rows = table_student.shape[0]
    micro, span, width = student_out.shape
    mine = places.size
    pick = (places[..., None] == jnp.arange(span)).astype(LOW)
    rows = jnp.stack(
        [
            product_of("bps,bsd->bpd", pick, out.astype(LOW)).astype(LOW).reshape(mine, width)
            for out in (student_out, teacher_out)
        ]
    )
    rows_all = lax.all_gather(rows, "fsdp", axis=1, tiled=True)
    all_student = rows_all[0]
    all_teacher = rows_all[1]
    row_index = jnp.arange(vocab_rows)
    real = (row_index % padded < share)[None, :]
    inside, local_target = owned(targets, share, padded, groups, own)
    hit = (row_index[None, :] == local_target[:, None]) & inside[:, None]
    student = jnp.where(real, product_of("pd,vd->pv", all_student, table_student), NEGATIVE)
    teacher = jnp.where(real, product_of("pd,vd->pv", all_teacher, table_teacher), NEGATIVE)
    top_student = jnp.max(student, axis=1)
    top_teacher = jnp.max(teacher, axis=1)
    half = jnp.exp((student - top_student[:, None]) / SOFTMAX_HEAT)
    teacher_exp = jnp.exp((teacher - top_teacher[:, None]) / SOFTMAX_HEAT)
    stats = jnp.stack(
        [
            top_student,
            jnp.sum(half * half, axis=1),
            jnp.sum(half, axis=1),
            top_teacher,
            jnp.sum(teacher_exp, axis=1),
            jnp.sum(teacher_exp * ((teacher - student) / SOFTMAX_HEAT), axis=1),
            jnp.sum(jnp.where(hit, student, 0.0), axis=1),
            jnp.zeros_like(top_student),
        ]
    )
    stats = lax.all_gather(stats, "fsdp")
    peak_student = jnp.max(stats[:, 0], axis=0)
    peak_teacher = jnp.max(stats[:, 3], axis=0)
    fall_student = jnp.exp((stats[:, 0] - peak_student) / SOFTMAX_HEAT)
    fall_teacher = jnp.exp((stats[:, 3] - peak_teacher) / SOFTMAX_HEAT)
    sum_plain = jnp.sum(stats[:, 1] * fall_student * fall_student, axis=0)
    sum_soft = jnp.sum(stats[:, 2] * fall_student, axis=0)
    sum_teacher = jnp.sum(stats[:, 4] * fall_teacher, axis=0)
    cross = jnp.sum(stats[:, 5] * fall_teacher, axis=0)
    target_logit = jnp.sum(stats[:, 6], axis=0)
    lse_plain = peak_student + jnp.log(sum_plain)
    lse_soft = peak_student / SOFTMAX_HEAT + jnp.log(sum_soft)
    lse_teacher = peak_teacher / SOFTMAX_HEAT + jnp.log(sum_teacher)
    cross_entropy = lse_plain - target_logit
    divergence_loss = cross / sum_teacher - lse_teacher + lse_soft
    share_lab = valid_mask / count
    hard = jnp.exp(student - lse_plain[:, None]) - hit.astype(jnp.float32)
    soft = jnp.exp(student / SOFTMAX_HEAT - lse_soft[:, None]) - jnp.exp(
        teacher / SOFTMAX_HEAT - lse_teacher[:, None]
    )
    d_logits = (
        share_lab[:, None]
        * ((1.0 - SOFT_FRACTION) * hard + SOFT_FRACTION * SOFTMAX_HEAT * soft)
    ).astype(LOW)
    d_rows = lax.psum_scatter(
        product_of("pv,vd->pd", d_logits, table_student).astype(LOW),
        "fsdp",
        scatter_dimension=0,
        tiled=True,
    )
    table_term = product_of("pv,pd->vd", d_logits, all_student)
    terms = share_lab * (
        (1.0 - SOFT_FRACTION) * cross_entropy
        + SOFT_FRACTION * SOFTMAX_HEAT * SOFTMAX_HEAT * divergence_loss
    )
    local = lax.dynamic_slice_in_dim(terms, own * mine, mine)
    d_out = product_of("bps,bpd->bsd", pick, d_rows.reshape(micro, -1, width))
    return (d_out, table_term, jnp.sum(local))


def pack_grads(matrices, small_grad, position_grad, devices):
    g_qkv, g_out, g_up, g_down = (g.astype(LOW) for g in matrices)
    width = g_qkv.shape[0]
    ff = g_down.shape[0]
    parts = ff // width
    g_down = (
        g_down.reshape(devices, parts, width // devices, width)
        .transpose(0, 2, 1, 3)
        .reshape(width, ff)
    )
    pad = -small_grad.shape[0] % 128
    return jnp.concatenate(
        [
            g_qkv,
            g_out,
            g_up,
            g_down,
            position_grad.astype(LOW).T,
            jnp.pad(small_grad, ((0, pad), (0, 0))).astype(LOW).T,
        ],
        axis=1,
    )


def unpack_grads(packed, width, span, slots):
    ff = 4 * width
    packed = packed.astype(jnp.float32)
    edges = [3 * width, 4 * width, 4 * width + ff, 4 * width + 2 * ff]
    down = packed[:, edges[2] : edges[3]]
    g_down = jnp.concatenate([down[:, k * width : (k + 1) * width] for k in range(4)], axis=0)
    return (
        packed[:, : edges[0]],
        packed[:, edges[0] : edges[1]],
        packed[:, edges[1] : edges[2]],
        g_down,
        packed[:, edges[3] + span : edges[3] + span + slots].T,
        packed[:, edges[3] : edges[3] + span].T,
    )


def unit_of(cls):
    scale = lax.rsqrt(jnp.sum(cls * cls, axis=-1, keepdims=True) + 1e-06)
    return cls * scale, scale


def on_device(
    tok_ids,
    segments,
    seq_len,
    label_pos,
    label_ids,
    table,
    w_qkv,
    w_out,
    w_up,
    w_down,
    small,
    position,
    t_table,
    t_qkv,
    t_out,
    t_up,
    t_down,
    t_small,
    t_position,
    mom_table,
    mom_qkv,
    mom_out,
    mom_up,
    mom_down,
    mom_small,
    mom_position,
    avg_table,
    avg_qkv,
    avg_out,
    avg_up,
    avg_down,
    avg_small,
    avg_position,
):
    micro, span = tok_ids.shape
    labels = label_pos.shape[1]
    share, width = table.shape
    groups = lax.axis_size("fsdp")
    dp = lax.axis_size("dp")
    devices = groups * dp
    own = lax.axis_index("fsdp")
    pad = -share % 16
    padded = share + pad
    rows_own = w_qkv.shape[0]
    slots = small.shape[0]

    info = jnp.concatenate(
        [tok_ids, label_ids, jnp.broadcast_to(seq_len[:, None], (micro, labels))], axis=1
    )
    info = lax.all_gather(info, "fsdp", axis=0, tiled=True)
    ids_all = info[:, :span]
    targets_all = info[:, span : span + labels].reshape(-1)
    lengths_all = info[:, span + labels]
    student_table = lax.all_gather(
        jnp.pad(table.astype(LOW), ((0, pad), (0, 0))), "dp", axis=0, tiled=True
    )
    teacher_table = lax.all_gather(jnp.pad(t_table, ((0, pad), (0, 0))), "dp", axis=0, tiled=True)
    tables = (student_table, teacher_table)
    vocab_rows = student_table.shape[0]

    valid_local = label_valid(seq_len, labels, span)
    counts = jnp.stack([jnp.sum(valid_local), jnp.sum((seq_len > 0).astype(jnp.float32))])
    extra = jnp.broadcast_to(counts.astype(LOW)[None, :], (rows_own, 2))

    inside, safe_ids = owned(ids_all, share, padded, groups, own)
    blank = jnp.zeros((), LOW)
    picked_student = jnp.where(inside[..., None], student_table[safe_ids], blank)
    picked_teacher = jnp.where(inside[..., None], teacher_table[safe_ids], blank)
    tokens_student = lax.psum_scatter(
        picked_student, "fsdp", scatter_dimension=0, tiled=True
    ).astype(jnp.float32)
    tokens_teacher = lax.psum_scatter(
        picked_teacher, "fsdp", scatter_dimension=0, tiled=True
    ).astype(jnp.float32)

    packed_student = pack_layer((w_qkv, w_out, w_up, w_down, small, position), extra)
    packed_teacher = pack_layer((t_qkv, t_out, t_up, t_down, t_small, t_position), None)
    packed_student = lax.all_gather(packed_student, BOTH, axis=0, tiled=True)
    packed_teacher = lax.all_gather(packed_teacher, BOTH, axis=0, tiled=True)
    weights, rest = unpack_layer(packed_student, devices, span, slots)
    teacher, _ = unpack_layer(packed_teacher, devices, span, slots)
    counted = jnp.sum(rest[::rows_own, :2].astype(jnp.float32), axis=0)
    label_count, count_seq = counted[0], counted[1]

    start, normed_start, inverse_start = embed_forward(tokens_student, weights, segments)
    teacher_start = embed_forward(tokens_teacher, teacher, segments)[0]
    student_out, kept = layer_forward(start, weights, seq_len)
    teacher_out = layer_forward(teacher_start, teacher, seq_len)[0]
    valid_group = label_valid(lengths_all, labels, span).reshape(-1)
    d_out, table_grad, label_loss = label_head(
        student_out,
        teacher_out,
        label_pos,
        tables,
        targets_all,
        valid_group,
        own,
        share,
        padded,
        groups,
        label_count,
    )
    cls_student = student_out[:, 0]
    unit_student, scale_student = unit_of(cls_student)
    unit_teacher = unit_of(teacher_out[:, 0])[0]
    weight_pkd = (PKD_WEIGHT * (seq_len > 0).astype(jnp.float32) / count_seq)[:, None]
    gap = unit_student - unit_teacher
    d_unit = 2.0 * weight_pkd * gap
    d_cls = scale_student * d_unit - cls_student * scale_student**3 * jnp.sum(
        cls_student * d_unit, axis=-1, keepdims=True
    )
    first_row = (jnp.arange(span) == 0).astype(jnp.float32)[None, :, None]
    d_out = d_out + first_row * d_cls[:, None, :]
    loss_part = label_loss + jnp.sum(weight_pkd * gap * gap)

    matrices, rows_grad, d_start = layer_backward(d_out, weights, kept, seq_len)
    d_embed, gain_embed, shift_embed = layer_norm_back(
        d_start, normed_start, inverse_start, weights[4][12]
    )
    zero_segment = (segments == 0).astype(jnp.float32)[..., None]
    small_grad = jnp.concatenate(
        [
            rows_grad,
            gain_embed[None],
            shift_embed[None],
            jnp.sum(d_embed * zero_segment, axis=(0, 1))[None],
            jnp.sum(d_embed * (1.0 - zero_segment), axis=(0, 1))[None],
        ]
    )
    embed_grads = lax.all_gather(d_embed.astype(LOW), "fsdp", axis=0, tiled=True)
    packed_grads = pack_grads(matrices, small_grad, jnp.sum(d_embed, axis=0), devices)
    packed_grads = lax.psum_scatter(packed_grads, BOTH, scatter_dimension=0, tiled=True)
    flat = jnp.where(inside[..., None], embed_grads.astype(jnp.float32), 0.0).reshape(-1, width)
    table_grad = table_grad + jax.ops.segment_sum(
        flat, safe_ids.reshape(-1), num_segments=vocab_rows
    )
    table_shard = lax.psum_scatter(
        table_grad.astype(LOW), "dp", scatter_dimension=0, tiled=True
    ).astype(jnp.float32)[:share]
    grads = (table_shard,) + unpack_grads(packed_grads, width, span, slots)
    squares = jnp.zeros((), jnp.float32)
    for grad in grads:
        squares = squares + jnp.sum(grad * grad)
    sums = jnp.broadcast_to(jnp.stack([squares, loss_part])[:, None], (2, 128))
    sums = jnp.sum(lax.all_gather(sums, "dp"), axis=0)
    sums = jnp.sum(lax.all_gather(sums, "fsdp"), axis=0)
    total_sq, loss_value = sums[0, 0], sums[1, 0]
    grad_norm = jnp.sqrt(total_sq)
    factor = CLIP / jnp.maximum(grad_norm, CLIP)
    rate = RATE_SCALE * math.sqrt(NPARAM)
    params = (table, w_qkv, w_out, w_up, w_down, small, position)
    moms = (mom_table, mom_qkv, mom_out, mom_up, mom_down, mom_small, mom_position)
    avgs = (avg_table, avg_qkv, avg_out, avg_up, avg_down, avg_small, avg_position)
    news, moments, averages = ([], [], [])
    for weight, grad, momentum, average in zip(params, grads, moms, avgs):
        clipped = grad * factor
        moment = MOMENTUM * momentum + clipped
        fresh = weight - rate * (clipped + MOMENTUM * moment)
        news.append(fresh)
        moments.append(moment)
        averages.append(AVERAGE * average + (1.0 - AVERAGE) * fresh)
    return tuple(news) + tuple(moments) + tuple(averages) + (grad_norm, loss_value)


def solution(mesh):
    placed = (
        P(("dp", "fsdp"), None),
        P(("dp", "fsdp"), None),
        P(("dp", "fsdp")),
        P(("dp", "fsdp"), None),
        P(("dp", "fsdp"), None),
        P(("dp", "fsdp"), None),
        P(("dp", "fsdp"), None),
        P(("dp", "fsdp"), None),
        P(("dp", "fsdp"), None),
        P(("dp", "fsdp"), None),
        P(None, ("dp", "fsdp")),
        P(None, ("dp", "fsdp")),
        P(("dp", "fsdp"), None),
        P(("dp", "fsdp"), None),
        P(("dp", "fsdp"), None),
        P(("dp", "fsdp"), None),
        P(("dp", "fsdp"), None),
        P(None, ("dp", "fsdp")),
        P(None, ("dp", "fsdp")),
        P(("dp", "fsdp"), None),
        P(("dp", "fsdp"), None),
        P(("dp", "fsdp"), None),
        P(("dp", "fsdp"), None),
        P(("dp", "fsdp"), None),
        P(None, ("dp", "fsdp")),
        P(None, ("dp", "fsdp")),
        P(("dp", "fsdp"), None),
        P(("dp", "fsdp"), None),
        P(("dp", "fsdp"), None),
        P(("dp", "fsdp"), None),
        P(("dp", "fsdp"), None),
        P(None, ("dp", "fsdp")),
        P(None, ("dp", "fsdp")),
    )
    return jax.shard_map(
        on_device,
        mesh=mesh,
        in_specs=placed,
        out_specs=(
            P(("dp", "fsdp"), None),
            P(("dp", "fsdp"), None),
            P(("dp", "fsdp"), None),
            P(("dp", "fsdp"), None),
            P(("dp", "fsdp"), None),
            P(None, ("dp", "fsdp")),
            P(None, ("dp", "fsdp")),
            P(("dp", "fsdp"), None),
            P(("dp", "fsdp"), None),
            P(("dp", "fsdp"), None),
            P(("dp", "fsdp"), None),
            P(("dp", "fsdp"), None),
            P(None, ("dp", "fsdp")),
            P(None, ("dp", "fsdp")),
            P(("dp", "fsdp"), None),
            P(("dp", "fsdp"), None),
            P(("dp", "fsdp"), None),
            P(("dp", "fsdp"), None),
            P(("dp", "fsdp"), None),
            P(None, ("dp", "fsdp")),
            P(None, ("dp", "fsdp")),
            P(),
            P(),
        ),
        check_vma=False,
    )
```

time: 2260 us -> 1490 us (0.66)
  blocking collectives: 692 us -> 51.7 us
  local copies, waits for them, and re-layouts: 274 us -> 202 us
    all_gather x26 -> x3, blocking collectives: 482 us -> 42.3 us  [the longest x1 15.7 us: on_device(): info = lax.all_gather(info, 'fsdp', axis=0, tiled=True)]
    reduce_scatter x4 -> x1, waiting for transfers between devices: 364 us -> 63.3 us  [on_device(): lax.psum_scatter(table_grad.astype(LOW), 'dp', scatter_dimension=0, tiled...]
    reduce_scatter x1, waiting for transfers between devices: 0.02 us -> 128 us  [on_device(): lax.psum_scatter(picked_teacher, 'fsdp', scatter_dimension=0, tiled=True)]
    unnamed x3 -> x1, blocking collectives: 128 us -> 9.39 us
    psum x2 -> x0, blocking collectives: 82.1 us -> none  [the longest x1 41.8 us: on_device(): lax.psum((jnp.sum(valid_local), jnp.sum((seq_len > 0).astype(jnp.float32)...]
    reduce_scatter x1, waiting for transfers between devices: 15.9 us -> 91.7 us  [on_device(): lax.psum_scatter(picked_student, 'fsdp', scatter_dimension=0, tiled=True)]
    dot_general x38 -> x29, matrix products: 187 us -> 262 us  [product_of(): return jnp.einsum(form, left, right, preferred_element_type=jnp.float32)]
    dot_general x14 -> x0, matrix products: 74.5 us -> none  [the longest x4 30.1 us: layer_forward(): jnp.dot(act_low, w_down, preferred_element_type=jnp.float32) + small[7]]
  transfers between devices with their start and end apart: 21 -> 11, of which waited for: 12 -> 11; matrix products, arithmetic and copies ran while one was open for 23% -> 22% of each run, Pallas kernels for 0% -> 0%
where the time goes in v1:
time: 1490 us
  waiting for transfers between devices  693 us (47%)
  matrix products  278 us (19%)
  other arithmetic  236 us (16%)
  local copies, waits for them, and re-layouts  202 us (14%)
  blocking collectives  51.7 us (3%)
  between operations  24.7 us (2%)
    dot_general x29, matrix products, product_of(): return jnp.einsum(form, left, right, preferred_element_type=jnp.float32)  262 us
    reduce_scatter x1, waiting for transfers between devices, on_device(): lax.psum_scatter(picked_teacher, 'fsdp', scatter_dimension=0, tiled=True)  128 us
    reduce_scatter x1, waiting for transfers between devices, on_device(): lax.psum_scatter(picked_student, 'fsdp', scatter_dimension=0, tiled=True)  91.7 us
    all_gather x1, waiting for transfers between devices, on_device(): packed_student = lax.all_gather(packed_student, BOTH, axis=0, tiled=True)  87.5 us
    unnamed x12, waiting for transfers between devices  83.2 us
    scatter-add x1, other arithmetic, on_device(): jax.ops.segment_sum(flat, safe_ids.reshape(-1), num_segments=vocab_rows)  64.4 us
    reduce_scatter x1, waiting for transfers between devices, on_device(): lax.psum_scatter(table_grad.astype(LOW), 'dp', scatter_dimension=0, tiled...  63.3 us
    all_gather x1, waiting for transfers between devices, on_device(): lax.all_gather(d_embed.astype(LOW), 'fsdp', axis=0, tiled=True)  51.3 us
  transfers between devices with their start and end apart: 11, of which 11 were waited for; matrix products, arithmetic and copies ran while one was open for 22% of the time, Pallas kernels for 0%

profile of v1, /device:TPU:0, one launch (start us, length us, event | category | flops | bytes accessed | tf_op | source)
XLA Modules:
  0.0 1486.7 jit_solution(18175856902515951601)
XLA Ops:
  17.6 15.7 %all-gather.3 = s32[8,2,640]{2,1,0:T(2,128)S(1)} all-gather(s32[1,2,640]{2,1,0:T(2,128)S(1)} %add_bitcast_fusion), channel_id=1, replica_groups=mesh['dp'=4,'fsdp'=8] {'fsdp'}, dimensions={0}, use_global_device_ids=true | all-gather | bytes 46080 | tf_op jit(solution)/shard_map/all_gather | solution.py:395
  34.0 46.2 %all-gather.14.cloned.1.call-done = bf16[3840,768]{1,0:T(8,128)(2,1)} async-done(((bf16[960,768]{1,0:T(8,128)(2,1)}), bf16[3840,768]{1,0:T(8,128)(2,1)}) %all-gather.14.cloned.1.call-update) | async-done | bytes 5898256 | tf_op jit(solution)/shard_map/all_gather | solution.py:399
  80.2 40.5 %gather_fusion = bf16[8192,768]{1,0:T(8,128)(2,1)} fusion(bf16[3840,768]{1,0:T(8,128)(2,1)} %all-gather.14.cloned.1.call-done, s32[8192]{0:T(1024)S(1)} %broadcast_clamp_fusion), kind=kCustom, calls=%fused_computation | custom fusion | bytes 25198592 | tf_op jit(solution)/shard_map/gather | solution.py:412
  120.7 28.8 %all-gather.16.cloned.1.call-done = bf16[3840,768]{1,0:T(8,128)(2,1)} async-done(((bf16[960,768]{1,0:T(8,128)(2,1)}), bf16[3840,768]{1,0:T(8,128)(2,1)}) %all-gather.16.cloned.1.call-update) | async-done | bytes 5898256 | tf_op jit(solution)/shard_map/all_gather | solution.py:402
  149.6 40.6 %gather_fusion.1 = bf16[8192,768]{1,0:T(8,128)(2,1)} fusion(bf16[3840,768]{1,0:T(8,128)(2,1)} %all-gather.16.cloned.1.call-done, s32[8192]{0:T(1024)S(1)} %broadcast_clamp_fusion), kind=kCustom, calls=%fused_computation.1 | custom fusion | bytes 25198592 | tf_op jit(solution)/shard_map/gather | solution.py:413
  190.1 17.4 %broadcast_select_fusion.1 = (bf16[16,512,768]{2,1,0:T(8,128)(2,1)}, bf16[16,512,768]{2,1,0:T(8,128)(2,1)}) fusion(bf16[16,512,768]{2,1,0:T(8,128)(2,1)} %bitcast.316, pred[16,512]{1,0:T(8,128)(4,1)S(1)} %get-tuple-element.257, bf16[16,512,768]{2,1,0:T(8,128)(2,1)} %bitcast.317), kind=kLoop, calls=%fused_computation.44 | loop fusion | flops 12582912 | bytes 50339840 | tf_op jit(solution)/shard_map/jit(_where)/select_n | solution.py:412
  208.9 51.0 %all-gather.18.cloned.1.call-done = bf16[768,9856]{1,0:T(8,128)(2,1)} async-done(((bf16[24,9856]{1,0:T(8,128)(2,1)}), bf16[768,9856]{1,0:T(8,128)(2,1)}) %all-gather.18.cloned.1.call-update) | async-done | bytes 15138832 | tf_op jit(solution)/shard_map/all_gather | solution.py:424
  281.4 87.5 %all-gather.12.cloned.1.call-done = bf16[768,9856]{1,0:T(8,128)(2,1)} async-done(((bf16[24,9856]{1,0:T(8,128)(2,1)}), bf16[768,9856]{1,0:T(8,128)(2,1)}) %all-gather.12.cloned.1.call-update) | async-done | bytes 15138832 | tf_op jit(solution)/shard_map/all_gather | solution.py:423
  406.8 91.7 %reduce-scatter.8.cloned.1.call-done = bf16[2,512,768]{2,1,0:T(8,128)(2,1)} async-done(((bf16[16,512,768]{2,1,0:T(8,128)(2,1)}), bf16[2,512,768]{2,1,0:T(8,128)(2,1)}) %reduce-scatter.8.cloned.1.call-update) | async-done | bytes 1572880 | tf_op jit(solution)/shard_map/reduce_scatter | solution.py:414
  500.6 127.6 %reduce-scatter.10.cloned.1.call-done = bf16[2,512,768]{2,1,0:T(8,128)(2,1)} async-done(((bf16[16,512,768]{2,1,0:T(8,128)(2,1)}), bf16[2,512,768]{2,1,0:T(8,128)(2,1)}) %reduce-scatter.10.cloned.1.call-update) | async-done | bytes 1572880 | tf_op jit(solution)/shard_map/reduce_scatter | solution.py:417
  647.8 16.1 %fusion.172 = (f32[2,12,512]{2,1,0:T(8,128)S(1)}, f32[2,12,512,512]{2,3,1,0:T(8,128)}) fusion(pred[2,512]{1,0:T(4,128)(4,1)S(1)} %iota_compare_fusion.6, bf16[2,512,3,12,64]{1,4,3,2,0:T(8,128)(2,1)} %bitcast.340), kind=kOutput, calls=%fused_computation.398 | convolution fusion | flops 830472704 | bytes 28361728 | tf_op jit(solution)/shard_map/sub | solution.py:122
  681.2 17.8 %fusion.174 = (f32[2,512]{1,0:T(2,128)S(1)}, f32[2,512,768]{2,1,0:T(8,128)}) fusion(f32[768]{0:T(1024)S(1)} %get-tuple-element.197, bf16[3072,768,1]{1,0,2:T(8,128)(2,1)} %bitcast.337, f32[3072]{0:T(1024)S(1)} %add.536, bf16[768,9856]{1,0:T(8,128)(2,1)} %all-gather.18.cloned.1.call-done, f32[2,512,768]{2,1,0:T(8,128)} %copy-done.23, ...), kind=kOutput, calls=%fused_computation.400 | convolution fusion | flops 9691986944 | bytes 18927616 | tf_op jit(solution)/shard_map/bsf,fd->bsd/dot_general | solution.py:26
  785.5 33.5 %all-gather.20.cloned.1.call-done = bf16[2,1024,768]{2,1,0:T(8,128)(2,1)} async-done(((bf16[2,128,768]{2,1,0:T(8,128)(2,1)}), bf16[2,1024,768]{2,1,0:T(8,128)(2,1)}) %all-gather.20.cloned.1.call-update) | async-done | bytes 3145744 | tf_op jit(solution)/shard_map/all_gather | solution.py:235
  831.7 15.8 %select_reduce_fusion.1 = (f32[1024]{0:T(1024)S(1)}, f32[1024]{0:T(1024)S(1)}, f32[1024,3840]{1,0:T(8,128)}) fusion(pred[3840]{0:T(1024)(128)(4,1)S(1)} %fusion.117, f32[1024,3840]{1,0:T(8,128)} %fusion.80, bf16[3840,768]{1,0:T(8,128)(2,1)} %all-gather.16.cloned.1.call-done, bf16[2,1024,768]{2,1,0:T(8,128)(2,1)S(1)} %copy-done.91), kind=kOutput, calls=%fused_computation.28 | convolution fusion | flops 6055524352 | bytes 38940672 | tf_op jit(solution)/shard_map/pd,vd->pv/dot_general | solution.py:26
  847.5 18.9 %multiply_reduce_fusion.1 = (f32[1024]{0:T(1024)S(1)}, f32[1024]{0:T(1024)S(1)}, f32[1024]{0:T(1024)S(1)}, f32[1024]{0:T(1024)S(1)}, f32[1024]{0:T(1024)S(1)}) fusion(f32[1024,3840]{1,0:T(8,128)} %get-tuple-element.310, f32[1024,3840]{1,0:T(8,128)} %fusion.80, f32[1024]{0:T(1024)S(1)} %get-tuple-element.216, pred[3840]{0:T(1024)(128)(4,1)S(1)} %fusion.117, ...), kind=kLoop, calls=%fused_computation.21 | loop fusion | flops 70773760 | bytes 31494912 | tf_op jit(solution)/shard_map/reduce_sum | solution.py:255
  881.5 18.4 %multiply_convert_fusion.1 = bf16[1024,3840]{1,0:T(8,128)(2,1)S(1)} fusion(f32[1024,3840]{1,0:T(8,128)} %get-tuple-element.310, f32[1024,3840]{1,0:T(8,128)} %fusion.80, f32[1024]{0:T(1024)S(1)} %get-tuple-element.283, f32[1024]{0:T(1024)S(1)} %get-tuple-element.254, f32[1024]{0:T(1024)S(1)} %get-tuple-element.253, s32[1024]{0:T(1024)S(1)} %fusion.134, ...), kind=kLoop, calls=%fused_computation.18 | loop fusion | flops 62914560 | bytes 39346944 | tf_op jit(solution)/shard_map/convert_element_type | solution.py:283
  915.0 28.8 %reduce-scatter.12.cloned.1.call-done = bf16[128,768]{1,0:T(8,128)(2,1)} async-done(((bf16[1024,768]{1,0:T(8,128)(2,1)}), bf16[128,768]{1,0:T(8,128)(2,1)}) %reduce-scatter.12.cloned.1.call-update) | async-done | bytes 196624 | tf_op jit(solution)/shard_map/reduce_scatter | solution.py:284
  993.0 18.1 %multiply_reduce_fusion = (f32[2,12,512]{2,1,0:T(8,128)S(1)}, f32[2,12,512,512]{2,3,1,0:T(8,128)}) fusion(f32[2,12,512]{2,1,0:T(8,128)S(1)} %log_add_fusion, f32[2,12,512,512]{2,3,1,0:T(8,128)} %get-tuple-element.303, pred[2,512]{1,0:T(4,128)(4,1)S(1)} %iota_compare_fusion.6, bf16[2,512,12,64]{1,3,2,0:T(8,128)(2,1)S(1)} %bitcast.332, ...), kind=kOutput, calls=%fused_computation.6 | convolution fusion | flops 836751360 | bytes 53576704 | tf_op jit(solution)/shard_map/bqhd,bkhd->bhqk/dot_general | solution.py:26
  1011.1 21.7 %multiply_convert_fusion = bf16[2,12,512,512]{2,3,1,0:T(8,128)(2,1)} fusion(f32[2,12,512,512]{2,3,1,0:T(8,128)} %get-tuple-element.314, f32[2,12,512]{2,1,0:T(8,128)S(1)} %get-tuple-element.313, f32[2,12,512]{2,1,0:T(8,128)S(1)} %log_add_fusion, f32[2,12,512,512]{2,3,1,0:T(8,128)} %get-tuple-element.303, pred[2,512]{1,0:T(4,128)(4,1)S(1)} %iota_compare_fusion.6), kind=kLoop, calls=%fused_computation.5 | loop fusion | flops 37748736 | bytes 63013888 | tf_op jit(solution)/shard_map/convert_element_type | solution.py:190
  1131.3 51.3 %all-gather.22.cloned.1.call-done = bf16[16,512,768]{2,1,0:T(8,128)(2,1)} async-done(((bf16[2,512,768]{2,1,0:T(8,128)(2,1)}), bf16[16,512,768]{2,1,0:T(8,128)(2,1)}) %all-gather.22.cloned.1.call-update) | async-done | bytes 12582928 | tf_op jit(solution)/shard_map/all_gather | solution.py:475
  1182.5 14.2 convert_select_fusion
  1196.8 64.4 %scatter_fusion = f32[3840,768]{1,0:T(8,128)} fusion(f32[3840,768]{1,0:T(8,128)} %fusion.79, s32[8192]{0:T(1024)S(1)} %bitcast.348, f32[8192,768]{1,0:T(8,128)} %bitcast.315), kind=kCustom, calls=%fused_computation.2 | custom fusion | flops 6291456 | bytes 75530240 | tf_op jit(solution)/shard_map/scatter-add | solution.py:479
  1273.5 82.5 %reduce-scatter.16.cloned.1.call-done = bf16[24,9856]{1,0:T(8,128)(2,1)} async-done(((bf16[768,9856]{1,0:T(8,128)(2,1)}), bf16[24,9856]{1,0:T(8,128)(2,1)}) %reduce-scatter.16.cloned.1.call-update) | async-done | bytes 473104
  1361.8 63.3 %reduce-scatter.14.cloned.1.call-done = bf16[960,768]{1,0:T(8,128)(2,1)} async-done(((bf16[3840,768]{1,0:T(8,128)(2,1)}), bf16[960,768]{1,0:T(8,128)(2,1)}) %reduce-scatter.14.cloned.1.call-update) | async-done | bytes 1474576 | tf_op jit(solution)/shard_map/reduce_scatter | solution.py:482
  (446 shorter events, 450.3 us)
Async XLA Ops:
  7.2 73.1 %all-gather.14.cloned.1.call-start = ((), (), s32[]{:S(2)}) async-start(), calls=%async_computation.6 | async-start | bytes 7372800 | tf_op jit(solution)/shard_map/all_gather | solution.py:399
  10.6 139.0 %all-gather.16.cloned.1.call-start = ((), (), s32[]{:S(2)}) async-start(), calls=%async_computation.8 | async-start | bytes 7372800 | tf_op jit(solution)/shard_map/all_gather | solution.py:402
  12.4 247.6 %all-gather.18.cloned.1.call-start = ((), (), s32[]{:S(2)}) async-start(), calls=%async_computation.10 | async-start | bytes 15611904 | tf_op jit(solution)/shard_map/all_gather | solution.py:424
  13.5 355.4 %all-gather.12.cloned.1.call-start = ((), (), s32[]{:S(2)}) async-start(), calls=%async_computation.5 | async-start | bytes 15611904 | tf_op jit(solution)/shard_map/all_gather | solution.py:423
  17.4 481.1 %reduce-scatter.8.cloned.1.call-start = ((), (), s32[]{:S(2)}) async-start(), calls=%async_computation.7 | async-start | bytes 14155776 | tf_op jit(solution)/shard_map/reduce_scatter | solution.py:414
  34.0 156.2 %copy-start.52 = (pred[16,512]{1,0:T(8,128)(4,1)}, pred[16,512]{1,0:T(8,128)(4,1)S(1)}, u32[]{:S(2)}) copy-start(pred[16,512]{1,0:T(8,128)(4,1)S(1)} %get-tuple-element.257) | copy-start | bytes 24580
  207.6 420.7 %reduce-scatter.10.cloned.1.call-start = ((), (), s32[]{:S(2)}) async-start(), calls=%async_computation.9 | async-start | bytes 14155776 | tf_op jit(solution)/shard_map/reduce_scatter | solution.py:417
  208.1 610.9 %all-gather.20.cloned.1.call-start = ((), (), s32[]{:S(2)}) async-start(), calls=%async_computation.11 | async-start | bytes 3538944 | tf_op jit(solution)/shard_map/all_gather | solution.py:235
  373.2 379.6 %copy-start.2 = (f32[512,768]{1,0:T(8,128)}, f32[512,768]{1,0:T(8,128)S(1)}, u32[]{:S(2)}) copy-start(f32[512,768]{1,0:T(8,128)S(1)} %copy.299) | copy-start | bytes 4718596
  406.7 346.1 %copy-start.54 = (f32[768]{0:T(1024)}, f32[768]{0:T(1024)S(1)}, u32[]{:S(2)}) copy-start(f32[768]{0:T(1024)S(1)} %get-tuple-element.193) | copy-start | bytes 9220
  406.7 346.1 %copy-start.56 = (f32[768]{0:T(1024)}, f32[768]{0:T(1024)S(1)}, u32[]{:S(2)}) copy-start(f32[768]{0:T(1024)S(1)} %get-tuple-element.194) | copy-start | bytes 9220
  406.7 346.1 %copy-start.68 = (f32[768]{0:T(1024)}, f32[768]{0:T(1024)S(1)}, u32[]{:S(2)}) copy-start(f32[768]{0:T(1024)S(1)} %get-tuple-element.192) | copy-start | bytes 9220
  406.7 346.1 %copy-start.80 = (f32[768]{0:T(1024)}, f32[768]{0:T(1024)S(1)}, u32[]{:S(2)}) copy-start(f32[768]{0:T(1024)S(1)} %get-tuple-element.191) | copy-start | bytes 9220
  500.6 252.3 %copy-start.61 = (f32[2,512]{1,0:T(2,128)}, f32[2,512]{1,0:T(2,128)S(1)}, u32[]{:S(2)}) copy-start(f32[2,512]{1,0:T(2,128)S(1)} %broadcast_multiply_fusion.11) | copy-start | bytes 12292
  782.2 161.5 %reduce-scatter.12.cloned.1.call-start = ((), (), s32[]{:S(2)}) async-start(), calls=%async_computation.12 | async-start | bytes 1769472 | tf_op jit(solution)/shard_map/reduce_scatter | solution.py:284
  910.3 272.2 %all-gather.22.cloned.1.call-start = ((), (), s32[]{:S(2)}) async-start(), calls=%async_computation.13 | async-start | bytes 14155776 | tf_op jit(solution)/shard_map/all_gather | solution.py:475
  1067.7 288.3 %reduce-scatter.16.cloned.1.call-start = ((), (), s32[]{:S(2)}) async-start(), calls=%async_computation.15 | async-start | bytes 15611904
  1117.3 307.8 %reduce-scatter.14.cloned.1.call-start = ((), (), s32[]{:S(2)}) async-start(), calls=%async_computation.14 | async-start | bytes 7372800 | tf_op jit(solution)/shard_map/reduce_scatter | solution.py:482
  1268.7 196.6 %copy-start.36 = (f32[24,2304]{1,0:T(8,128)S(1)}, f32[24,2304]{1,0:T(8,128)}, u32[]{:S(2)}) copy-start(f32[24,2304]{1,0:T(8,128)} %param.39) | copy-start | bytes 663556
  1268.8 196.6 %copy-start.45 = (f32[24,2304]{1,0:T(8,128)S(1)}, f32[24,2304]{1,0:T(8,128)}, u32[]{:S(2)}) copy-start(f32[24,2304]{1,0:T(8,128)} %param.60) | copy-start | bytes 663556
  1269.4 197.9 %copy-start.42 = (f32[24,768]{1,0:T(8,128)S(1)}, f32[24,768]{1,0:T(8,128)}, u32[]{:S(2)}) copy-start(f32[24,768]{1,0:T(8,128)} %param.40) | copy-start | bytes 221188
  1273.5 195.5 %copy-start.32 = (f32[24,3072]{1,0:T(8,128)S(1)}, f32[24,3072]{1,0:T(8,128)}, u32[]{:S(2)}) copy-start(f32[24,3072]{1,0:T(8,128)} %param.41) | copy-start | bytes 884740
  1273.5 195.5 %copy-start.37 = (f32[24,3072]{1,0:T(8,128)S(1)}, f32[24,3072]{1,0:T(8,128)}, u32[]{:S(2)}) copy-start(f32[24,3072]{1,0:T(8,128)} %param.62) | copy-start | bytes 884740
  1273.5 195.5 %copy-start.38 = (f32[24,3072]{1,0:T(8,128)S(1)}, f32[24,3072]{1,0:T(8,128)}, u32[]{:S(2)}) copy-start(f32[24,3072]{1,0:T(8,128)} %param.55) | copy-start | bytes 884740
  (92 other events, 1057.4 us)
Sparse Core Ops, SparseCore 0:
  10.6 69.5 all-gather.13
  82.7 66.8 all-gather.15
  152.4 107.4 all-gather.17
  263.2 105.6 all-gather.11
  371.0 127.3 reduce-scatter.7
  500.6 127.5 reduce-scatter.9
  782.4 36.6 all-gather.19
  910.5 33.2 reduce-scatter.11
  1067.8 114.6 all-gather.21
  1188.6 167.3 reduce-scatter.15
  1359.3 65.7 reduce-scatter.13

commit v2 on v1

--- a/solution.py
+++ b/solution.py
@@ -1,8 +1,11 @@
+import functools
 import math
 
 import jax
 import jax.numpy as jnp
 from jax import lax
+from jax.experimental import pallas as pl
+from jax.experimental.pallas import tpu as pltpu
 from jax.sharding import PartitionSpec as P
 
 HD = 64
@@ -20,6 +23,252 @@
 NEGATIVE = -1e30
 BOTH = ("dp", "fsdp")
 LOW = jnp.bfloat16
+MIB = 1 << 20
+
+
+def push(src, dst, send, recv, where):
+    copy = pltpu.make_async_remote_copy(
+        src_ref=src,
+        dst_ref=dst,
+        send_sem=send,
+        recv_sem=recv,
+        device_id=where,
+        device_id_type=pl.DeviceIdType.MESH,
+    )
+    copy.start()
+    return copy
+
+
+def greet(peers):
+    barrier = pltpu.get_barrier_semaphore()
+    for peer in peers:
+        pl.semaphore_signal(barrier, inc=1, device_id=peer, device_id_type=pl.DeviceIdType.MESH)
+    pl.semaphore_wait(barrier, len(peers))
+
+
+def flipped(index, bit):
+    return index + bit - 2 * bit * (lax.div(index, bit) % 2)
+
+
+def spread_body(dp, count, *refs):
+    blocks, outs = refs[:count], refs[count : 2 * count]
+    local, send, recv = refs[2 * count :]
+    me = lax.axis_index("dp")
+    own = [pltpu.make_async_copy(blocks[k], outs[k].at[me], local.at[k]) for k in range(count)]
+    for copy in own:
+        copy.start()
+    if dp == 4:
+        near = [flipped(me, 1), flipped(me, 2)]
+        greet([{"dp": near[0]}, {"dp": near[1]}])
+        first = []
+        for k in range(count):
+            for step in range(2):
+                for link in range(2):
+                    half = step if link == 0 else 1 - step
+                    first.append(
+                        push(
+                            blocks[k].at[half],
+                            outs[k].at[me, half],
+                            send.at[k, link, half],
+                            recv.at[k, link, half],
+                            {"dp": near[link]},
+                        )
+                    )
+        for k in range(count):
+            for link in range(2):
+                first[k * 4 + link].wait_recv()
+                origin = near[link]
+                other = 1 - link
+                first.append(
+                    push(
+                        outs[k].at[origin, link],
+                        outs[k].at[origin, link],
+                        send.at[k, 2, other],
+                        recv.at[k, 2, other],
+                        {"dp": near[other]},
+                    )
+                )
+        for place, copy in enumerate(first):
+            if place >= 4 * count or place % 4 >= 2:
+                copy.wait_recv()
+        for copy in first:
+            copy.wait_send()
+    else:
+        peers = [lax.rem(me + hop, dp) for hop in range(1, dp)]
+        greet([{"dp": peer} for peer in peers])
+        sent = []
+        for k in range(count):
+            for hop, peer in enumerate(peers):
+                sent.append(
+                    push(
+                        blocks[k],
+                        outs[k].at[me],
+                        send.at[k, hop, 0],
+                        recv.at[k, hop, 0],
+                        {"dp": peer},
+                    )
+                )
+        for copy in sent:
+            copy.wait()
+    for copy in own:
+        copy.wait()
+
+
+def spread_dp(blocks, dp, identity):
+    count = len(blocks)
+    rows, width = blocks[0].shape
+    cut = [block.reshape(2, rows // 2, width) for block in blocks]
+    outs = pl.pallas_call(
+        functools.partial(spread_body, dp, count),
+        out_shape=[jax.ShapeDtypeStruct((dp, 2, rows // 2, width), LOW)] * count,
+        in_specs=[pl.BlockSpec(memory_space=pl.ANY)] * count,
+        out_specs=[pl.BlockSpec(memory_space=pl.ANY)] * count,
+        scratch_shapes=[
+            pltpu.SemaphoreType.DMA((count,)),
+            pltpu.SemaphoreType.DMA((count, max(3, dp - 1), 2)),
+            pltpu.SemaphoreType.DMA((count, max(3, dp - 1), 2)),
+        ],
+        compiler_params=pltpu.CompilerParams(collective_id=identity, has_side_effects=True),
+        name="spread_tables",
+    )(*cut)
+    return [out.reshape(dp * rows, width) for out in outs]
+
+
+def fold_body(dp, pieces, g, out, near_buffer, far_buffer, last_buffer, sems):
+    me = lax.axis_index("dp")
+    half_rows = pieces
+    if dp == 4:
+        near = [flipped(me, 1), flipped(me, 2)]
+        far = flipped(near[0], 2)
+        greet([{"dp": near[0]}, {"dp": near[1]}])
+        firsts = []
+        seconds = []
+        for i in range(pieces):
+            for link in range(2):
+                firsts.append(
+                    push(
+                        g.at[far, link, i],
+                        far_buffer.at[link, i],
+                        sems.at[0, 0, link, i],
+                        sems.at[1, 0, link, i],
+                        {"dp": near[link]},
+                    )
+                )
+        for i in range(pieces):
+            for link in range(2):
+                firsts.append(
+                    push(
+                        g.at[near[link], link, i],
+                        near_buffer.at[link, i],
+                        sems.at[0, 1, link, i],
+                        sems.at[1, 1, link, i],
+                        {"dp": near[link]},
+                    )
+                )
+        for i in range(pieces):
+            for link in range(2):
+                firsts[2 * i + link].wait_recv()
+                far_buffer[link, i] = (
+                    far_buffer[link, i].astype(jnp.float32)
+                    + g[near[1 - link], link, i].astype(jnp.float32)
+                ).astype(LOW)
+                seconds.append(
+                    push(
+                        far_buffer.at[link, i],
+                        last_buffer.at[link, i],
+                        sems.at[0, 2, link, i],
+                        sems.at[1, 2, link, i],
+                        {"dp": near[1 - link]},
+                    )
+                )
+        for i in range(pieces):
+            for link in range(2):
+                firsts[2 * pieces + 2 * i + link].wait_recv()
+                seconds[2 * i + link].wait_recv()
+                out[link, i] = (
+                    g[me, link, i].astype(jnp.float32)
+                    + near_buffer[link, i].astype(jnp.float32)
+                    + last_buffer[link, i].astype(jnp.float32)
+                )
+        for copy in firsts + seconds:
+            copy.wait_send()
+    else:
+        peers = [lax.rem(me + hop, dp) for hop in range(1, dp)]
+        greet([{"dp": peer} for peer in peers])
+        sent = []
+        for hop, peer in enumerate(peers):
+            sent.append(
+                push(
+                    g.at[peer],
+                    near_buffer.at[hop],
+                    sems.at[0, hop, 0, 0],
+                    sems.at[1, hop, 0, 0],
+                    {"dp": peer},
+                )
+            )
+        out[...] = g[me].astype(jnp.float32)
+        for hop in range(dp - 1):
+            sent[hop].wait()
+            out[...] = out[...] + near_buffer[hop].astype(jnp.float32)
+
+
+def fold_dp(g, dp, pieces, identity):
+    rows, width = g.shape[0] // dp, g.shape[1]
+    piece = rows // (2 * pieces)
+    g = g.reshape(dp, 2, pieces, piece, width)
+    small = pltpu.VMEM((2, pieces, piece, width), LOW)
+    first = small if dp == 4 else pltpu.VMEM((dp - 1, 2, pieces, piece, width), LOW)
+    out = pl.pallas_call(
+        functools.partial(fold_body, dp, pieces),
+        out_shape=jax.ShapeDtypeStruct((2, pieces, piece, width), jnp.float32),
+        in_specs=[pl.BlockSpec(memory_space=pltpu.VMEM)],
+        out_specs=pl.BlockSpec(memory_space=pltpu.VMEM),
+        scratch_shapes=[first, small, small, pltpu.SemaphoreType.DMA((2, max(3, dp - 1), 2, pieces))],
+        compiler_params=pltpu.CompilerParams(
+            collective_id=identity, has_side_effects=True, vmem_limit_bytes=56 * MIB
+        ),
+        name="fold_table",
+    )(g)
+    return out.reshape(rows, width)
+
+
+def total_body(dp, groups, x, out, buffer, send, recv):
+    steps = []
+    bit = 1
+    while bit < groups:
+        steps.append({"fsdp": flipped(lax.axis_index("fsdp"), bit)})
+        bit *= 2
+    bit = 1
+    while bit < dp:
+        steps.append({"dp": flipped(lax.axis_index("dp"), bit)})
+        bit *= 2
+    greet(steps)
+    buffer[0, 0] = x[...]
+    for k, peer in enumerate(steps):
+        copy = push(buffer.at[0, k], buffer.at[1, k], send.at[k], recv.at[k], peer)
+        copy.wait()
+        value = buffer[0, k] + buffer[1, k]
+        if k + 1 < len(steps):
+            buffer[0, k + 1] = value
+        else:
+            out[...] = value
+
+
+def total_all(x, dp, groups, identity):
+    count = (dp - 1).bit_length() + (groups - 1).bit_length()
+    return pl.pallas_call(
+        functools.partial(total_body, dp, groups),
+        out_shape=jax.ShapeDtypeStruct((8, 128), jnp.float32),
+        in_specs=[pl.BlockSpec(memory_space=pltpu.VMEM)],
+        out_specs=pl.BlockSpec(memory_space=pltpu.VMEM),
+        scratch_shapes=[
+            pltpu.VMEM((2, count, 8, 128), jnp.float32),
+            pltpu.SemaphoreType.DMA((count,)),
+            pltpu.SemaphoreType.DMA((count,)),
+        ],
+        compiler_params=pltpu.CompilerParams(collective_id=identity, has_side_effects=True),
+        name="total",
+    )(x)
 
 
 def product_of(form, left, right):
@@ -30,7 +279,7 @@
     block = ids // share
     inside = block % groups == own
     local = block // groups * padded + ids % share
-    return (inside, jnp.where(inside, local, 0))
+    return (inside, jnp.where(inside, local, share))
 
 
 def layer_norm_keep(value, gain, shift):
@@ -73,31 +322,31 @@
 
 def pack_layer(weights, extra):
     w_qkv, w_out, w_up, w_down, small, position = (w.astype(LOW) for w in weights)
-    rows = w_qkv.shape[0]
-    parts = w_down.shape[0] // rows
-    pieces = [w_qkv, w_out, w_up]
-    pieces += [w_down[k * rows : (k + 1) * rows] for k in range(parts)]
-    pieces += [position.T, small.T]
-    filled = small.shape[0]
-    if extra is not None:
-        pieces.append(extra)
-        filled += extra.shape[1]
-    pieces.append(jnp.zeros((rows, -filled % 128), LOW))
-    return jnp.concatenate(pieces, axis=1)
-
-
-def unpack_layer(packed, devices, span, slots):
-    width = packed.shape[0]
+    rows, width = w_out.shape
+    pieces = [w_qkv[:, k * width : (k + 1) * width] for k in range(3)]
+    pieces += [w_out]
+    pieces += [w_up[:, k * width : (k + 1) * width] for k in range(w_up.shape[1] // width)]
+    pieces += [w_down]
+    rest = [position.T, small.T] + ([] if extra is None else [extra])
+    rest = jnp.concatenate(rest, axis=1)
+    pieces += [jnp.pad(rest, ((0, 0), (0, width - rest.shape[1])))]
+    packed = jnp.concatenate(pieces, axis=0)
+    return jnp.pad(packed, ((0, -packed.shape[0] % 32), (0, 0)))
+
+
+def unpack_layer(packed, span, slots):
+    devices, _, width = packed.shape
+    rows = width // devices
     ff = 4 * width
-    edges = [3 * width, 4 * width, 4 * width + ff, 4 * width + 2 * ff]
-    w_qkv = packed[:, : edges[0]]
-    w_out = packed[:, edges[0] : edges[1]]
-    w_up = packed[:, edges[1] : edges[2]]
-    down = packed[:, edges[2] : edges[3]]
-    w_down = (
-        down.reshape(devices, width // devices, 4, width).transpose(0, 2, 1, 3).reshape(ff, width)
-    )
-    rest = packed[:, edges[3] :]
+
+    def part(first, count):
+        return packed[:, first : first + count].reshape(devices * count, width)
+
+    w_qkv = jnp.concatenate([part(k * rows, rows) for k in range(3)], axis=1)
+    w_out = part(3 * rows, rows)
+    w_up = jnp.concatenate([part((4 + k) * rows, rows) for k in range(4)], axis=1)
+    w_down = part(8 * rows, ff // devices)
+    rest = part(8 * rows + ff // devices, rows)
     position = rest[:, :span].T.astype(jnp.float32)
     small = rest[:, span : span + slots].T.astype(jnp.float32)
     return (w_qkv, w_out, w_up, w_down, small, position), rest[:, span + slots :]
@@ -384,8 +633,8 @@
     dp = lax.axis_size("dp")
     devices = groups * dp
     own = lax.axis_index("fsdp")
-    pad = -share % 16
-    padded = share + pad
+    padded = (share // 32 + 1) * 32
+    pad = padded - share
     rows_own = w_qkv.shape[0]
     slots = small.shape[0]
 
@@ -396,10 +645,8 @@
     ids_all = info[:, :span]
     targets_all = info[:, span : span + labels].reshape(-1)
     lengths_all = info[:, span + labels]
-    student_table = lax.all_gather(
-        jnp.pad(table.astype(LOW), ((0, pad), (0, 0))), "dp", axis=0, tiled=True
-    )
-    teacher_table = lax.all_gather(jnp.pad(t_table, ((0, pad), (0, 0))), "dp", axis=0, tiled=True)
+    student_table = spread_dp([jnp.pad(table.astype(LOW), ((0, pad), (0, 0)))], dp, 1)[0]
+    teacher_table = spread_dp([jnp.pad(t_table, ((0, pad), (0, 0)))], dp, 2)[0]
     tables = (student_table, teacher_table)
     vocab_rows = student_table.shape[0]
 
@@ -407,23 +654,20 @@
     counts = jnp.stack([jnp.sum(valid_local), jnp.sum((seq_len > 0).astype(jnp.float32))])
     extra = jnp.broadcast_to(counts.astype(LOW)[None, :], (rows_own, 2))
 
-    inside, safe_ids = owned(ids_all, share, padded, groups, own)
-    blank = jnp.zeros((), LOW)
-    picked_student = jnp.where(inside[..., None], student_table[safe_ids], blank)
-    picked_teacher = jnp.where(inside[..., None], teacher_table[safe_ids], blank)
+    safe_ids = owned(ids_all, share, padded, groups, own)[1]
     tokens_student = lax.psum_scatter(
-        picked_student, "fsdp", scatter_dimension=0, tiled=True
+        student_table[safe_ids], "fsdp", scatter_dimension=0, tiled=True
     ).astype(jnp.float32)
     tokens_teacher = lax.psum_scatter(
-        picked_teacher, "fsdp", scatter_dimension=0, tiled=True
+        teacher_table[safe_ids], "fsdp", scatter_dimension=0, tiled=True
     ).astype(jnp.float32)
 
     packed_student = pack_layer((w_qkv, w_out, w_up, w_down, small, position), extra)
     packed_teacher = pack_layer((t_qkv, t_out, t_up, t_down, t_small, t_position), None)
-    packed_student = lax.all_gather(packed_student, BOTH, axis=0, tiled=True)
-    packed_teacher = lax.all_gather(packed_teacher, BOTH, axis=0, tiled=True)
-    weights, rest = unpack_layer(packed_student, devices, span, slots)
-    teacher, _ = unpack_layer(packed_teacher, devices, span, slots)
+    packed_student = lax.all_gather(packed_student, BOTH)
+    packed_teacher = lax.all_gather(packed_teacher, BOTH)
+    weights, rest = unpack_layer(packed_student, span, slots)
+    teacher, _ = unpack_layer(packed_teacher, span, slots)
     counted = jnp.sum(rest[::rows_own, :2].astype(jnp.float32), axis=0)
     label_count, count_seq = counted[0], counted[1]
 
@@ -475,21 +719,20 @@
     embed_grads = lax.all_gather(d_embed.astype(LOW), "fsdp", axis=0, tiled=True)
     packed_grads = pack_grads(matrices, small_grad, jnp.sum(d_embed, axis=0), devices)
     packed_grads = lax.psum_scatter(packed_grads, BOTH, scatter_dimension=0, tiled=True)
-    flat = jnp.where(inside[..., None], embed_grads.astype(jnp.float32), 0.0).reshape(-1, width)
     table_grad = table_grad + jax.ops.segment_sum(
-        flat, safe_ids.reshape(-1), num_segments=vocab_rows
-    )
-    table_shard = lax.psum_scatter(
-        table_grad.astype(LOW), "dp", scatter_dimension=0, tiled=True
-    ).astype(jnp.float32)[:share]
+        embed_grads.astype(jnp.float32).reshape(-1, width),
+        safe_ids.reshape(-1),
+        num_segments=vocab_rows,
+    )
+    table_shard = fold_dp(table_grad.astype(LOW), dp, 1, 3)[:share]
     grads = (table_shard,) + unpack_grads(packed_grads, width, span, slots)
     squares = jnp.zeros((), jnp.float32)
     for grad in grads:
         squares = squares + jnp.sum(grad * grad)
-    sums = jnp.broadcast_to(jnp.stack([squares, loss_part])[:, None], (2, 128))
-    sums = jnp.sum(lax.all_gather(sums, "dp"), axis=0)
-    sums = jnp.sum(lax.all_gather(sums, "fsdp"), axis=0)
-    total_sq, loss_value = sums[0, 0], sums[1, 0]
+    column = jnp.arange(128)[None, :]
+    sums = jnp.where(column == 0, squares, jnp.where(column == 1, loss_part, 0.0))
+    sums = total_all(jnp.broadcast_to(sums, (8, 128)), dp, groups, 4)
+    total_sq, loss_value = sums[0, 0], sums[0, 1]
     grad_norm = jnp.sqrt(total_sq)
     factor = CLIP / jnp.maximum(grad_norm, CLIP)
     rate = RATE_SCALE * math.sqrt(NPARAM)

time: 1490 us -> 1420 us (0.953)
  waiting for transfers between devices: 693 us -> 452 us
  Pallas kernels: 0 us -> 203 us
  other arithmetic: 236 us -> 204 us
  blocking collectives: 51.7 us -> 29.9 us
    reduce_scatter x3 -> x2, waiting for transfers between devices: 283 us -> 65.4 us  [the longest x1 65.4 us: on_device(): lax.psum_scatter(teacher_table[safe_ids], 'fsdp', scatter_dimension=0, ti...]
    pallas_call x0 -> x4, Pallas kernels: none -> 203 us  [the longest x2 133 us: spread_dp(): pl.pallas_call(functools.partial(spread_body, dp, count), out_shape=[jax....]
    unnamed x12 -> x9, waiting for transfers between devices: 83.2 us -> 212 us
    all_gather x4 -> x2, waiting for transfers between devices: 214 us -> 112 us  [the longest x1 112 us: on_device(): packed_student = lax.all_gather(packed_student, BOTH)]
    all_gather x1, waiting for transfers between devices: 51.3 us -> 0.01 us  [on_device(): lax.all_gather(d_embed.astype(LOW), 'fsdp', axis=0, tiled=True)]
    select_n x3 -> x2, other arithmetic: 31.6 us -> 0.03 us  [the longest x1 0.02 us: owned(): return (inside, jnp.where(inside, local, share))]
    unnamed x228 -> x298, local copies, waits for them, and re-layouts: 33.9 us -> 56.4 us
    reshape x2 -> x0, local copies, waits for them, and re-layouts: 19.7 us -> none  [unpack_layer(): down.reshape(devices, width // devices, 4, width).transpose(0, 2, 1, 3)]
  transfers between devices with their start and end apart: 11 -> 8, of which waited for: 11 -> 5; matrix products, arithmetic and copies ran while one was open for 22% -> 12% of each run, Pallas kernels for 0% -> 9%
where the time goes in v2:
time: 1420 us; the launch traced here: 1410 us
  waiting for transfers between devices  452 us (32%)
  matrix products  281 us (20%)
  local copies, waits for them, and re-layouts  215 us (15%)
  other arithmetic  204 us (14%)
  Pallas kernels  203 us (14%)
  blocking collectives  29.9 us (2%)
  between operations  26.3 us (2%)
    dot_general x30, matrix products, product_of(): return jnp.einsum(form, left, right, preferred_element_type=jnp.float32)  265 us
    unnamed x9, waiting for transfers between devices  212 us
    pallas_call x2, Pallas kernels, spread_dp(): pl.pallas_call(functools.partial(spread_body, dp, count), out_shape=[jax....  133 us
    all_gather x1, waiting for transfers between devices, on_device(): packed_student = lax.all_gather(packed_student, BOTH)  112 us
    reduce_scatter x1, waiting for transfers between devices, on_device(): lax.psum_scatter(teacher_table[safe_ids], 'fsdp', scatter_dimension=0, ti...  65.4 us
    scatter-add x1, other arithmetic, on_device(): jax.ops.segment_sum(embed_grads.astype(jnp.float32).reshape(-1, width), s...  64 us
    unnamed x298, local copies, waits for them, and re-layouts  56.4 us
    pallas_call x1, Pallas kernels, fold_dp(): pl.pallas_call(functools.partial(fold_body, dp, pieces), out_shape=jax.Sh...  53.9 us
  transfers between devices with their start and end apart: 8, of which 5 were waited for; matrix products, arithmetic and copies ran while one was open for 12% of the time, Pallas kernels for 9%

profile of v2, /device:TPU:0, one launch (start us, length us, event | category | flops | bytes accessed | tf_op | source)
XLA Modules:
  0.0 1411.4 jit_solution(17801878651438335180)
XLA Ops:
  36.4 15.7 %all-gather.3 = s32[8,2,640]{2,1,0:T(2,128)S(1)} all-gather(s32[1,2,640]{2,1,0:T(2,128)S(1)} %add_bitcast_fusion), channel_id=1, replica_groups=mesh['dp'=4,'fsdp'=8] {'fsdp'}, dimensions={0}, use_global_device_ids=true | all-gather | bytes 46080 | tf_op jit(solution)/shard_map/all_gather | solution.py:644
  53.5 81.3 %spread_tables.2 = bf16[4,2,480,768]{3,2,1,0:T(8,128)(2,1)} custom-call(bf16[2,480,768]{2,1,0:T(8,128)(2,1)} %bitcast.363), custom_call_target="tpu_custom_call" | custom-call | tf_op jit(solution)/shard_map/spread_tables/pallas_call | solution.py:121
  135.5 40.5 %gather_fusion = bf16[8192,768]{1,0:T(8,128)(2,1)} fusion(bf16[3840,768]{1,0:T(8,128)(2,1)} %bitcast.335, s32[8192]{0:T(1024)S(1)} %broadcast_clamp_fusion), kind=kCustom, calls=%fused_computation | custom fusion | bytes 25198592 | tf_op jit(solution)/shard_map/gather | solution.py:659
  178.7 52.1 %spread_tables.3 = bf16[4,2,480,768]{3,2,1,0:T(8,128)(2,1)} custom-call(bf16[2,480,768]{2,1,0:T(8,128)(2,1)} %bitcast.364), custom_call_target="tpu_custom_call" | custom-call | tf_op jit(solution)/shard_map/spread_tables/pallas_call | solution.py:121
  230.8 40.6 %gather_fusion.1 = bf16[8192,768]{1,0:T(8,128)(2,1)} fusion(bf16[3840,768]{1,0:T(8,128)(2,1)} %bitcast.340, s32[8192]{0:T(1024)S(1)} %broadcast_clamp_fusion), kind=kCustom, calls=%fused_computation.1 | custom fusion | bytes 25198592 | tf_op jit(solution)/shard_map/gather | solution.py:662
  277.5 112.4 %all-gather.13.cloned.1.call-done = bf16[10240,768]{1,0:T(8,128)(2,1)} async-done(((bf16[320,768]{1,0:T(8,128)(2,1)}), bf16[10240,768]{1,0:T(8,128)(2,1)}) %all-gather.13.cloned.1.call-update) | async-done | bytes 15728656 | tf_op jit(solution)/shard_map/all_gather | solution.py:667
  429.1 65.4 %reduce-scatter.9.cloned.1.call-done = bf16[2,512,768]{2,1,0:T(8,128)(2,1)} async-done(((bf16[16,512,768]{2,1,0:T(8,128)(2,1)}), bf16[2,512,768]{2,1,0:T(8,128)(2,1)}) %reduce-scatter.9.cloned.1.call-update) | async-done | bytes 1572880 | tf_op jit(solution)/shard_map/reduce_scatter | solution.py:661
  513.9 16.4 %fusion.187 = (f32[2,12,512]{2,1,0:T(8,128)}, f32[2,12,512,512]{2,3,1,0:T(8,128)}) fusion(pred[2,512]{1,0:T(4,128)(4,1)S(1)} %iota_compare_fusion.7, bf16[2,512,3,12,64]{1,4,3,2,0:T(8,128)(2,1)} %bitcast.376), kind=kOutput, calls=%fused_computation.431 | convolution fusion | flops 830472704 | bytes 28361728 | tf_op jit(solution)/shard_map/sub | solution.py:371
  589.4 12.9 fusion.23
  631.7 13.5 multiply_convert_fusion.3
  663.8 33.2 %all-gather.9.cloned.1.call-done = bf16[2,1024,768]{2,1,0:T(8,128)(2,1)} async-done(((bf16[2,128,768]{2,1,0:T(8,128)(2,1)}), bf16[2,1024,768]{2,1,0:T(8,128)(2,1)}) %all-gather.9.cloned.1.call-update) | async-done | bytes 3145744 | tf_op jit(solution)/shard_map/all_gather | solution.py:484
  709.8 15.8 %select_reduce_fusion.1 = (f32[1024]{0:T(1024)S(1)}, f32[1024]{0:T(1024)S(1)}, f32[1024,3840]{1,0:T(8,128)}) fusion(pred[3840]{0:T(1024)(128)(4,1)S(1)} %fusion.128, f32[1024,3840]{1,0:T(8,128)} %fusion.89, bf16[3840,768]{1,0:T(8,128)(2,1)} %bitcast.341, bf16[2,1024,768]{2,1,0:T(8,128)(2,1)S(1)} %copy-done.123), kind=kOutput, calls=%fused_computation.29 | convolution fusion | flops 6055524352 | bytes 38940672 | tf_op jit(solution)/shard_map/pd,vd->pv/dot_general | solution.py:275
  725.6 18.9 %multiply_reduce_fusion.1 = (f32[1024]{0:T(1024)S(1)}, f32[1024]{0:T(1024)S(1)}, f32[1024]{0:T(1024)S(1)}, f32[1024]{0:T(1024)S(1)}, f32[1024]{0:T(1024)S(1)}) fusion(f32[1024,3840]{1,0:T(8,128)} %get-tuple-element.340, f32[1024,3840]{1,0:T(8,128)} %fusion.89, f32[1024]{0:T(1024)S(1)} %get-tuple-element.239, pred[3840]{0:T(1024)(128)(4,1)S(1)} %fusion.128, ...), kind=kLoop, calls=%fused_computation.22 | loop fusion | flops 70773760 | bytes 31494912 | tf_op jit(solution)/shard_map/reduce_sum | solution.py:504
  744.6 14.2 %all-gather.2 = f32[64,1024]{1,0:T(8,128)S(1)} all-gather(f32[8,1024]{1,0:T(8,128)S(1)} %stack.59), channel_id=4, replica_groups=mesh['dp'=4,'fsdp'=8] {'fsdp'}, dimensions={0}, use_global_device_ids=true | all-gather | bytes 294912 | tf_op jit(solution)/shard_map/all_gather | solution.py:509
  759.7 18.6 %multiply_convert_fusion.1 = bf16[1024,3840]{1,0:T(8,128)(2,1)S(1)} fusion(f32[1024,3840]{1,0:T(8,128)} %get-tuple-element.340, f32[1024,3840]{1,0:T(8,128)} %fusion.89, f32[1024]{0:T(1024)S(1)} %get-tuple-element.315, f32[1024]{0:T(1024)S(1)} %get-tuple-element.275, f32[1024]{0:T(1024)S(1)} %get-tuple-element.274, s32[1024]{0:T(1024)S(1)} %fusion.145, ...), kind=kLoop, calls=%fused_computation.19 | loop fusion | flops 62914560 | bytes 39346944 | tf_op jit(solution)/shard_map/convert_element_type | solution.py:532
  793.1 28.7 %reduce-scatter.11.cloned.1.call-done = bf16[128,768]{1,0:T(8,128)(2,1)} async-done(((bf16[1024,768]{1,0:T(8,128)(2,1)}), bf16[128,768]{1,0:T(8,128)(2,1)}) %reduce-scatter.11.cloned.1.call-update) | async-done | bytes 196624 | tf_op jit(solution)/shard_map/reduce_scatter | solution.py:533
  827.4 14.2 %fusion.194 = (bf16[3072]{0:T(1024)(128)(2,1)S(1)}, bf16[2,512,3072]{2,1,0:T(8,128)(2,1)}) fusion(f32[2,512,3072]{2,1,0:T(8,128)} %get-tuple-element.337, f32[3072]{0:T(1024)S(1)} %add.513, bf16[2,512,768]{2,1,0:T(8,128)(2,1)S(1)} %get-tuple-element.265, bf16[3072,768,1]{1,0,2:T(8,128)(2,1)} %bitcast.368), kind=kOutput, calls=%fused_computation.436 | convolution fusion | flops 4869583872 | bytes 25184256 | tf_op jit(solution)/shard_map/bsd,fd->bsf/dot_general | solution.py:275
  873.0 18.1 %multiply_reduce_fusion = (f32[2,12,512]{2,1,0:T(8,128)S(1)}, f32[2,12,512,512]{2,3,1,0:T(8,128)}) fusion(f32[2,12,512]{2,1,0:T(8,128)S(1)} %log_add_fusion, f32[2,12,512,512]{2,3,1,0:T(8,128)} %get-tuple-element.333, pred[2,512]{1,0:T(4,128)(4,1)S(1)} %iota_compare_fusion.7, bf16[2,512,12,64]{1,3,2,0:T(8,128)(2,1)S(1)} %bitcast.362, ...), kind=kOutput, calls=%fused_computation.7 | convolution fusion | flops 836751360 | bytes 53576704 | tf_op jit(solution)/shard_map/bqhd,bkhd->bhqk/dot_general | solution.py:275
  891.1 21.8 %multiply_convert_fusion = bf16[2,12,512,512]{2,3,1,0:T(8,128)(2,1)} fusion(f32[2,12,512,512]{2,3,1,0:T(8,128)} %get-tuple-element.344, f32[2,12,512]{2,1,0:T(8,128)S(1)} %get-tuple-element.343, f32[2,12,512]{2,1,0:T(8,128)S(1)} %log_add_fusion, f32[2,12,512,512]{2,3,1,0:T(8,128)} %get-tuple-element.333, pred[2,512]{1,0:T(4,128)(4,1)S(1)} %iota_compare_fusion.7), kind=kLoop, calls=%fused_computation.6 | loop fusion | flops 37748736 | bytes 63013888 | tf_op jit(solution)/shard_map/convert_element_type | solution.py:439
  1005.1 13.3 fusion.88
  1018.4 211.6 %reduce-scatter.13.cloned.1.call-done = bf16[24,9856]{1,0:T(8,128)(2,1)} async-done(((bf16[768,9856]{1,0:T(8,128)(2,1)}), bf16[24,9856]{1,0:T(8,128)(2,1)}) %reduce-scatter.13.cloned.1.call-update) | async-done | bytes 473104
  1235.9 64.0 %scatter_custom_fusion = f32[3840,768]{1,0:T(8,128)} fusion(f32[3840,768]{1,0:T(8,128)} %fusion.88, s32[8192]{0:T(1024)S(1)} %bitcast.409, bf16[8192,768]{1,0:T(8,128)(2,1)} %bitcast.360), kind=kCustom, calls=%fused_computation.4 | custom fusion | flops 12582912 | bytes 24379392 | tf_op jit(solution)/shard_map/scatter-add | solution.py:722
  1307.3 53.9 %fold_table.1 = f32[2,1,480,768]{3,2,1,0:T(8,128)} custom-call(bf16[4,2,1,480,768]{4,3,2,1,0:T(8,128)(2,1)} %bitcast.353), custom_call_target="tpu_custom_call" | custom-call | tf_op jit(solution)/shard_map/fold_table/pallas_call | solution.py:221
  1369.7 15.3 %total.1 = f32[8,128]{1,0:T(8,128)} custom-call(f32[8,128]{1,0:T(8,128)} %broadcast_in_dim.245.x), custom_call_target="tpu_custom_call" | custom-call | tf_op jit(solution)/shard_map/total/pallas_call | solution.py:259
  (500 shorter events, 392.8 us)
Async XLA Ops:
  8.0 24.2 %copy-start.62 = (f32[512,24]{0,1:T(8,128)S(1)}, f32[512,24]{0,1:T(8,128)}, u32[]{:S(2)}) copy-start(f32[512,24]{0,1:T(8,128)} %param.44) | copy-start | bytes 147460
  8.0 25.9 %copy-start.40 = (f32[96,768]{1,0:T(8,128)S(1)}, f32[96,768]{1,0:T(8,128)}, u32[]{:S(2)}) copy-start(f32[96,768]{1,0:T(8,128)} %param.42) | copy-start | bytes 884740
  8.0 44.1 %copy-start.16 = (f32[956,768]{1,0:T(8,128)S(1)}, f32[956,768]{1,0:T(8,128)}, u32[]{:S(2)}) copy-start(f32[956,768]{1,0:T(8,128)} %param.38) | copy-start | bytes 8810500
  8.1 264.7 %all-gather.15.cloned.1.call-start = ((), (), s32[]{:S(2)}) async-start(), calls=%async_computation.10 | async-start | bytes 16220160 | tf_op jit(solution)/shard_map/all_gather | solution.py:668
  24.9 365.0 %all-gather.13.cloned.1.call-start = ((), (), s32[]{:S(2)}) async-start(), calls=%async_computation.9 | async-start | bytes 16220160 | tf_op jit(solution)/shard_map/all_gather | solution.py:667
  34.8 391.6 %reduce-scatter.7.cloned.1.call-start = ((), (), s32[]{:S(2)}) async-start(), calls=%async_computation.4 | async-start | bytes 14155776 | tf_op jit(solution)/shard_map/reduce_scatter | solution.py:658
  52.2 82.7 %copy-start.58 = (s32[16,640]{1,0:T(8,128)}, s32[16,640]{1,0:T(8,128)S(1)}, u32[]{:S(2)}) copy-start(s32[16,640]{1,0:T(8,128)S(1)} %reshape.608) | copy-start | bytes 122884
  176.1 318.4 %reduce-scatter.9.cloned.1.call-start = ((), (), s32[]{:S(2)}) async-start(), calls=%async_computation.5 | async-start | bytes 14155776 | tf_op jit(solution)/shard_map/reduce_scatter | solution.py:661
  271.5 425.5 %all-gather.9.cloned.1.call-start = ((), (), s32[]{:S(2)}) async-start(), calls=%async_computation.6 | async-start | bytes 3538944 | tf_op jit(solution)/shard_map/all_gather | solution.py:484
  404.5 220.9 %copy-start.3 = (f32[512,768]{1,0:T(8,128)}, f32[512,768]{1,0:T(8,128)S(1)}, u32[]{:S(2)}) copy-start(f32[512,768]{1,0:T(8,128)S(1)} %copy.342) | copy-start | bytes 4718596
  426.4 199.0 %copy-start.67 = (f32[768]{0:T(1024)}, f32[768]{0:T(1024)S(1)}, u32[]{:S(2)}) copy-start(f32[768]{0:T(1024)S(1)} %get-tuple-element.216) | copy-start | bytes 9220
  426.4 199.0 %copy-start.69 = (f32[768]{0:T(1024)}, f32[768]{0:T(1024)S(1)}, u32[]{:S(2)}) copy-start(f32[768]{0:T(1024)S(1)} %get-tuple-element.217) | copy-start | bytes 9220
  626.6 18.7 %slice-start.4 = ((s8[4718592]{0:T(1024)(128)(4,1)}), s8[4194304]{0:T(1024)(128)(4,1)S(1)}, s32[]{:S(2)}) async-start(s8[4718592]{0:T(1024)(128)(4,1)} %bitcast.369), calls=%async_computation.16 | async-start | bytes 8388608
  628.9 16.3 %copy-start.12 = (f32[2,512,768]{2,1,0:T(8,128)}, f32[2,512,768]{2,1,0:T(8,128)S(1)}, u32[]{:S(2)}) copy-start(f32[2,512,768]{2,1,0:T(8,128)S(1)} %get-tuple-element.335) | copy-start | bytes 9437188
  660.6 161.2 %reduce-scatter.11.cloned.1.call-start = ((), (), s32[]{:S(2)}) async-start(), calls=%async_computation.7 | async-start | bytes 1769472 | tf_op jit(solution)/shard_map/reduce_scatter | solution.py:533
  725.6 55.9 %slice-start = ((s8[5898240]{0:T(1024)(128)(4,1)}), s8[1703936]{0:T(1024)(128)(4,1)S(1)}, s32[]{:S(2)}) async-start(s8[5898240]{0:T(1024)(128)(4,1)} %bitcast.337), calls=%async_computation.12 | async-start | bytes 3407872
  759.7 21.8 %slice-start.1 = ((s8[5898240]{0:T(1024)(128)(4,1)}), s8[4194304]{0:T(1024)(128)(4,1)S(1)}, s32[]{:S(2)}) async-start(s8[5898240]{0:T(1024)(128)(4,1)} %bitcast.337), calls=%async_computation.13 | async-start | bytes 8388608
  788.8 441.1 %reduce-scatter.13.cloned.1.call-start = ((), (), s32[]{:S(2)}) async-start(), calls=%async_computation.11 | async-start | bytes 15611904
  827.4 14.2 %copy-start.13 = (f32[2,512,768]{2,1,0:T(8,128)S(1)}, f32[2,512,768]{2,1,0:T(8,128)}, u32[]{:S(2)}) copy-start(f32[2,512,768]{2,1,0:T(8,128)} %copy-done.12) | copy-start | bytes 9437188
  873.0 39.9 %slice-start.2 = ((s8[4718592]{0:T(1024)(128)(4,1)}), s8[524288]{0:T(1024)(128)(4,1)S(1)}, s32[]{:S(2)}) async-start(s8[4718592]{0:T(1024)(128)(4,1)} %bitcast.347), calls=%async_computation.14 | async-start | bytes 1048576
  891.1 21.8 %slice-start.3 = ((s8[4718592]{0:T(1024)(128)(4,1)}), s8[4194304]{0:T(1024)(128)(4,1)S(1)}, s32[]{:S(2)}) async-start(s8[4718592]{0:T(1024)(128)(4,1)} %bitcast.347), calls=%async_computation.15 | async-start | bytes 8388608
  942.4 14.4 %copy-start.23 = (bf16[2,512,3,12,64]{1,4,3,2,0:T(8,128)(2,1)}, bf16[2,512,3,12,64]{1,4,3,2,0:T(8,128)(2,1)S(1)}, u32[]{:S(2)}) copy-start(bf16[2,512,3,12,64]{1,4,3,2,0:T(8,128)(2,1)S(1)} %copy.368) | copy-start | bytes 14155780
  1001.4 234.5 %all-gather.11.cloned.1.call-start = ((), (), s32[]{:S(2)}) async-start(), calls=%async_computation.8 | async-start | bytes 14155776 | tf_op jit(solution)/shard_map/all_gather | solution.py:719
  1361.2 28.6 %copy-start.2 = (f32[2,1,480,768]{3,2,1,0:T(8,128)S(1)}, f32[2,1,480,768]{3,2,1,0:T(8,128)}, u32[]{:S(2)}) copy-start(f32[2,1,480,768]{3,2,1,0:T(8,128)} %fold_table.1) | copy-start | bytes 8847364
  (117 other events, 637.7 us)
Sparse Core Ops, SparseCore 0:
  25.0 140.9 all-gather.14
  169.6 220.3 all-gather.12
  1001.5 228.4 reduce-scatter.12
Sparse Core Ops, SparseCore 1:
  176.1 172.0 reduce-scatter.6
  350.4 144.1 reduce-scatter.8
  660.7 36.3 all-gather.8
  788.9 32.8 reduce-scatter.10
  1004.4 128.4 all-gather.10

commit v3 on v2

--- a/solution.py
+++ b/solution.py
@@ -24,6 +24,7 @@
 BOTH = ("dp", "fsdp")
 LOW = jnp.bfloat16
 MIB = 1 << 20
+CHUNK = 512
 
 
 def push(src, dst, send, recv, where):
@@ -132,6 +133,222 @@
         name="spread_tables",
     )(*cut)
     return [out.reshape(dp * rows, width) for out in outs]
+
+
+def ways_of(me, dp):
+    if dp == 4:
+        return [flipped(me, 1), flipped(me, 2)]
+    return [lax.rem(me + hop, dp) for hop in range(1, dp)]
+
+
+def sources_of(me, dp):
+    if dp == 4:
+        return [flipped(me, 1), flipped(me, 2)]
+    return [lax.rem(me + dp - hop, dp) for hop in range(1, dp)]
+
+
+def gather_body(dp, n, count, *refs):
+    blocks, outs = refs[:count], refs[count : 2 * count]
+    local, z_send, z_recv, way_send, way_recv, far_send, far_recv, core_send, core_recv = refs[
+        2 * count :
+    ]
+    me = lax.axis_index("fsdp")
+    row = lax.axis_index("dp")
+    p = lax.div(me, 2)
+    c = lax.rem(me, 2)
+    partner = me + 1 - 2 * c
+    ways = ways_of(row, dp)
+    sources = sources_of(row, dp)
+    barrier = pltpu.get_barrier_semaphore()
+
+    def hello(where):
+        pl.semaphore_signal(barrier, inc=1, device_id=where, device_id_type=pl.DeviceIdType.MESH)
+
+    hello({"fsdp": partner})
+    for way in ways:
+        hello({"dp": way})
+
+    @pl.when(p > 0)
+    def _():
+        hello({"fsdp": me - 2})
+
+    @pl.when(p < n - 1)
+    def _():
+        hello({"fsdp": me + 2})
+
+    @pl.when((p > 0) & (p < n - 1))
+    def _():
+        pl.semaphore_wait(barrier, 3 + len(ways))
+
+    @pl.when((p == 0) | (p == n - 1))
+    def _():
+        pl.semaphore_wait(barrier, 2 + len(ways))
+
+    def remote(src, dst, send, recv, where):
+        return pltpu.make_async_remote_copy(
+            src_ref=src,
+            dst_ref=dst,
+            send_sem=send,
+            recv_sem=recv,
+            device_id=where,
+            device_id_type=pl.DeviceIdType.MESH,
+        )
+
+    def line(m, q, side):
+        shard = outs[m].at[row, 2 * q + c]
+        where = {"fsdp": me + 2 - 4 * side}
+        return remote(shard, shard, z_send.at[m, side, q], z_recv.at[m, q], where)
+
+    def way_copy(m, w, half, q):
+        shard = outs[m].at[row, 2 * q + c, half]
+        return remote(
+            shard, shard, way_send.at[m, w, half, q], way_recv.at[m, w, half, q], {"dp": ways[w]}
+        )
+
+    def far_copy(m, w, q):
+        shard = outs[m].at[sources[w], 2 * q + c, w]
+        return remote(
+            shard, shard, far_send.at[m, w, q], far_recv.at[m, w, q], {"dp": ways[1 - w]}
+        )
+
+    def core_copy(m, j, q, half):
+        shard = outs[m].at[j, 2 * q + c, half]
+        return remote(
+            shard,
+            shard,
+            core_send.at[m, j, q, half],
+            core_recv.at[m, j, q, half],
+            {"fsdp": partner},
+        )
+
+    def onward(m, q):
+        for half in range(2):
+            for w in range(len(ways)):
+                way_copy(m, w, half if w == 0 else 1 - half, q).start()
+        for half in range(2):
+            core_copy(m, row, q, half).start()
+
+    def landed(m, q):
+        for half in range(2):
+            for w in range(len(ways)):
+                part = half if w == 0 else 1 - half
+                way_copy(m, w, part, q).wait_recv()
+                if dp == 4 and part == w:
+                    far_copy(m, w, q).start()
+                core_copy(m, sources[w], q, part).start()
+
+    def far_landed(m, q):
+        if dp == 4:
+            for w in range(2):
+                far_copy(m, w, q).wait_recv()
+                core_copy(m, dp - 1 - row, q, w).start()
+
+    def each(distance, act):
+        if distance == 0:
+            act(p)
+            return
+
+        @pl.when(p >= distance)
+        def _():
+            act(p - distance)
+
+        @pl.when(p + distance < n)
+        def _():
+            act(p + distance)
+
+    for m in range(count):
+        copy = pltpu.make_async_copy(blocks[m], outs[m].at[row, me], local.at[m])
+        copy.start()
+        copy.wait()
+
+        @pl.when(p < n - 1)
+        def _():
+            line(m, p, 0).start()
+
+        @pl.when(p > 0)
+        def _():
+            line(m, p, 1).start()
+
+        onward(m, p)
+    for distance in range(1, n + 2):
+        for m in range(count):
+            if distance < n:
+
+                @pl.when(p >= distance)
+                def _():
+                    line(m, p - distance, 0).wait_recv()
+
+                    @pl.when(p < n - 1)
+                    def _():
+                        line(m, p - distance, 0).start()
+
+                    onward(m, p - distance)
+
+                @pl.when(p + distance < n)
+                def _():
+                    line(m, p + distance, 1).wait_recv()
+
+                    @pl.when(p > 0)
+                    def _():
+                        line(m, p + distance, 1).start()
+
+                    onward(m, p + distance)
+
+            if distance <= n:
+                each(distance - 1, functools.partial(landed, m))
+            if distance >= 2:
+                each(distance - 2, functools.partial(far_landed, m))
+
+    def settle(q, carry):
+        for m in range(count):
+
+            @pl.when((q <= p) & (p < n - 1))
+            def _():
+                line(m, q, 0).wait_send()
+
+            @pl.when((q >= p) & (p > 0))
+            def _():
+                line(m, q, 1).wait_send()
+
+            for half in range(2):
+                for w in range(len(ways)):
+                    way_copy(m, w, half, q).wait_send()
+                if dp == 4:
+                    far_copy(m, half, q).wait_send()
+                for j in range(dp):
+                    core_copy(m, j, q, half).wait()
+        return carry
+
+    lax.fori_loop(0, n, settle, 0)
+
+
+def gather_weights(blocks, dp, groups, identity):
+    count = len(blocks)
+    rows, width = blocks[0].shape
+    n = groups // 2
+    cut = [block.reshape(2, rows // 2, width) for block in blocks]
+    ways = 2 if dp == 4 else dp - 1
+    dma = pltpu.SemaphoreType.DMA
+    outs = pl.pallas_call(
+        functools.partial(gather_body, dp, n, count),
+        out_shape=[jax.ShapeDtypeStruct((dp, groups, 2, rows // 2, width), LOW)] * count,
+        in_specs=[pl.BlockSpec(memory_space=pl.ANY)] * count,
+        out_specs=[pl.BlockSpec(memory_space=pl.ANY)] * count,
+        scratch_shapes=[
+            dma((count,)),
+            dma((count, 2, n)),
+            dma((count, n)),
+            dma((count, ways, 2, n)),
+            dma((count, ways, 2, n)),
+            dma((count, 2, n)),
+            dma((count, 2, n)),
+            dma((count, dp, n, 2)),
+            dma((count, dp, n, 2)),
+        ],
+        compiler_params=pltpu.CompilerParams(collective_id=identity, has_side_effects=True),
+        name="gather_weights",
+    )(*cut)
+    return [out.reshape(dp * groups, rows, width) for out in outs]
 
 
 def fold_body(dp, pieces, g, out, near_buffer, far_buffer, last_buffer, sems):
@@ -271,6 +488,122 @@
     )(x)
 
 
+def dot_over(left, right, left_dim, right_dim):
+    return lax.dot_general(
+        left, right, (((left_dim,), (right_dim,)), ((), ())), preferred_element_type=jnp.float32
+    )
+
+
+def attend_body(lengths, q_ref, k_ref, v_ref, out_ref):
+    live = jnp.maximum(lengths[pl.program_id(0)], 1)
+    span = q_ref.shape[1]
+    k, v = k_ref[0], v_ref[0]
+    keep = lax.broadcasted_iota(jnp.int32, (span, CHUNK), 0) < live
+    low_lane = lax.broadcasted_iota(jnp.int32, (CHUNK, 2 * HD), 1) < HD
+    for first in range(0, span, CHUNK):
+        q = q_ref[0, first : first + CHUNK, :]
+        parts = []
+        for head in range(2):
+            mine = low_lane if head == 0 else jnp.logical_not(low_lane)
+            scores = dot_over(k, jnp.where(mine, q, jnp.zeros_like(q)), 1, 1)
+            scores = jnp.where(keep, scores * 0.125, NEGATIVE)
+            exponent = jnp.exp(scores - jnp.max(scores, axis=0, keepdims=True))
+            scale = 1.0 / jnp.sum(exponent, axis=0, keepdims=True)
+            parts.append(dot_over((exponent * scale).astype(LOW), v, 0, 0))
+        out_ref[0, first : first + CHUNK, :] = jnp.where(low_lane, parts[0], parts[1]).astype(LOW)
+
+
+def attend(joined, lengths):
+    micro, span, wide = joined.shape
+    width = wide // 3
+    pairs = width // (2 * HD)
+
+    def place(third):
+        return pl.BlockSpec((1, span, 2 * HD), lambda b, h, _: (b, 0, third * pairs + h))
+
+    return pl.pallas_call(
+        attend_body,
+        grid_spec=pltpu.PrefetchScalarGridSpec(
+            num_scalar_prefetch=1,
+            grid=(micro, pairs),
+            in_specs=[place(0), place(1), place(2)],
+            out_specs=pl.BlockSpec((1, span, 2 * HD), lambda b, h, _: (b, 0, h)),
+        ),
+        out_shape=jax.ShapeDtypeStruct((micro, span, width), LOW),
+        cost_estimate=pl.CostEstimate(
+            flops=4 * micro * span * span * width,
+            bytes_accessed=8 * micro * span * width,
+            transcendentals=micro * span * span * width // HD,
+        ),
+        name="attend",
+    )(lengths, joined, joined, joined)
+
+
+def attend_back_body(lengths, q_ref, k_ref, v_ref, d_ref, out_ref, g_keys, g_values):
+    live = jnp.maximum(lengths[pl.program_id(0)], 1)
+    span = q_ref.shape[1]
+    k, v = k_ref[0], v_ref[0]
+    keep = lax.broadcasted_iota(jnp.int32, (span, CHUNK), 0) < live
+    low_lane = lax.broadcasted_iota(jnp.int32, (CHUNK, 2 * HD), 1) < HD
+    low_wide = lax.broadcasted_iota(jnp.int32, (span, 2 * HD), 1) < HD
+    for first in range(0, span, CHUNK):
+        q = q_ref[0, first : first + CHUNK, :]
+        d = d_ref[0, first : first + CHUNK, :]
+        parts = []
+        for head in range(2):
+            mine = low_lane if head == 0 else jnp.logical_not(low_lane)
+            scores = dot_over(k, jnp.where(mine, q, jnp.zeros_like(q)), 1, 1)
+            scores = jnp.where(keep, scores * 0.125, NEGATIVE)
+            exponent = jnp.exp(scores - jnp.max(scores, axis=0, keepdims=True))
+            probs = exponent * (1.0 / jnp.sum(exponent, axis=0, keepdims=True))
+            d_probs = dot_over(v, jnp.where(mine, d, jnp.zeros_like(d)), 1, 1)
+            inner = jnp.sum(probs * d_probs, axis=0, keepdims=True)
+            d_scores = (probs * (d_probs - inner)).astype(LOW)
+            value_part = dot_over(probs.astype(LOW), d, 1, 0)
+            key_part = dot_over(d_scores, q, 1, 0)
+            if first == 0:
+                g_values[head] = value_part
+                g_keys[head] = key_part
+            else:
+                g_values[head] += value_part
+                g_keys[head] += key_part
+            parts.append(dot_over(d_scores, k, 0, 0))
+        out_ref[0, 0, first : first + CHUNK, :] = (
+            jnp.where(low_lane, parts[0], parts[1]) * 0.125
+        ).astype(LOW)
+    out_ref[1, 0] = (jnp.where(low_wide, g_keys[0], g_keys[1]) * 0.125).astype(LOW)
+    out_ref[2, 0] = jnp.where(low_wide, g_values[0], g_values[1]).astype(LOW)
+
+
+def attend_back(joined, d_context, lengths):
+    micro, span, width = d_context.shape
+    pairs = width // (2 * HD)
+
+    def place(third):
+        return pl.BlockSpec((1, span, 2 * HD), lambda b, h, _: (b, 0, third * pairs + h))
+
+    return pl.pallas_call(
+        attend_back_body,
+        grid_spec=pltpu.PrefetchScalarGridSpec(
+            num_scalar_prefetch=1,
+            grid=(micro, pairs),
+            in_specs=[place(0), place(1), place(2), place(0)],
+            out_specs=pl.BlockSpec((3, 1, span, 2 * HD), lambda b, h, _: (0, b, 0, h)),
+            scratch_shapes=[
+                pltpu.VMEM((2, span, 2 * HD), jnp.float32),
+                pltpu.VMEM((2, span, 2 * HD), jnp.float32),
+            ],
+        ),
+        out_shape=jax.ShapeDtypeStruct((3, micro, span, width), LOW),
+        cost_estimate=pl.CostEstimate(
+            flops=10 * micro * span * span * width,
+            bytes_accessed=14 * micro * span * width,
+            transcendentals=micro * span * span * width // HD,
+        ),
+        name="attend_back",
+    )(lengths, joined, joined, joined, d_context)
+
+
 def product_of(form, left, right):
     return jnp.einsum(form, left, right, preferred_element_type=jnp.float32)
 
@@ -312,12 +645,6 @@
 def label_valid(lengths, labels, span):
     needed = (lengths * labels + span - 1) // span
     return (jnp.arange(labels)[None, :] < needed[:, None]).astype(jnp.float32)
-
-
-def masked_scores(queries, keys, lengths):
-    raw = product_of("bqhd,bkhd->bhqk", queries, keys)
-    keep = jnp.arange(keys.shape[1])[None, :] < jnp.maximum(lengths, 1)[:, None]
-    return jnp.where(keep[:, None, None, :], raw * 0.125, NEGATIVE)
 
 
 def pack_layer(weights, extra):
@@ -361,20 +688,10 @@
 def layer_forward(value, weights, lengths):
     w_qkv, w_out, w_up, w_down, small = weights[:5]
     micro, span, width = value.shape
-    heads = width // HD
     value_low = value.astype(LOW)
     bias = jnp.concatenate([small[0], jnp.zeros_like(small[0]), small[1]])
     joined = (product_of("bsd,df->bsf", value_low, w_qkv) + bias).astype(LOW)
-    split = joined.reshape(micro, span, 3, heads, HD)
-    scores = masked_scores(split[:, :, 0], split[:, :, 1], lengths)
-    top = jnp.max(scores, axis=-1, keepdims=True)
-    exponent = jnp.exp(scores - top)
-    total = jnp.sum(exponent, axis=-1, keepdims=True)
-    probs = (exponent / total).astype(LOW)
-    logsum = top + jnp.log(total)
-    context = (
-        product_of("bhqk,bkhd->bqhd", probs, split[:, :, 2]).reshape(micro, span, width).astype(LOW)
-    )
+    context = attend(joined, lengths)
     attn = product_of("bsc,cd->bsd", context, w_out) + small[2]
     first, normed_first, inverse_first = layer_norm_keep(value + attn, small[8], small[9])
     first_low = first.astype(LOW)
@@ -388,7 +705,6 @@
         (
             value_low,
             joined,
-            logsum,
             context,
             normed_first,
             inverse_first,
@@ -401,12 +717,11 @@
     )
 
 
-def layer_backward(grad, weights, kept, lengths):
+def layer_backward(grad, weights, kept, lengths, devices):
     w_qkv, w_out, w_up, w_down, small = weights[:5]
     (
         value_low,
         joined,
-        logsum,
         context,
         normed_first,
         inverse_first,
@@ -417,7 +732,6 @@
         inverse_second,
     ) = kept
     micro, span, width = value_low.shape
-    heads = width // HD
     d_second, gain_second, shift_second = layer_norm_back(
         grad, normed_second, inverse_second, small[10]
     )
@@ -426,25 +740,13 @@
     d_up = (product_of("bsd,fd->bsf", d_down, w_down) * slope).astype(LOW)
     g_up = product_of("bsd,bsf->df", first_low, d_up)
     d_first = d_second + product_of("bsf,df->bsd", d_up, w_up)
+    wide = pack_wide(g_up, g_down, devices)
+    d_first, wide = lax.optimization_barrier((d_first, wide))
+    wide = lax.psum_scatter(wide, BOTH, scatter_dimension=0, tiled=True)
     d_sum, gain_first, shift_first = layer_norm_back(d_first, normed_first, inverse_first, small[8])
     d_attn = d_sum.astype(LOW)
-    g_out = product_of("bsc,bsd->cd", context, d_attn)
-    d_context = (
-        product_of("bsd,cd->bsc", d_attn, w_out).astype(LOW).reshape(micro, span, heads, HD)
-    )
-    split = joined.reshape(micro, span, 3, heads, HD)
-    probs = jnp.exp(masked_scores(split[:, :, 0], split[:, :, 1], lengths) - logsum)
-    g_values = product_of("bhqk,bqhd->bkhd", probs.astype(LOW), d_context)
-    d_probs = product_of("bqhd,bkhd->bhqk", d_context, split[:, :, 2])
-    d_scores = (probs * (d_probs - jnp.sum(probs * d_probs, axis=-1, keepdims=True))).astype(LOW)
-    g_queries = product_of("bhqk,bkhd->bqhd", d_scores, split[:, :, 1]) * 0.125
-    g_keys = product_of("bhqk,bqhd->bkhd", d_scores, split[:, :, 0]) * 0.125
-    d_joined = (
-        jnp.stack([g_queries, g_keys, g_values], axis=2)
-        .reshape(micro, span, 3 * width)
-        .astype(LOW)
-    )
-    g_qkv = product_of("bsd,bsf->df", value_low, d_joined)
+    d_context = product_of("bsd,cd->bsc", d_attn, w_out).astype(LOW)
+    d_joined = jnp.concatenate(list(attend_back(joined, d_context, lengths)), axis=-1)
     d_value = d_sum + product_of("bsf,df->bsd", d_joined, w_qkv)
 
     def column_sum(value):
@@ -464,26 +766,23 @@
             shift_second[None],
         ]
     )
-    return ((g_qkv, g_out, g_up, g_down), rows_grad, d_value)
+    return wide, (value_low, d_joined, context, d_attn), rows_grad, d_value
+
+
+def label_rows(pick, out):
+    micro, labels, _ = pick.shape
+    rows = product_of("bps,bsd->bpd", pick, out.astype(LOW)).astype(LOW)
+    return rows.reshape(micro * labels, out.shape[-1])
 
 
 def label_head(
-    student_out, teacher_out, places, tables, targets, valid_mask, own, share, padded, groups, count
+    all_student, all_teacher, pick, tables, targets, valid_mask, own, share, padded, groups, count
 ):
     table_student, table_teacher = tables
     vocab_rows = table_student.shape[0]
-    micro, span, width = student_out.shape
-    mine = places.size
-    pick = (places[..., None] == jnp.arange(span)).astype(LOW)
-    rows = jnp.stack(
-        [
-            product_of("bps,bsd->bpd", pick, out.astype(LOW)).astype(LOW).reshape(mine, width)
-            for out in (student_out, teacher_out)
-        ]
-    )
-    rows_all = lax.all_gather(rows, "fsdp", axis=1, tiled=True)
-    all_student = rows_all[0]
-    all_teacher = rows_all[1]
+    micro, labels, span = pick.shape
+    width = all_student.shape[1]
+    mine = micro * labels
     row_index = jnp.arange(vocab_rows)
     real = (row_index % padded < share)[None, :]
     inside, local_target = owned(targets, share, padded, groups, own)
@@ -537,6 +836,7 @@
         tiled=True,
     )
     table_term = product_of("pv,pd->vd", d_logits, all_student)
+    d_rows, table_term = lax.optimization_barrier((d_rows, table_term))
     terms = share_lab * (
         (1.0 - SOFT_FRACTION) * cross_entropy
         + SOFT_FRACTION * SOFTMAX_HEAT * SOFTMAX_HEAT * divergence_loss
@@ -546,23 +846,24 @@
     return (d_out, table_term, jnp.sum(local))
 
 
-def pack_grads(matrices, small_grad, position_grad, devices):
-    g_qkv, g_out, g_up, g_down = (g.astype(LOW) for g in matrices)
-    width = g_qkv.shape[0]
+def pack_wide(g_up, g_down, devices):
+    width = g_up.shape[0]
     ff = g_down.shape[0]
-    parts = ff // width
     g_down = (
-        g_down.reshape(devices, parts, width // devices, width)
+        g_down.astype(LOW)
+        .reshape(devices, ff // width, width // devices, width)
         .transpose(0, 2, 1, 3)
         .reshape(width, ff)
     )
+    return jnp.concatenate([g_up.astype(LOW), g_down], axis=1)
+
+
+def pack_narrow(g_qkv, g_out, small_grad, position_grad):
     pad = -small_grad.shape[0] % 128
     return jnp.concatenate(
         [
-            g_qkv,
-            g_out,
-            g_up,
-            g_down,
+            g_qkv.astype(LOW),
+            g_out.astype(LOW),
             position_grad.astype(LOW).T,
             jnp.pad(small_grad, ((0, pad), (0, 0))).astype(LOW).T,
         ],
@@ -570,19 +871,19 @@
     )
 
 
-def unpack_grads(packed, width, span, slots):
+def unpack_grads(wide, narrow, width, span, slots):
     ff = 4 * width
-    packed = packed.astype(jnp.float32)
-    edges = [3 * width, 4 * width, 4 * width + ff, 4 * width + 2 * ff]
-    down = packed[:, edges[2] : edges[3]]
+    wide = wide.astype(jnp.float32)
+    narrow = narrow.astype(jnp.float32)
+    down = wide[:, ff:]
     g_down = jnp.concatenate([down[:, k * width : (k + 1) * width] for k in range(4)], axis=0)
     return (
-        packed[:, : edges[0]],
-        packed[:, edges[0] : edges[1]],
-        packed[:, edges[1] : edges[2]],
+        narrow[:, : 3 * width],
+        narrow[:, 3 * width : 4 * width],
+        wide[:, :ff],
         g_down,
-        packed[:, edges[3] + span : edges[3] + span + slots].T,
-        packed[:, edges[3] : edges[3] + span].T,
+        narrow[:, 4 * width + span : 4 * width + span + slots].T,
+        narrow[:, 4 * width : 4 * width + span].T,
     )
 
 
@@ -646,40 +947,53 @@
     targets_all = info[:, span : span + labels].reshape(-1)
     lengths_all = info[:, span + labels]
     student_table = spread_dp([jnp.pad(table.astype(LOW), ((0, pad), (0, 0)))], dp, 1)[0]
-    teacher_table = spread_dp([jnp.pad(t_table, ((0, pad), (0, 0)))], dp, 2)[0]
-    tables = (student_table, teacher_table)
-    vocab_rows = student_table.shape[0]
-
     valid_local = label_valid(seq_len, labels, span)
     counts = jnp.stack([jnp.sum(valid_local), jnp.sum((seq_len > 0).astype(jnp.float32))])
     extra = jnp.broadcast_to(counts.astype(LOW)[None, :], (rows_own, 2))
 
     safe_ids = owned(ids_all, share, padded, groups, own)[1]
+    packed_teacher = pack_layer((t_qkv, t_out, t_up, t_down, t_small, t_position), None)
+    packed_teacher = lax.all_gather(packed_teacher, BOTH)
+    safe_flat = safe_ids.reshape(-1)
+    student_hits = student_table[safe_flat].reshape(groups * micro, span, width)
+    student_hits, t_table = lax.optimization_barrier((student_hits, t_table))
+    teacher_table = spread_dp([jnp.pad(t_table, ((0, pad), (0, 0)))], dp, 2)[0]
     tokens_student = lax.psum_scatter(
-        student_table[safe_ids], "fsdp", scatter_dimension=0, tiled=True
+        student_hits,
+        "fsdp",
+        scatter_dimension=0,
+        tiled=True,
     ).astype(jnp.float32)
-    tokens_teacher = lax.psum_scatter(
-        teacher_table[safe_ids], "fsdp", scatter_dimension=0, tiled=True
-    ).astype(jnp.float32)
-
-    packed_student = pack_layer((w_qkv, w_out, w_up, w_down, small, position), extra)
-    packed_teacher = pack_layer((t_qkv, t_out, t_up, t_down, t_small, t_position), None)
-    packed_student = lax.all_gather(packed_student, BOTH)
-    packed_teacher = lax.all_gather(packed_teacher, BOTH)
+    teacher_hits = teacher_table[safe_flat].reshape(groups * micro, span, width)
+    s_weights, teacher_hits, packed_teacher = lax.optimization_barrier(
+        ((w_qkv, w_out, w_up, w_down, small, position), teacher_hits, packed_teacher)
+    )
+    tokens_teacher = lax.psum_scatter(teacher_hits, "fsdp", scatter_dimension=0, tiled=True)
+    packed_student = gather_weights([pack_layer(s_weights, extra)], dp, groups, 5)[0]
     weights, rest = unpack_layer(packed_student, span, slots)
-    teacher, _ = unpack_layer(packed_teacher, span, slots)
     counted = jnp.sum(rest[::rows_own, :2].astype(jnp.float32), axis=0)
     label_count, count_seq = counted[0], counted[1]
 
+    tables = (student_table, teacher_table)
+    vocab_rows = student_table.shape[0]
     start, normed_start, inverse_start = embed_forward(tokens_student, weights, segments)
-    teacher_start = embed_forward(tokens_teacher, teacher, segments)[0]
     student_out, kept = layer_forward(start, weights, seq_len)
+    pick = (label_pos[..., None] == jnp.arange(span)).astype(LOW)
+    student_rows = label_rows(pick, student_out)
+    student_rows, tokens_teacher, packed_teacher = lax.optimization_barrier(
+        (student_rows, tokens_teacher, packed_teacher)
+    )
+    teacher, _ = unpack_layer(packed_teacher, span, slots)
+    student_rows = lax.all_gather(student_rows, "fsdp", axis=0, tiled=True)
+    teacher_start = embed_forward(tokens_teacher.astype(jnp.float32), teacher, segments)[0]
     teacher_out = layer_forward(teacher_start, teacher, seq_len)[0]
+    teacher_rows = label_rows(pick, teacher_out)
+    teacher_rows = lax.all_gather(teacher_rows, "fsdp", axis=0, tiled=True)
     valid_group = label_valid(lengths_all, labels, span).reshape(-1)
     d_out, table_grad, label_loss = label_head(
-        student_out,
-        teacher_out,
-        label_pos,
+        student_rows,
+        teacher_rows,
+        pick,
         tables,
         targets_all,
         valid_group,
@@ -702,7 +1016,7 @@
     d_out = d_out + first_row * d_cls[:, None, :]
     loss_part = label_loss + jnp.sum(weight_pkd * gap * gap)
 
-    matrices, rows_grad, d_start = layer_backward(d_out, weights, kept, seq_len)
+    wide, factors, rows_grad, d_start = layer_backward(d_out, weights, kept, seq_len, devices)
     d_embed, gain_embed, shift_embed = layer_norm_back(
         d_start, normed_start, inverse_start, weights[4][12]
     )
@@ -716,16 +1030,20 @@
             jnp.sum(d_embed * (1.0 - zero_segment), axis=(0, 1))[None],
         ]
     )
-    embed_grads = lax.all_gather(d_embed.astype(LOW), "fsdp", axis=0, tiled=True)
-    packed_grads = pack_grads(matrices, small_grad, jnp.sum(d_embed, axis=0), devices)
-    packed_grads = lax.psum_scatter(packed_grads, BOTH, scatter_dimension=0, tiled=True)
-    table_grad = table_grad + jax.ops.segment_sum(
-        embed_grads.astype(jnp.float32).reshape(-1, width),
-        safe_ids.reshape(-1),
-        num_segments=vocab_rows,
-    )
-    table_shard = fold_dp(table_grad.astype(LOW), dp, 1, 3)[:share]
-    grads = (table_shard,) + unpack_grads(packed_grads, width, span, slots)
+    position_grad = jnp.sum(d_embed, axis=0)
+    d_embed_low, factors = lax.optimization_barrier((d_embed.astype(LOW), factors))
+    embed_grads = lax.all_gather(d_embed_low, "fsdp", axis=0, tiled=True)
+    value_low, d_joined, context, d_attn = factors
+    g_qkv = product_of("bsd,bsf->df", value_low, d_joined)
+    g_out = product_of("bsc,bsd->cd", context, d_attn)
+    narrow = pack_narrow(g_qkv, g_out, small_grad, position_grad)
+    narrow, wide = lax.optimization_barrier((narrow, wide))
+    narrow = lax.psum_scatter(narrow, BOTH, scatter_dimension=0, tiled=True)
+    chosen = (safe_flat[:, None] == jnp.arange(vocab_rows)[None, :]).astype(LOW)
+    table_grad = table_grad + product_of("tv,td->vd", chosen, embed_grads.reshape(-1, width))
+    table_low, wide, narrow = lax.optimization_barrier((table_grad.astype(LOW), wide, narrow))
+    table_shard = fold_dp(table_low, dp, 1, 3)[:share]
+    grads = (table_shard,) + unpack_grads(wide, narrow, width, span, slots)
     squares = jnp.zeros((), jnp.float32)
     for grad in grads:
         squares = squares + jnp.sum(grad * grad)

time: 1420 us -> 1150 us (0.81)
  waiting for transfers between devices: 452 us -> 199 us
  Pallas kernels: 203 us -> 373 us
  other arithmetic: 204 us -> 127 us
  matrix products: 281 us -> 225 us
  local copies, waits for them, and re-layouts: 215 us -> 164 us
    unnamed x9, waiting for transfers between devices: 212 us -> 0.16 us
    pallas_call x0 -> x4, Pallas kernels: none -> 183 us  [the longest x1 115 us: gather_weights(): pl.pallas_call(functools.partial(gather_body, dp, n, count), out_shape=[j...]
    all_gather x3, waiting for transfers between devices: 146 us -> 8.58 us  [the longest x1 8.55 us: on_device(): teacher_rows = lax.all_gather(teacher_rows, 'fsdp', axis=0, tiled=True)]
    scatter-add x1 -> x0, other arithmetic: 64 us -> none  [on_device(): jax.ops.segment_sum(embed_grads.astype(jnp.float32).reshape(-1, width), s...]
    reduce_scatter x2 -> x3, waiting for transfers between devices: 65.4 us -> 120 us  [the longest x1 120 us: layer_backward(): wide = lax.psum_scatter(wide, BOTH, scatter_dimension=0, tiled=True)]
    optimization_barrier x0 -> x1, waiting for transfers between devices: none -> 53.6 us  [on_device(): lax.optimization_barrier((table_grad.astype(LOW), wide, narrow))]
    dot_general x30 -> x24, matrix products: 265 us -> 225 us  [product_of(): return jnp.einsum(form, left, right, preferred_element_type=jnp.float32)]
    convert_element_type x3, other arithmetic: 30.3 us -> 2.22 us  [the longest x1 1.14 us: unpack_grads(): narrow = narrow.astype(jnp.float32)]
  transfers between devices with their start and end apart: 8 -> 9, of which waited for: 5 -> 4; matrix products, arithmetic and copies ran while one was open for 12% -> 29% of each run, Pallas kernels for 9% -> 27%
where the time goes in v3:
time: 1150 us; the launch traced here: 1140 us
  Pallas kernels  373 us (32%)
  matrix products  225 us (20%)
  waiting for transfers between devices  199 us (17%)
  local copies, waits for them, and re-layouts  164 us (14%)
  other arithmetic  127 us (11%)
  blocking collectives  29.9 us (3%)
  between operations  25.8 us (2%)
    dot_general x24, matrix products, product_of(): return jnp.einsum(form, left, right, preferred_element_type=jnp.float32)  225 us
    pallas_call x2, Pallas kernels, spread_dp(): pl.pallas_call(functools.partial(spread_body, dp, count), out_shape=[jax....  122 us
    reduce_scatter x1, waiting for transfers between devices, layer_backward(): wide = lax.psum_scatter(wide, BOTH, scatter_dimension=0, tiled=True)  120 us
    pallas_call x1, Pallas kernels, gather_weights(): pl.pallas_call(functools.partial(gather_body, dp, n, count), out_shape=[j...  115 us
    optimization_barrier x1, waiting for transfers between devices, on_device(): lax.optimization_barrier((table_grad.astype(LOW), wide, narrow))  53.6 us
    pallas_call x1, Pallas kernels, fold_dp(): pl.pallas_call(functools.partial(fold_body, dp, pieces), out_shape=jax.Sh...  53.3 us
    gather x1, local copies, waits for them, and re-layouts, on_device(): teacher_hits = teacher_table[safe_flat].reshape(groups * micro, span, width)  40.6 us
    gather x1, local copies, waits for them, and re-layouts, on_device(): student_hits = student_table[safe_flat].reshape(groups * micro, span, width)  40.5 us
  transfers between devices with their start and end apart: 9, of which 4 were waited for; matrix products, arithmetic and copies ran while one was open for 29% of the time, Pallas kernels for 27%

profile of v3, /device:TPU:0, one launch (start us, length us, event | category | flops | bytes accessed | tf_op | source)
XLA Modules:
  0.0 1144.9 jit_solution(5177883374486610556)
XLA Ops:
  19.1 15.7 %all-gather.2 = s32[8,2,640]{2,1,0:T(2,128)S(1)} all-gather(s32[1,2,640]{2,1,0:T(2,128)S(1)} %add_bitcast_fusion), channel_id=1, replica_groups=mesh['dp'=4,'fsdp'=8] {'fsdp'}, dimensions={0}, use_global_device_ids=true | all-gather | bytes 46080 | tf_op jit(solution)/shard_map/all_gather | solution.py:945
  38.2 73.4 %spread_tables.2 = bf16[4,2,480,768]{3,2,1,0:T(8,128)(2,1)} custom-call(bf16[2,480,768]{2,1,0:T(8,128)(2,1)} %bitcast.275), custom_call_target="tpu_custom_call" | custom-call | tf_op jit(solution)/shard_map/spread_tables/pallas_call | solution.py:122
  111.6 40.5 %gather_fusion = bf16[8192,768]{1,0:T(8,128)(2,1)} fusion(bf16[3840,768]{1,0:T(8,128)(2,1)} %bitcast.258, s32[8192]{0:T(1024)S(1)} %broadcast_clamp_fusion), kind=kCustom, calls=%fused_computation | custom fusion | bytes 25198592 | tf_op jit(solution)/shard_map/gather | solution.py:958
  154.7 48.8 %spread_tables.3 = bf16[4,2,480,768]{3,2,1,0:T(8,128)(2,1)} custom-call(bf16[2,480,768]{2,1,0:T(8,128)(2,1)} %bitcast.276), custom_call_target="tpu_custom_call" | custom-call | tf_op jit(solution)/shard_map/spread_tables/pallas_call | solution.py:122
  203.5 40.6 %gather_fusion.1 = bf16[8192,768]{1,0:T(8,128)(2,1)} fusion(bf16[3840,768]{1,0:T(8,128)(2,1)} %bitcast.263, s32[8192]{0:T(1024)S(1)} %broadcast_clamp_fusion), kind=kCustom, calls=%fused_computation.1 | custom fusion | bytes 25198592 | tf_op jit(solution)/shard_map/gather | solution.py:967
  249.8 115.0 %gather_weights.1 = bf16[4,8,2,160,768]{4,3,2,1,0:T(8,128)(2,1)} custom-call(bf16[2,160,768]{2,1,0:T(8,128)(2,1)} %bitcast.296), custom_call_target="tpu_custom_call" | custom-call | tf_op jit(solution)/shard_map/gather_weights/pallas_call | solution.py:332
  394.6 19.4 %attend.2 = bf16[2,512,768]{2,1,0:T(8,128)(2,1)} custom-call(s32[2]{0:T(128)} %lengths.5, bf16[2,512,2304]{2,1,0:T(8,128)(2,1)} %add_convert_fusion.2.q_ref.k_ref.v_ref, bf16[2,512,2304]{2,1,0:T(8,128)(2,1)} %add_convert_fusion.2.q_ref.k_ref.v_ref, bf16[2,512,2304]{2,1,0:T(8,128)(2,1)} %add_convert_fusion.2.q_ref.k_ref.v_ref), custom_call_target="tpu_custom_call" | custom-call | flops 1610612736 | bytes 6291456 | tf_op jit(solution)/shard_map/attend/pallas_call | solution.py:524
  420.4 13.4 %multiply_convert_fusion.2 = (bf16[2,512,3072]{2,1,0:T(8,128)(2,1)}, f32[2,512,3072]{2,1,0:T(8,128)}) fusion(f32[3072]{0:T(1024)S(1)} %copy-done.86, bf16[768,768]{1,0:T(8,128)(2,1)S(1)} %bitcast.305, bf16[768,768]{1,0:T(8,128)(2,1)S(1)} %bitcast.307, bf16[768,768]{1,0:T(8,128)(2,1)S(1)} %bitcast.309, bf16[768,768]{1,0:T(8,128)(2,1)} %bitcast.311, ...), kind=kOutput, calls=%fused_computation.24 | convolution fusion | flops 4873519104 | bytes 26765312 | tf_op jit(solution)/shard_map/bsd,df->bsf/dot_general | solution.py:608
  472.2 19.2 %attend.3 = bf16[2,512,768]{2,1,0:T(8,128)(2,1)} custom-call(s32[2]{0:T(128)} %lengths.5, bf16[2,512,2304]{2,1,0:T(8,128)(2,1)} %add_convert_fusion.1.q_ref.k_ref.v_ref, bf16[2,512,2304]{2,1,0:T(8,128)(2,1)} %add_convert_fusion.1.q_ref.k_ref.v_ref, bf16[2,512,2304]{2,1,0:T(8,128)(2,1)} %add_convert_fusion.1.q_ref.k_ref.v_ref), custom_call_target="tpu_custom_call" | custom-call | flops 1610612736 | bytes 6291456 | tf_op jit(solution)/shard_map/attend/pallas_call | solution.py:524
  516.8 12.9 %fusion.157 = f32[1024,3840]{1,0:T(8,128)} fusion(bf16[1024,768]{1,0:T(8,128)(2,1)} %all-gather.8.cloned.1.call-done, bf16[3840,768]{1,0:T(8,128)(2,1)} %bitcast.259), kind=kOutput, calls=%fused_computation.387 | convolution fusion | flops 6039797760 | bytes 23199744 | tf_op jit(solution)/shard_map/pd,vd->pv/dot_general | solution.py:608
  538.2 16.1 %select_reduce_fusion.1 = (f32[1024]{0:T(1024)S(1)}, f32[1024]{0:T(1024)S(1)}, f32[1024,3840]{1,0:T(8,128)}) fusion(pred[3840]{0:T(1024)(128)(4,1)S(1)} %fusion.99, f32[1024,3840]{1,0:T(8,128)} %fusion.157, bf16[1024,768]{1,0:T(8,128)(2,1)} %all-gather.10.cloned.1.call-done, bf16[3840,768]{1,0:T(8,128)(2,1)} %bitcast.264), kind=kOutput, calls=%fused_computation.16 | convolution fusion | flops 6055524352 | bytes 38940416 | tf_op jit(solution)/shard_map/pd,vd->pv/dot_general | solution.py:608
  554.3 18.9 %multiply_reduce_fusion = (f32[1024]{0:T(1024)S(1)}, f32[1024]{0:T(1024)S(1)}, f32[1024]{0:T(1024)S(1)}, f32[1024]{0:T(1024)S(1)}, f32[1024]{0:T(1024)S(1)}) fusion(f32[1024,3840]{1,0:T(8,128)} %get-tuple-element.385, f32[1024,3840]{1,0:T(8,128)} %fusion.157, f32[1024]{0:T(1024)S(1)} %get-tuple-element.293, pred[3840]{0:T(1024)(128)(4,1)S(1)} %fusion.99, ...), kind=kLoop, calls=%fused_computation.9 | loop fusion | flops 70773760 | bytes 31494912 | tf_op jit(solution)/shard_map/reduce_sum | solution.py:803
  573.3 14.2 %all-gather.1 = f32[64,1024]{1,0:T(8,128)S(1)} all-gather(f32[8,1024]{1,0:T(8,128)S(1)} %stack.43), channel_id=3, replica_groups=mesh['dp'=4,'fsdp'=8] {'fsdp'}, dimensions={0}, use_global_device_ids=true | all-gather | bytes 294912 | tf_op jit(solution)/shard_map/all_gather | solution.py:808
  587.8 18.8 %multiply_convert_fusion = bf16[1024,3840]{1,0:T(8,128)(2,1)S(1)} fusion(f32[1024,3840]{1,0:T(8,128)} %get-tuple-element.385, f32[1024,3840]{1,0:T(8,128)} %fusion.157, f32[1024]{0:T(1024)S(1)} %get-tuple-element.366, f32[1024]{0:T(1024)S(1)} %get-tuple-element.318, f32[1024]{0:T(1024)S(1)} %get-tuple-element.317, s32[1024]{0:T(1024)S(1)} %fusion.116, ...), kind=kLoop, calls=%fused_computation.6 | loop fusion | flops 62914560 | bytes 39346944 | tf_op jit(solution)/shard_map/convert_element_type | solution.py:831
  621.3 12.2 %fusion.158 = f32[3840,768]{1,0:T(8,128)} fusion(bf16[1024,3840]{1,0:T(8,128)(2,1)} %copy-done.15, bf16[1024,768]{1,0:T(8,128)(2,1)} %all-gather.8.cloned.1.call-done), kind=kOutput, calls=%fused_computation.388 | convolution fusion | flops 6039797760 | bytes 21233664 | tf_op jit(solution)/shard_map/pv,pd->vd/dot_general | solution.py:608
  633.6 16.9 %reduce-scatter.12.cloned.1.call-done = bf16[128,768]{1,0:T(8,128)(2,1)} async-done(((bf16[1024,768]{1,0:T(8,128)(2,1)}), bf16[128,768]{1,0:T(8,128)(2,1)}) %reduce-scatter.12.cloned.1.call-update) | async-done | bytes 196624 | tf_op jit(solution)/shard_map/reduce_scatter | solution.py:832
  663.1 13.8 %fusion.156 = (bf16[3072]{0:T(1024)(128)(2,1)S(1)}, bf16[2,512,3072]{2,1,0:T(8,128)(2,1)}) fusion(f32[2,512,3072]{2,1,0:T(8,128)} %get-tuple-element.378, f32[3072]{0:T(1024)S(1)} %copy-done.87, bf16[2,512,768]{2,1,0:T(8,128)(2,1)S(1)} %get-tuple-element.323, bf16[3072,768,1]{1,0,2:T(8,128)(2,1)S(1)} %bitcast.286), kind=kOutput, calls=%fused_computation.386 | convolution fusion | flops 4869583872 | bytes 25184256 | tf_op jit(solution)/shard_map/bsd,fd->bsf/dot_general | solution.py:608
  712.0 29.4 %attend_back.1 = bf16[3,2,512,768]{3,2,1,0:T(8,128)(2,1)} custom-call(s32[2]{0:T(128)} %lengths.5, bf16[2,512,2304]{2,1,0:T(8,128)(2,1)} %add_convert_fusion.2.q_ref.k_ref.v_ref, bf16[2,512,2304]{2,1,0:T(8,128)(2,1)} %add_convert_fusion.2.q_ref.k_ref.v_ref, bf16[2,512,2304]{2,1,0:T(8,128)(2,1)} %add_convert_fusion.2.q_ref.k_ref.v_ref, ...), custom_call_target="tpu_custom_call" | custom-call | flops 4026531840 | bytes 11010048 | tf_op jit(solution)/shard_map/attend_back/pallas_call | solution.py:585
  761.8 21.1 %iota_compare_fusion.14 = pred[8192,3840]{1,0:T(32,128)(4,1)} fusion(s32[8192]{0:T(1024)S(1)} %bitcast.324), kind=kLoop, calls=%fused_computation.2.clone.clone.clone.clone.1 | loop fusion | flops 31457280 | bytes 31490048 | tf_op jit(solution)/shard_map/tv,td->vd/dot_general | solution.py:608
  796.4 119.6 %reduce-scatter.14.cloned.1.call-done = bf16[24,6144]{1,0:T(8,128)(2,1)} async-done(((bf16[768,6144]{1,0:T(8,128)(2,1)}), bf16[24,6144]{1,0:T(8,128)(2,1)}) %reduce-scatter.14.cloned.1.call-update) | async-done | bytes 294928 | tf_op jit(solution)/shard_map/reduce_scatter | solution.py:745
  916.1 60.1 %add_convert_fusion = bf16[3840,768]{1,0:T(8,128)(2,1)} fusion(f32[3840,768]{1,0:T(8,128)} %fusion.158, bf16[8192,768]{1,0:T(8,128)(2,1)} %bitcast.337, pred[8192,3840]{1,0:T(32,128)(4,1)} %iota_compare_fusion.14), kind=kOutput, calls=%fused_computation.26 | convolution fusion | flops 48324280320 | bytes 61734912 | tf_op jit(solution)/shard_map/tv,td->vd/dot_general | solution.py:608
  976.2 53.6 %reduce-scatter.16.cloned.1.call-done = bf16[24,3712]{1,0:T(8,128)(2,1)} async-done(((bf16[768,3712]{1,0:T(8,128)(2,1)}), bf16[24,3712]{1,0:T(8,128)(2,1)}) %reduce-scatter.16.cloned.1.call-update) | async-done | bytes 178192 | tf_op jit(solution)/shard_map/optimization_barrier | solution.py:1044
  1034.1 53.3 %fold_table.1 = f32[2,1,480,768]{3,2,1,0:T(8,128)} custom-call(bf16[4,2,1,480,768]{4,3,2,1,0:T(8,128)(2,1)} %bitcast.277), custom_call_target="tpu_custom_call" | custom-call | tf_op jit(solution)/shard_map/fold_table/pallas_call | solution.py:438
  1098.2 14.8 %total.1 = f32[8,128]{1,0:T(8,128)} custom-call(f32[8,128]{1,0:T(8,128)} %broadcast_in_dim.206.x), custom_call_target="tpu_custom_call" | custom-call | tf_op jit(solution)/shard_map/total/pallas_call | solution.py:476
  (447 shorter events, 257.4 us)
Async XLA Ops:
  8.0 236.1 %all-gather.14.cloned.1.call-start = ((), (), s32[]{:S(2)}) async-start(), calls=%async_computation.12 | async-start | bytes 16220160 | tf_op jit(solution)/shard_map/all_gather | solution.py:956
  17.5 365.2 %reduce-scatter.8.cloned.1.call-start = ((), (), s32[]{:S(2)}) async-start(), calls=%async_computation.5 | async-start | bytes 14155776 | tf_op jit(solution)/shard_map/reduce_scatter | solution.py:961
  34.9 213.2 %copy-start.54 = (s32[16,640]{1,0:T(8,128)}, s32[16,640]{1,0:T(8,128)S(1)}, u32[]{:S(2)}) copy-start(s32[16,640]{1,0:T(8,128)S(1)} %reshape.590) | copy-start | bytes 122884
  152.2 293.6 %reduce-scatter.10.cloned.1.call-start = ((), (), s32[]{:S(2)}) async-start(), calls=%async_computation.6 | async-start | bytes 14155776 | tf_op jit(solution)/shard_map/reduce_scatter | solution.py:971
  244.2 272.5 %all-gather.8.cloned.1.call-start = ((), (), s32[]{:S(2)}) async-start(), calls=%async_computation.7 | async-start | bytes 1769472 | tf_op jit(solution)/shard_map/all_gather | solution.py:987
  248.1 243.4 %copy-start.58 = (pred[2,512]{1,0:T(4,128)(4,1)}, pred[2,512]{1,0:T(4,128)(4,1)S(1)}, u32[]{:S(2)}) copy-start(pred[2,512]{1,0:T(4,128)(4,1)S(1)} %get-tuple-element.321) | copy-start | bytes 3076
  379.2 34.7 %copy-start = (f32[512,768]{1,0:T(8,128)}, f32[512,768]{1,0:T(8,128)S(1)}, u32[]{:S(2)}) copy-start(f32[512,768]{1,0:T(8,128)S(1)} %copy.227) | copy-start | bytes 4718596
  382.2 31.8 %copy-start.60 = (f32[768]{0:T(1024)}, f32[768]{0:T(1024)S(1)}, u32[]{:S(2)}) copy-start(f32[768]{0:T(1024)S(1)} %get-tuple-element.282) | copy-start | bytes 9220
  382.2 31.8 %copy-start.62 = (f32[768]{0:T(1024)}, f32[768]{0:T(1024)S(1)}, u32[]{:S(2)}) copy-start(f32[768]{0:T(1024)S(1)} %get-tuple-element.283) | copy-start | bytes 9220
  382.2 51.6 %copy-start.68 = (f32[768]{0:T(1024)}, f32[768]{0:T(1024)S(1)}, u32[]{:S(2)}) copy-start(f32[768]{0:T(1024)S(1)} %get-tuple-element.276) | copy-start | bytes 9220
  385.0 28.9 %copy-start.66 = (f32[2,512]{1,0:T(2,128)}, f32[2,512]{1,0:T(2,128)S(1)}, u32[]{:S(2)}) copy-start(f32[2,512]{1,0:T(2,128)S(1)} %broadcast_multiply_fusion.11) | copy-start | bytes 12292
  386.1 27.8 %copy-start.77 = (f32[2,512]{1,0:T(2,128)}, f32[2,512]{1,0:T(2,128)S(1)}, u32[]{:S(2)}) copy-start(f32[2,512]{1,0:T(2,128)S(1)} %add_rsqrt_fusion.5) | copy-start | bytes 12292
  461.3 76.9 %all-gather.10.cloned.1.call-start = ((), (), s32[]{:S(2)}) async-start(), calls=%async_computation.8 | async-start | bytes 1769472 | tf_op jit(solution)/shard_map/all_gather | solution.py:991
  512.2 138.3 %reduce-scatter.12.cloned.1.call-start = ((), (), s32[]{:S(2)}) async-start(), calls=%async_computation.9 | async-start | bytes 1769472 | tf_op jit(solution)/shard_map/reduce_scatter | solution.py:832
  554.3 55.4 %slice-start = ((s8[5898240]{0:T(1024)(128)(4,1)}), s8[1703936]{0:T(1024)(128)(4,1)S(1)}, s32[]{:S(2)}) async-start(s8[5898240]{0:T(1024)(128)(4,1)} %bitcast.260), calls=%async_computation.14 | async-start | bytes 3407872
  587.8 22.0 %slice-start.1 = ((s8[5898240]{0:T(1024)(128)(4,1)}), s8[4194304]{0:T(1024)(128)(4,1)S(1)}, s32[]{:S(2)}) async-start(s8[5898240]{0:T(1024)(128)(4,1)} %bitcast.260), calls=%async_computation.15 | async-start | bytes 8388608
  617.1 298.9 %reduce-scatter.14.cloned.1.call-start = ((), (), s32[]{:S(2)}) async-start(), calls=%async_computation.11 | async-start | bytes 9732096 | tf_op jit(solution)/shard_map/reduce_scatter | solution.py:745
  621.3 29.1 %copy-start.5 = (f32[2,512,768]{2,1,0:T(8,128)S(1)}, f32[2,512,768]{2,1,0:T(8,128)}, u32[]{:S(2)}) copy-start(f32[2,512,768]{2,1,0:T(8,128)} %copy-done.4) | copy-start | bytes 9437188
  703.1 213.0 %all-gather.12.cloned.1.call-start = ((), (), s32[]{:S(2)}) async-start(), calls=%async_computation.10 | async-start | bytes 14155776 | tf_op jit(solution)/shard_map/all_gather | solution.py:1035
  760.8 268.9 %reduce-scatter.16.cloned.1.call-start = ((), (), s32[]{:S(2)}) async-start(), calls=%async_computation.13 | async-start | bytes 5879808
  916.1 113.7 %copy-start.27 = (bf16[24,6144]{1,0:T(8,128)(2,1)S(1)}, bf16[24,6144]{1,0:T(8,128)(2,1)}, u32[]{:S(2)}) copy-start(bf16[24,6144]{1,0:T(8,128)(2,1)} %reduce-scatter.14.cloned.1.call-done) | copy-start | bytes 884740
  1030.5 60.2 %copy-start.19 = (f32[24,6144]{1,0:T(8,128)}, f32[24,6144]{1,0:T(8,128)S(1)}, u32[]{:S(2)}) copy-start(f32[24,6144]{1,0:T(8,128)S(1)} %convert_element_type.248) | copy-start | bytes 1769476
  1034.1 96.1 %copy-start.18 = (f32[956,768]{1,0:T(8,128)S(1)}, f32[956,768]{1,0:T(8,128)}, u32[]{:S(2)}) copy-start(f32[956,768]{1,0:T(8,128)} %param.59) | copy-start | bytes 8810500
  1087.4 38.8 %copy-start.49 = (f32[24,2304]{1,0:T(8,128)S(1)}, f32[24,2304]{1,0:T(8,128)}, u32[]{:S(2)}) copy-start(f32[24,2304]{1,0:T(8,128)} %param.39) | copy-start | bytes 663556
  (93 other events, 534.8 us)
Sparse Core Ops, SparseCore 0:
  17.6 132.8 all-gather.13
  703.2 212.7 reduce-scatter.13
  922.8 106.9 reduce-scatter.15
Sparse Core Ops, SparseCore 1:
  152.3 137.6 reduce-scatter.7
  292.1 131.8 reduce-scatter.9
  461.3 25.9 all-gather.7
  512.2 25.9 all-gather.9
  617.2 33.2 reduce-scatter.11
  760.9 128.5 all-gather.11

commit v4 on v3

--- a/solution.py
+++ b/solution.py
@@ -351,135 +351,425 @@
     return [out.reshape(dp * groups, rows, width) for out in outs]
 
 
-def fold_body(dp, pieces, g, out, near_buffer, far_buffer, last_buffer, sems):
+def dot_over(left, right, left_dim, right_dim):
+    return lax.dot_general(
+        left, right, (((left_dim,), (right_dim,)), ((), ())), preferred_element_type=jnp.float32
+    )
+
+
+def added(*values):
+    total = values[0].astype(jnp.float32)
+    for value in values[1:]:
+        total = total + value.astype(jnp.float32)
+    return total
+
+
+def reduce_body(dp, n, g, out, core, far, near, last, right, left, core_sem, far_sem, near_sem,
+                last_sem, line_sem):
+    me = lax.axis_index("fsdp")
+    row = lax.axis_index("dp")
+    p = lax.div(me, 2)
+    c = lax.rem(me, 2)
+    partner = me + 1 - 2 * c
+    ways = ways_of(row, dp)
+    opposite = dp - 1 - row
+    barrier = pltpu.get_barrier_semaphore()
+    order = []
+    for k in range((n + 1) // 2):
+        order += [n - 1 - k] + ([k] if k != n - 1 - k else [])
+
+    def hello(where):
+        pl.semaphore_signal(barrier, inc=1, device_id=where, device_id_type=pl.DeviceIdType.MESH)
+
+    hello({"fsdp": partner})
+    for way in ways:
+        hello({"dp": way})
+
+    @pl.when(p > 0)
+    def _():
+        hello({"fsdp": me - 2})
+
+    @pl.when(p < n - 1)
+    def _():
+        hello({"fsdp": me + 2})
+
+    @pl.when((p > 0) & (p < n - 1))
+    def _():
+        pl.semaphore_wait(barrier, 3 + len(ways))
+
+    @pl.when((p == 0) | (p == n - 1))
+    def _():
+        pl.semaphore_wait(barrier, 2 + len(ways))
+
+    def remote(src, dst, sems, index, where):
+        return pltpu.make_async_remote_copy(
+            src_ref=src,
+            dst_ref=dst,
+            send_sem=sems.at[(0,) + index],
+            recv_sem=sems.at[(1,) + index],
+            device_id=where,
+            device_id_type=pl.DeviceIdType.MESH,
+        )
+
+    def core_copy(j, q, half):
+        return remote(
+            g.at[j, 2 * q + 1 - c, half],
+            core.at[j, q, half],
+            core_sem,
+            (j, q, half),
+            {"fsdp": partner},
+        )
+
+    def far_copy(q, w):
+        return remote(
+            core.at[opposite, q, w], far.at[q, w], far_sem, (q, w), {"dp": ways[w]}
+        )
+
+    def near_copy(q, w):
+        return remote(
+            core.at[ways[w], q, w], near.at[q, w], near_sem, (q, w, 0), {"dp": ways[w]}
+        )
+
+    def last_copy(q, w):
+        return remote(
+            far.at[q, w], last.at[q, w], last_sem, (q, w), {"dp": ways[1 - w]}
+        )
+
+    def direct_copy(hop, q, half):
+        return remote(
+            core.at[ways[hop], q, half],
+            near.at[hop, q, half],
+            near_sem,
+            (q, half, hop),
+            {"dp": ways[hop]},
+        )
+
+    def line_copy(buffer, q, side):
+        return remote(
+            buffer.at[q], buffer.at[q], line_sem, (q, side), {"fsdp": me + 2 - 4 * side}
+        )
+
+    for q in order:
+        for j in [opposite, *ways, row] if dp == 4 else range(dp):
+            for half in range(2):
+                core_copy(j, q, half).start()
+
+    def pair(j, q, half):
+        core_copy(j, q, half).wait_recv()
+        core[j, q, half] = added(core[j, q, half], g[j, 2 * q + c, half]).astype(LOW)
+
+    for q in order:
+        if dp == 4:
+            for w in range(2):
+                pair(opposite, q, w)
+                far_copy(q, w).start()
+            for w in range(2):
+                pair(ways[w], q, w)
+                near_copy(q, w).start()
+            for w in range(2):
+                pair(ways[w], q, 1 - w)
+                pair(row, q, w)
+        else:
+            for half in range(2):
+                for j in range(dp):
+                    pair(j, q, half)
+                for hop in range(dp - 1):
+                    direct_copy(hop, q, half).start()
+    if dp == 4:
+        for q in order:
+            for w in range(2):
+                far_copy(q, w).wait_recv()
+                far[q, w] = added(far[q, w], core[ways[1 - w], q, w]).astype(LOW)
+                last_copy(q, w).start()
+
+    def total(q, half):
+        if dp == 4:
+            near_copy(q, half).wait_recv()
+            last_copy(q, half).wait_recv()
+            return added(core[row, q, half], near[q, half], last[q, half])
+        parts = [core[row, q, half]]
+        for hop in range(dp - 1):
+            direct_copy(hop, q, half).wait_recv()
+            parts.append(near[hop, q, half])
+        return added(*parts)
+
+    for q in order:
+        sums = [total(q, half) for half in range(2)]
+
+        def store(buffer, side, first):
+            for half in range(2):
+                if first:
+                    buffer[q, half] = sums[half].astype(LOW)
+                else:
+                    buffer[q, half] = added(sums[half], buffer[q, half]).astype(LOW)
+            line_copy(buffer, q, side).start()
+
+        if q > 0:
+
+            @pl.when((p > 0) & (p < q))
+            def _():
+                line_copy(right, q, 0).wait_recv()
+                store(right, 0, False)
+
+            @pl.when((p == 0) & (p < q))
+            def _():
+                store(right, 0, True)
+
+        if q < n - 1:
+
+            @pl.when((p < n - 1) & (p > q))
+            def _():
+                line_copy(left, q, 1).wait_recv()
+                store(left, 1, False)
+
+            @pl.when((p == n - 1) & (p > q))
+            def _():
+                store(left, 1, True)
+
+        @pl.when(p == q)
+        def _():
+            for half in range(2):
+                out[half] = sums[half]
+
+    @pl.when(p > 0)
+    def _():
+        line_copy(right, p, 0).wait_recv()
+        out[...] = added(out[...], right[p])
+
+    @pl.when(p < n - 1)
+    def _():
+        line_copy(left, p, 1).wait_recv()
+        out[...] = added(out[...], left[p])
+
+    for q in order:
+        for half in range(2):
+            for j in range(dp):
+                core_copy(j, q, half).wait_send()
+            if dp == 4:
+                far_copy(q, half).wait_send()
+                near_copy(q, half).wait_send()
+                last_copy(q, half).wait_send()
+            else:
+                for hop in range(dp - 1):
+                    direct_copy(hop, q, half).wait_send()
+
+        @pl.when(p < q)
+        def _():
+            line_copy(right, q, 0).wait_send()
+
+        @pl.when(p > q)
+        def _():
+            line_copy(left, q, 1).wait_send()
+
+
+def reduce_weights(g, dp, groups, identity):
+    devices, rows, width = g.shape
+    n = groups // 2
+    half = rows // 2
+    g = g.reshape(dp, groups, 2, half, width)
+    dma = pltpu.SemaphoreType.DMA
+    block = pltpu.VMEM((n, 2, half, width), LOW)
+    near = block if dp == 4 else pltpu.VMEM((dp - 1, n, 2, half, width), LOW)
+    out = pl.pallas_call(
+        functools.partial(reduce_body, dp, n),
+        out_shape=jax.ShapeDtypeStruct((2, half, width), jnp.float32),
+        in_specs=[pl.BlockSpec(memory_space=pltpu.VMEM)],
+        out_specs=pl.BlockSpec(memory_space=pltpu.VMEM),
+        scratch_shapes=[
+            pltpu.VMEM((dp, n, 2, half, width), LOW),
+            block,
+            near,
+            block,
+            block,
+            block,
+            dma((2, dp, n, 2)),
+            dma((2, n, 2)),
+            dma((2, n, 2, max(1, dp - 1))),
+            dma((2, n, 2)),
+            dma((2, n, 2)),
+        ],
+        compiler_params=pltpu.CompilerParams(
+            collective_id=identity, has_side_effects=True, vmem_limit_bytes=56 * MIB
+        ),
+        name="reduce_weights",
+    )(g)
+    return out.reshape(rows, width)
+
+
+def fold_body(dp, step, share, ids, rows, base, out, squares, g, near_buffer, far_buffer, last_buffer, sems):
     me = lax.axis_index("dp")
-    half_rows = pieces
+    half_rows = base.shape[2]
+    tokens = rows.shape[0]
+
+    def fill(dest, half):
+        first = (dest * 2 + half) * half_rows
+        vocab = lax.broadcasted_iota(jnp.int32, (half_rows, step), 0) + first
+
+        def turn(k, total):
+            chosen = (vocab == ids[k]).astype(jnp.float32).astype(LOW)
+            start = pl.multiple_of(k * step, step)
+            return total + dot_over(chosen, rows[pl.ds(start, step), :], 1, 0)
+
+        return lax.fori_loop(0, tokens // step, turn, base[dest, half])
+
     if dp == 4:
         near = [flipped(me, 1), flipped(me, 2)]
-        far = flipped(near[0], 2)
+        far = dp - 1 - me
         greet([{"dp": near[0]}, {"dp": near[1]}])
-        firsts = []
-        seconds = []
-        for i in range(pieces):
-            for link in range(2):
-                firsts.append(
-                    push(
-                        g.at[far, link, i],
-                        far_buffer.at[link, i],
-                        sems.at[0, 0, link, i],
-                        sems.at[1, 0, link, i],
-                        {"dp": near[link]},
-                    )
-                )
-        for i in range(pieces):
-            for link in range(2):
-                firsts.append(
-                    push(
-                        g.at[near[link], link, i],
-                        near_buffer.at[link, i],
-                        sems.at[0, 1, link, i],
-                        sems.at[1, 1, link, i],
-                        {"dp": near[link]},
-                    )
-                )
-        for i in range(pieces):
-            for link in range(2):
-                firsts[2 * i + link].wait_recv()
-                far_buffer[link, i] = (
-                    far_buffer[link, i].astype(jnp.float32)
-                    + g[near[1 - link], link, i].astype(jnp.float32)
-                ).astype(LOW)
-                seconds.append(
-                    push(
-                        far_buffer.at[link, i],
-                        last_buffer.at[link, i],
-                        sems.at[0, 2, link, i],
-                        sems.at[1, 2, link, i],
-                        {"dp": near[1 - link]},
-                    )
-                )
-        for i in range(pieces):
-            for link in range(2):
-                firsts[2 * pieces + 2 * i + link].wait_recv()
-                seconds[2 * i + link].wait_recv()
-                out[link, i] = (
-                    g[me, link, i].astype(jnp.float32)
-                    + near_buffer[link, i].astype(jnp.float32)
-                    + last_buffer[link, i].astype(jnp.float32)
-                )
-        for copy in firsts + seconds:
+
+        def send(kind, w, src, dst, way):
+            return push(src, dst, sems.at[0, kind, w], sems.at[1, kind, w], {"dp": near[way]})
+
+        first, second, third = [], [], []
+        for w in range(2):
+            g[far, w] = fill(far, w).astype(LOW)
+            first.append(send(0, w, g.at[far, w], far_buffer.at[w], w))
+        for w in range(2):
+            g[near[w], w] = fill(near[w], w).astype(LOW)
+            second.append(send(1, w, g.at[near[w], w], near_buffer.at[w], w))
+        for w in range(2):
+            part = fill(near[1 - w], w)
+            first[w].wait_recv()
+            far_buffer[w] = (part + far_buffer[w].astype(jnp.float32)).astype(LOW)
+            third.append(send(2, w, far_buffer.at[w], last_buffer.at[w], 1 - w))
+        for w in range(2):
+            out[w] = fill(me, w)
+        for w in range(2):
+            second[w].wait_recv()
+            third[w].wait_recv()
+            out[w] = (
+                out[w]
+                + near_buffer[w].astype(jnp.float32)
+                + last_buffer[w].astype(jnp.float32)
+            )
+        for copy in first + second + third:
             copy.wait_send()
     else:
         peers = [lax.rem(me + hop, dp) for hop in range(1, dp)]
         greet([{"dp": peer} for peer in peers])
         sent = []
         for hop, peer in enumerate(peers):
+            for half in range(2):
+                g[peer, half] = fill(peer, half).astype(LOW)
             sent.append(
                 push(
                     g.at[peer],
                     near_buffer.at[hop],
-                    sems.at[0, hop, 0, 0],
-                    sems.at[1, hop, 0, 0],
+                    sems.at[0, hop, 0],
+                    sems.at[1, hop, 0],
                     {"dp": peer},
                 )
             )
-        out[...] = g[me].astype(jnp.float32)
+        for half in range(2):
+            out[half] = fill(me, half)
         for hop in range(dp - 1):
             sent[hop].wait()
             out[...] = out[...] + near_buffer[hop].astype(jnp.float32)
-
-
-def fold_dp(g, dp, pieces, identity):
-    rows, width = g.shape[0] // dp, g.shape[1]
-    piece = rows // (2 * pieces)
-    g = g.reshape(dp, 2, pieces, piece, width)
-    small = pltpu.VMEM((2, pieces, piece, width), LOW)
-    first = small if dp == 4 else pltpu.VMEM((dp - 1, 2, pieces, piece, width), LOW)
-    out = pl.pallas_call(
-        functools.partial(fold_body, dp, pieces),
-        out_shape=jax.ShapeDtypeStruct((2, pieces, piece, width), jnp.float32),
+    total = jnp.zeros((1, out.shape[2]), jnp.float32)
+    for half in range(2):
+        index = lax.broadcasted_iota(jnp.int32, (half_rows, 1), 0) + half * half_rows
+        value = jnp.where(index < share, out[half], 0.0)
+        total = total + jnp.sum(value * value, axis=0, keepdims=True)
+    squares[...] = total
+
+
+def fold_dp(ids, rows, base, dp, share, step, identity):
+    tokens, width = rows.shape
+    padded = base.shape[0] // dp
+    half = padded // 2
+    block = pltpu.VMEM((2, half, width), LOW)
+    first = block if dp == 4 else pltpu.VMEM((dp - 1, 2, half, width), LOW)
+    vmem = pl.BlockSpec(memory_space=pltpu.VMEM)
+    out, squares = pl.pallas_call(
+        functools.partial(fold_body, dp, step, share),
+        out_shape=[
+            jax.ShapeDtypeStruct((2, half, width), jnp.float32),
+            jax.ShapeDtypeStruct((1, width), jnp.float32),
+        ],
+        in_specs=[vmem, vmem, vmem],
+        out_specs=[vmem, vmem],
+        scratch_shapes=[
+            pltpu.VMEM((dp, 2, half, width), LOW),
+            first,
+            block,
+            block,
+            pltpu.SemaphoreType.DMA((2, max(3, dp - 1), 2)),
+        ],
+        compiler_params=pltpu.CompilerParams(
+            collective_id=identity, has_side_effects=True, vmem_limit_bytes=58 * MIB
+        ),
+        name="fold_table",
+    )(ids.reshape(tokens // step, 1, step), rows, base.reshape(dp, 2, half, width))
+    return out.reshape(padded, width), squares
+
+
+def share_body(groups, x, out, send, recv):
+    me = lax.axis_index("fsdp")
+    peers = [lax.rem(me + hop, groups) for hop in range(1, groups)]
+    greet([{"fsdp": peer} for peer in peers])
+    sent = []
+    for hop, peer in enumerate(peers):
+        sent.append(push(x, out.at[me], send.at[hop], recv.at[hop], {"fsdp": peer}))
+    out[me] = x[...]
+    for copy in sent:
+        copy.wait()
+
+
+def share_small(x, groups, identity):
+    return pl.pallas_call(
+        functools.partial(share_body, groups),
+        out_shape=jax.ShapeDtypeStruct((groups,) + x.shape, x.dtype),
         in_specs=[pl.BlockSpec(memory_space=pltpu.VMEM)],
         out_specs=pl.BlockSpec(memory_space=pltpu.VMEM),
-        scratch_shapes=[first, small, small, pltpu.SemaphoreType.DMA((2, max(3, dp - 1), 2, pieces))],
-        compiler_params=pltpu.CompilerParams(
-            collective_id=identity, has_side_effects=True, vmem_limit_bytes=56 * MIB
-        ),
-        name="fold_table",
-    )(g)
-    return out.reshape(rows, width)
-
-
-def total_body(dp, groups, x, out, buffer, send, recv):
-    steps = []
-    bit = 1
-    while bit < groups:
-        steps.append({"fsdp": flipped(lax.axis_index("fsdp"), bit)})
-        bit *= 2
-    bit = 1
-    while bit < dp:
-        steps.append({"dp": flipped(lax.axis_index("dp"), bit)})
-        bit *= 2
-    greet(steps)
-    buffer[0, 0] = x[...]
-    for k, peer in enumerate(steps):
-        copy = push(buffer.at[0, k], buffer.at[1, k], send.at[k], recv.at[k], peer)
+        scratch_shapes=[pltpu.SemaphoreType.DMA((groups - 1,))] * 2,
+        compiler_params=pltpu.CompilerParams(collective_id=identity, has_side_effects=True),
+        name="share_small",
+    )(x)
+
+
+def total_body(dp, groups, x, out, fsdp_parts, dp_value, dp_parts, send, recv):
+    me = lax.axis_index("fsdp")
+    row = lax.axis_index("dp")
+    peers = [lax.rem(me + hop, groups) for hop in range(1, groups)]
+    rows = [lax.rem(row + hop, dp) for hop in range(1, dp)]
+    greet([{"fsdp": peer} for peer in peers] + [{"dp": peer} for peer in rows])
+    sent = []
+    for hop, peer in enumerate(peers):
+        sent.append(push(x, fsdp_parts.at[me], send.at[hop], recv.at[hop], {"fsdp": peer}))
+    fsdp_parts[me] = x[...]
+    for copy in sent:
         copy.wait()
-        value = buffer[0, k] + buffer[1, k]
-        if k + 1 < len(steps):
-            buffer[0, k + 1] = value
-        else:
-            out[...] = value
+    value = fsdp_parts[0]
+    for k in range(1, groups):
+        value = value + fsdp_parts[k]
+    dp_value[...] = value
+    dp_parts[row] = value
+    sent = []
+    for hop, peer in enumerate(rows):
+        place = groups - 1 + hop
+        sent.append(
+            push(dp_value, dp_parts.at[row], send.at[place], recv.at[place], {"dp": peer})
+        )
+    for copy in sent:
+        copy.wait()
+    value = dp_parts[0]
+    for k in range(1, dp):
+        value = value + dp_parts[k]
+    out[...] = value
 
 
 def total_all(x, dp, groups, identity):
-    count = (dp - 1).bit_length() + (groups - 1).bit_length()
+    count = dp + groups - 2
+    tile = (8, 128)
     return pl.pallas_call(
         functools.partial(total_body, dp, groups),
-        out_shape=jax.ShapeDtypeStruct((8, 128), jnp.float32),
+        out_shape=jax.ShapeDtypeStruct(tile, jnp.float32),
         in_specs=[pl.BlockSpec(memory_space=pltpu.VMEM)],
         out_specs=pl.BlockSpec(memory_space=pltpu.VMEM),
         scratch_shapes=[
-            pltpu.VMEM((2, count, 8, 128), jnp.float32),
+            pltpu.VMEM((groups,) + tile, jnp.float32),
+            pltpu.VMEM(tile, jnp.float32),
+            pltpu.VMEM((dp,) + tile, jnp.float32),
             pltpu.SemaphoreType.DMA((count,)),
             pltpu.SemaphoreType.DMA((count,)),
         ],
@@ -488,10 +778,145 @@
     )(x)
 
 
-def dot_over(left, right, left_dim, right_dim):
-    return lax.dot_general(
-        left, right, (((left_dim,), (right_dim,)), ((), ())), preferred_element_type=jnp.float32
-    )
+def block_rows(ref_rows, share):
+    block = pl.program_id(0)
+    index = lax.broadcasted_iota(jnp.int32, (ref_rows, 1), 0)
+    real = index + lax.rem(block, 2) * ref_rows < share
+    return index + block * ref_rows, real
+
+
+def student_logits_body(share, rows, table, target, logits, stats):
+    index, real = block_rows(table.shape[0], share)
+    value = jnp.where(real, dot_over(table[...], rows[...], 1, 1), NEGATIVE)
+    logits[...] = value
+    top = jnp.max(value, axis=0, keepdims=True)
+    hit = jnp.sum(jnp.where(index == target[...], value, 0.0), axis=0, keepdims=True)
+
+    @pl.when(pl.program_id(0) == 0)
+    def _():
+        half = jnp.exp((value - top) / SOFTMAX_HEAT)
+        stats[0:1] = top
+        stats[1:2] = jnp.sum(half * half, axis=0, keepdims=True)
+        stats[2:3] = jnp.sum(half, axis=0, keepdims=True)
+        stats[3:4] = hit
+
+    @pl.when(pl.program_id(0) > 0)
+    def _():
+        before = stats[0:1]
+        peak = jnp.maximum(before, top)
+        fall = jnp.exp((before - peak) / SOFTMAX_HEAT)
+        half = jnp.exp((value - peak) / SOFTMAX_HEAT)
+        stats[0:1] = peak
+        stats[1:2] = stats[1:2] * fall * fall + jnp.sum(half * half, axis=0, keepdims=True)
+        stats[2:3] = stats[2:3] * fall + jnp.sum(half, axis=0, keepdims=True)
+        stats[3:4] = stats[3:4] + hit
+
+
+def teacher_logits_body(share, rows, table, student, logits, stats):
+    _, real = block_rows(table.shape[0], share)
+    value = jnp.where(real, dot_over(table[...], rows[...], 1, 1), NEGATIVE)
+    logits[...] = value
+    top = jnp.max(value, axis=0, keepdims=True)
+    gap = (value - student[...]) / SOFTMAX_HEAT
+
+    @pl.when(pl.program_id(0) == 0)
+    def _():
+        exponent = jnp.exp((value - top) / SOFTMAX_HEAT)
+        stats[0:1] = top
+        stats[1:2] = jnp.sum(exponent, axis=0, keepdims=True)
+        stats[2:3] = jnp.sum(exponent * gap, axis=0, keepdims=True)
+        stats[3:4] = jnp.zeros_like(top)
+
+    @pl.when(pl.program_id(0) > 0)
+    def _():
+        before = stats[0:1]
+        peak = jnp.maximum(before, top)
+        fall = jnp.exp((before - peak) / SOFTMAX_HEAT)
+        exponent = jnp.exp((value - peak) / SOFTMAX_HEAT)
+        stats[0:1] = peak
+        stats[1:2] = stats[1:2] * fall + jnp.sum(exponent, axis=0, keepdims=True)
+        stats[2:3] = stats[2:3] * fall + jnp.sum(exponent * gap, axis=0, keepdims=True)
+
+
+def logits_call(body, rows, table, other, block, name):
+    count, width = rows.shape
+    vocab = table.shape[0]
+    wide = pl.BlockSpec((block, count), lambda v: (v, 0))
+    whole = pl.BlockSpec(memory_space=pltpu.VMEM)
+    return pl.pallas_call(
+        body,
+        grid=(vocab // block,),
+        in_specs=[
+            whole,
+            pl.BlockSpec((block, width), lambda v: (v, 0)),
+            wide if other.shape[0] == vocab else whole,
+        ],
+        out_specs=[wide, pl.BlockSpec((4, count), lambda v: (0, 0))],
+        out_shape=[
+            jax.ShapeDtypeStruct((vocab, count), jnp.float32),
+            jax.ShapeDtypeStruct((4, count), jnp.float32),
+        ],
+        compiler_params=pltpu.CompilerParams(vmem_limit_bytes=40 * MIB),
+        cost_estimate=pl.CostEstimate(
+            flops=2 * vocab * count * width,
+            bytes_accessed=4 * vocab * count + 2 * vocab * width,
+            transcendentals=vocab * count,
+        ),
+        name=name,
+    )(rows, table, other)
+
+
+def logits_back_body(student, teacher, table, consts, target, d_logits, d_rows, total):
+    index = lax.broadcasted_iota(jnp.int32, (table.shape[0], 1), 0)
+    index = index + pl.program_id(0) * table.shape[0]
+    value = student[...]
+    hard = jnp.exp(value - consts[0:1]) - (index == target[...]).astype(jnp.float32)
+    soft = jnp.exp(value / SOFTMAX_HEAT - consts[1:2]) - jnp.exp(
+        teacher[...] / SOFTMAX_HEAT - consts[2:3]
+    )
+    mixed = consts[3:4] * (
+        (1.0 - SOFT_FRACTION) * hard + SOFT_FRACTION * SOFTMAX_HEAT * soft
+    )
+    low = mixed.astype(LOW)
+    d_logits[...] = low
+    part = dot_over(low, table[...], 0, 0)
+
+    @pl.when(pl.program_id(0) == 0)
+    def _():
+        total[...] = part
+
+    @pl.when(pl.program_id(0) > 0)
+    def _():
+        total[...] += part
+
+    @pl.when(pl.program_id(0) == pl.num_programs(0) - 1)
+    def _():
+        d_rows[...] = total[...].astype(LOW)
+
+
+def logits_back(student, teacher, table, consts, target, block):
+    vocab, count = student.shape
+    width = table.shape[1]
+    wide = pl.BlockSpec((block, count), lambda v: (v, 0))
+    whole = pl.BlockSpec(memory_space=pltpu.VMEM)
+    return pl.pallas_call(
+        logits_back_body,
+        grid=(vocab // block,),
+        in_specs=[wide, wide, pl.BlockSpec((block, width), lambda v: (v, 0)), whole, whole],
+        out_specs=[wide, pl.BlockSpec((count, width), lambda v: (0, 0))],
+        out_shape=[
+            jax.ShapeDtypeStruct((vocab, count), LOW),
+            jax.ShapeDtypeStruct((count, width), LOW),
+        ],
+        scratch_shapes=[pltpu.VMEM((count, width), jnp.float32)],
+        compiler_params=pltpu.CompilerParams(vmem_limit_bytes=48 * MIB),
+        cost_estimate=pl.CostEstimate(
+            flops=2 * vocab * count * width,
+            bytes_accessed=10 * vocab * count + 2 * vocab * width,
+            transcendentals=3 * vocab * count,
+        ),
+        name="logits_back",
+    )(student, teacher, table, consts, target)
 
 
 def attend_body(lengths, q_ref, k_ref, v_ref, out_ref):
@@ -717,7 +1142,7 @@
     )
 
 
-def layer_backward(grad, weights, kept, lengths, devices):
+def layer_backward(grad, weights, kept, lengths):
     w_qkv, w_out, w_up, w_down, small = weights[:5]
     (
         value_low,
@@ -736,13 +1161,8 @@
         grad, normed_second, inverse_second, small[10]
     )
     d_down = d_second.astype(LOW)
-    g_down = product_of("bsf,bsd->fd", act_low, d_down)
     d_up = (product_of("bsd,fd->bsf", d_down, w_down) * slope).astype(LOW)
-    g_up = product_of("bsd,bsf->df", first_low, d_up)
     d_first = d_second + product_of("bsf,df->bsd", d_up, w_up)
-    wide = pack_wide(g_up, g_down, devices)
-    d_first, wide = lax.optimization_barrier((d_first, wide))
-    wide = lax.psum_scatter(wide, BOTH, scatter_dimension=0, tiled=True)
     d_sum, gain_first, shift_first = layer_norm_back(d_first, normed_first, inverse_first, small[8])
     d_attn = d_sum.astype(LOW)
     d_context = product_of("bsd,cd->bsc", d_attn, w_out).astype(LOW)
@@ -766,7 +1186,13 @@
             shift_second[None],
         ]
     )
-    return wide, (value_low, d_joined, context, d_attn), rows_grad, d_value
+    factors = (
+        (value_low, d_joined),
+        (context, d_attn),
+        (first_low, d_up),
+        (act_low, d_down),
+    )
+    return factors, rows_grad, d_value
 
 
 def label_rows(pick, out):
@@ -783,59 +1209,45 @@
     micro, labels, span = pick.shape
     width = all_student.shape[1]
     mine = micro * labels
-    row_index = jnp.arange(vocab_rows)
-    real = (row_index % padded < share)[None, :]
     inside, local_target = owned(targets, share, padded, groups, own)
-    hit = (row_index[None, :] == local_target[:, None]) & inside[:, None]
-    student = jnp.where(real, product_of("pd,vd->pv", all_student, table_student), NEGATIVE)
-    teacher = jnp.where(real, product_of("pd,vd->pv", all_teacher, table_teacher), NEGATIVE)
-    top_student = jnp.max(student, axis=1)
-    top_teacher = jnp.max(teacher, axis=1)
-    half = jnp.exp((student - top_student[:, None]) / SOFTMAX_HEAT)
-    teacher_exp = jnp.exp((teacher - top_teacher[:, None]) / SOFTMAX_HEAT)
-    stats = jnp.stack(
-        [
-            top_student,
-            jnp.sum(half * half, axis=1),
-            jnp.sum(half, axis=1),
-            top_teacher,
-            jnp.sum(teacher_exp, axis=1),
-            jnp.sum(teacher_exp * ((teacher - student) / SOFTMAX_HEAT), axis=1),
-            jnp.sum(jnp.where(hit, student, 0.0), axis=1),
-            jnp.zeros_like(top_student),
-        ]
-    )
-    stats = lax.all_gather(stats, "fsdp")
+    target = jnp.where(inside, local_target, -1)[None, :]
+    block = padded // 2
+    student, student_stats = logits_call(
+        functools.partial(student_logits_body, share),
+        all_student,
+        table_student,
+        target,
+        block,
+        "student_logits",
+    )
+    teacher, teacher_stats = logits_call(
+        functools.partial(teacher_logits_body, share),
+        all_teacher,
+        table_teacher,
+        student,
+        block,
+        "teacher_logits",
+    )
+    stats = share_small(jnp.concatenate([student_stats, teacher_stats]), groups, 8)
     peak_student = jnp.max(stats[:, 0], axis=0)
-    peak_teacher = jnp.max(stats[:, 3], axis=0)
+    peak_teacher = jnp.max(stats[:, 4], axis=0)
     fall_student = jnp.exp((stats[:, 0] - peak_student) / SOFTMAX_HEAT)
-    fall_teacher = jnp.exp((stats[:, 3] - peak_teacher) / SOFTMAX_HEAT)
+    fall_teacher = jnp.exp((stats[:, 4] - peak_teacher) / SOFTMAX_HEAT)
     sum_plain = jnp.sum(stats[:, 1] * fall_student * fall_student, axis=0)
     sum_soft = jnp.sum(stats[:, 2] * fall_student, axis=0)
-    sum_teacher = jnp.sum(stats[:, 4] * fall_teacher, axis=0)
-    cross = jnp.sum(stats[:, 5] * fall_teacher, axis=0)
-    target_logit = jnp.sum(stats[:, 6], axis=0)
+    sum_teacher = jnp.sum(stats[:, 5] * fall_teacher, axis=0)
+    cross = jnp.sum(stats[:, 6] * fall_teacher, axis=0)
+    target_logit = jnp.sum(stats[:, 3], axis=0)
     lse_plain = peak_student + jnp.log(sum_plain)
     lse_soft = peak_student / SOFTMAX_HEAT + jnp.log(sum_soft)
     lse_teacher = peak_teacher / SOFTMAX_HEAT + jnp.log(sum_teacher)
     cross_entropy = lse_plain - target_logit
     divergence_loss = cross / sum_teacher - lse_teacher + lse_soft
     share_lab = valid_mask / count
-    hard = jnp.exp(student - lse_plain[:, None]) - hit.astype(jnp.float32)
-    soft = jnp.exp(student / SOFTMAX_HEAT - lse_soft[:, None]) - jnp.exp(
-        teacher / SOFTMAX_HEAT - lse_teacher[:, None]
-    )
-    d_logits = (
-        share_lab[:, None]
-        * ((1.0 - SOFT_FRACTION) * hard + SOFT_FRACTION * SOFTMAX_HEAT * soft)
-    ).astype(LOW)
-    d_rows = lax.psum_scatter(
-        product_of("pv,vd->pd", d_logits, table_student).astype(LOW),
-        "fsdp",
-        scatter_dimension=0,
-        tiled=True,
-    )
-    table_term = product_of("pv,pd->vd", d_logits, all_student)
+    consts = jnp.stack([lse_plain, lse_soft, lse_teacher, share_lab])
+    d_logits, d_rows = logits_back(student, teacher, table_student, consts, target, block)
+    d_rows = lax.psum_scatter(d_rows, "fsdp", scatter_dimension=0, tiled=True)
+    table_term = product_of("vp,pd->vd", d_logits, all_student)
     d_rows, table_term = lax.optimization_barrier((d_rows, table_term))
     terms = share_lab * (
         (1.0 - SOFT_FRACTION) * cross_entropy
@@ -846,44 +1258,43 @@
     return (d_out, table_term, jnp.sum(local))
 
 
-def pack_wide(g_up, g_down, devices):
-    width = g_up.shape[0]
-    ff = g_down.shape[0]
-    g_down = (
-        g_down.astype(LOW)
-        .reshape(devices, ff // width, width // devices, width)
-        .transpose(0, 2, 1, 3)
-        .reshape(width, ff)
-    )
-    return jnp.concatenate([g_up.astype(LOW), g_down], axis=1)
-
-
-def pack_narrow(g_qkv, g_out, small_grad, position_grad):
-    pad = -small_grad.shape[0] % 128
-    return jnp.concatenate(
-        [
-            g_qkv.astype(LOW),
-            g_out.astype(LOW),
-            position_grad.astype(LOW).T,
-            jnp.pad(small_grad, ((0, pad), (0, 0))).astype(LOW).T,
-        ],
-        axis=1,
-    )
-
-
-def unpack_grads(wide, narrow, width, span, slots):
-    ff = 4 * width
-    wide = wide.astype(jnp.float32)
-    narrow = narrow.astype(jnp.float32)
-    down = wide[:, ff:]
-    g_down = jnp.concatenate([down[:, k * width : (k + 1) * width] for k in range(4)], axis=0)
+def pack_grads(g_qkv, g_out, g_up, g_down, small_grad, position_grad, devices):
+    width = g_out.shape[0]
+    rows = width // devices
+
+    def shards(grad):
+        return grad.astype(LOW).reshape(devices, -1, width)
+
+    pieces = [shards(g_qkv[:, k * width : (k + 1) * width]) for k in range(3)]
+    pieces += [shards(g_out)]
+    pieces += [shards(g_up[:, k * width : (k + 1) * width]) for k in range(4)]
+    pieces += [shards(g_down)]
+    rest = jnp.concatenate([position_grad, small_grad], axis=0)
+    rest = jnp.pad(rest, ((0, width - rest.shape[0]), (0, 0))).T
+    pieces += [shards(rest)]
+    filled = 8 * rows + g_down.shape[0] // devices + rows
+    pad = -filled % 32
+    if pad:
+        pieces += [jnp.zeros((devices, pad, width), LOW)]
+    return jnp.concatenate(pieces, axis=1)
+
+
+def unpack_grads(packed, rows, span, slots):
+    width = packed.shape[1]
+    down = packed.shape[1] * 4 * rows // width
+    low = 8 * rows
+
+    def part(first):
+        return packed[first * rows : (first + 1) * rows]
+
+    rest = packed[low + down : low + down + rows]
     return (
-        narrow[:, : 3 * width],
-        narrow[:, 3 * width : 4 * width],
-        wide[:, :ff],
-        g_down,
-        narrow[:, 4 * width + span : 4 * width + span + slots].T,
-        narrow[:, 4 * width : 4 * width + span].T,
+        jnp.concatenate([part(k) for k in range(3)], axis=1),
+        part(3),
+        jnp.concatenate([part(4 + k) for k in range(4)], axis=1),
+        packed[low : low + down],
+        rest[:, span : span + slots].T,
+        rest[:, :span].T,
     )
 
 
@@ -942,7 +1353,8 @@
     info = jnp.concatenate(
         [tok_ids, label_ids, jnp.broadcast_to(seq_len[:, None], (micro, labels))], axis=1
     )
-    info = lax.all_gather(info, "fsdp", axis=0, tiled=True)
+    info = jnp.pad(info, ((0, -micro % 8), (0, 0)))
+    info = share_small(info, groups, 7)[:, :micro].reshape(groups * micro, span + 2 * labels)
     ids_all = info[:, :span]
     targets_all = info[:, span : span + labels].reshape(-1)
     lengths_all = info[:, span + labels]
@@ -952,7 +1364,10 @@
     extra = jnp.broadcast_to(counts.astype(LOW)[None, :], (rows_own, 2))
 
     safe_ids = owned(ids_all, share, padded, groups, own)[1]
-    packed_teacher = pack_layer((t_qkv, t_out, t_up, t_down, t_small, t_position), None)
+    t_weights, student_table = lax.optimization_barrier(
+        ((t_qkv, t_out, t_up, t_down, t_small, t_position), student_table)
+    )
+    packed_teacher = pack_layer(t_weights, None)
     packed_teacher = lax.all_gather(packed_teacher, BOTH)
     safe_flat = safe_ids.reshape(-1)
     student_hits = student_table[safe_flat].reshape(groups * micro, span, width)
@@ -1016,7 +1431,7 @@
     d_out = d_out + first_row * d_cls[:, None, :]
     loss_part = label_loss + jnp.sum(weight_pkd * gap * gap)
 
-    wide, factors, rows_grad, d_start = layer_backward(d_out, weights, kept, seq_len, devices)
+    factors, rows_grad, d_start = layer_backward(d_out, weights, kept, seq_len)
     d_embed, gain_embed, shift_embed = layer_norm_back(
         d_start, normed_start, inverse_start, weights[4][12]
     )
@@ -1033,20 +1448,21 @@
     position_grad = jnp.sum(d_embed, axis=0)
     d_embed_low, factors = lax.optimization_barrier((d_embed.astype(LOW), factors))
     embed_grads = lax.all_gather(d_embed_low, "fsdp", axis=0, tiled=True)
-    value_low, d_joined, context, d_attn = factors
-    g_qkv = product_of("bsd,bsf->df", value_low, d_joined)
-    g_out = product_of("bsc,bsd->cd", context, d_attn)
-    narrow = pack_narrow(g_qkv, g_out, small_grad, position_grad)
-    narrow, wide = lax.optimization_barrier((narrow, wide))
-    narrow = lax.psum_scatter(narrow, BOTH, scatter_dimension=0, tiled=True)
-    chosen = (safe_flat[:, None] == jnp.arange(vocab_rows)[None, :]).astype(LOW)
-    table_grad = table_grad + product_of("tv,td->vd", chosen, embed_grads.reshape(-1, width))
-    table_low, wide, narrow = lax.optimization_barrier((table_grad.astype(LOW), wide, narrow))
-    table_shard = fold_dp(table_low, dp, 1, 3)[:share]
-    grads = (table_shard,) + unpack_grads(wide, narrow, width, span, slots)
-    squares = jnp.zeros((), jnp.float32)
-    for grad in grads:
-        squares = squares + jnp.sum(grad * grad)
+    matrices = [
+        product_of("bsd,bsf->df", left, right) for left, right in factors
+    ]
+    packed_grads = pack_grads(*matrices, small_grad, position_grad, devices)
+    packed_grads = reduce_weights(packed_grads, dp, groups, 6)
+    layer_squares = jnp.sum(packed_grads * packed_grads)
+    table_grad, embed_grads, packed_grads, layer_squares = lax.optimization_barrier(
+        (table_grad, embed_grads, packed_grads, layer_squares)
+    )
+    table_shard, table_squares = fold_dp(
+        safe_flat, embed_grads.reshape(-1, width), table_grad, dp, share, 2048, 3
+    )
+    table_shard = table_shard[:share]
+    grads = (table_shard,) + unpack_grads(packed_grads, rows_own, span, slots)
+    squares = layer_squares + jnp.sum(table_squares)
     column = jnp.arange(128)[None, :]
     sums = jnp.where(column == 0, squares, jnp.where(column == 1, loss_part, 0.0))
     sums = total_all(jnp.broadcast_to(sums, (8, 128)), dp, groups, 4)

time: 1150 us -> 995 us (0.87)
  Pallas kernels: 373 us -> 589 us
  waiting for transfers between devices: 199 us -> 32.3 us
  matrix products: 225 us -> 123 us
  other arithmetic: 127 us -> 52.2 us
  blocking collectives: 29.9 us -> 0 us
    pallas_call x1 -> x7, Pallas kernels: 53.3 us -> 274 us  [the longest x1 122 us: reduce_weights(): pl.pallas_call(functools.partial(reduce_body, dp, n), out_shape=jax.Shape...]
    reduce_scatter x2 -> x1, waiting for transfers between devices: 136 us -> 18 us  [label_head(): d_rows = lax.psum_scatter(d_rows, 'fsdp', scatter_dimension=0, tiled=True)]
    dot_general x24 -> x20, matrix products: 225 us -> 123 us  [product_of(): return jnp.einsum(form, left, right, preferred_element_type=jnp.float32)]
    optimization_barrier x1 -> x0, waiting for transfers between devices: 53.6 us -> none  [on_device(): lax.optimization_barrier((table_grad.astype(LOW), wide, narrow))]
    all_gather x2 -> x0, blocking collectives: 29.9 us -> none  [the longest x1 15.7 us: on_device(): info = lax.all_gather(info, 'fsdp', axis=0, tiled=True)]
    reduce_sum x10 -> x3, other arithmetic: 33.7 us -> 6.82 us  [the longest x1 3.33 us: on_device(): jnp.sum(d_embed * (1.0 - zero_segment), axis=(0, 1))[None]]
    dot_general x1 -> x0, other arithmetic: 21.1 us -> none  [product_of(): return jnp.einsum(form, left, right, preferred_element_type=jnp.float32)]
    convert_element_type x3 -> x1, other arithmetic: 20 us -> 0.55 us  [layer_forward(): first_low = first.astype(LOW)]
  transfers between devices with their start and end apart: 9 -> 7, of which waited for: 4 -> 3; matrix products, arithmetic and copies ran while one was open for 29% -> 23% of each run, Pallas kernels for 27% -> 37%
where the time goes in v4:
time: 995 us; the launch traced here: 989 us
  Pallas kernels  589 us (59%)
  local copies, waits for them, and re-layouts  170 us (17%)
  matrix products  123 us (12%)
  other arithmetic  52.2 us (5%)
  waiting for transfers between devices  32.3 us (3%)
  between operations  22.7 us (2%)
    pallas_call x2, Pallas kernels, spread_dp(): pl.pallas_call(functools.partial(spread_body, dp, count), out_shape=[jax....  132 us
    dot_general x20, matrix products, product_of(): return jnp.einsum(form, left, right, preferred_element_type=jnp.float32)  123 us
    pallas_call x1, Pallas kernels, reduce_weights(): pl.pallas_call(functools.partial(reduce_body, dp, n), out_shape=jax.Shape...  122 us
    pallas_call x1, Pallas kernels, gather_weights(): pl.pallas_call(functools.partial(gather_body, dp, n, count), out_shape=[j...  106 us
    pallas_call x1, Pallas kernels, fold_dp(): pl.pallas_call(functools.partial(fold_body, dp, step, share), out_shape=[...  75.5 us
    gather x1, local copies, waits for them, and re-layouts, on_device(): teacher_hits = teacher_table[safe_flat].reshape(groups * micro, span, width)  40.6 us
    gather x1, local copies, waits for them, and re-layouts, on_device(): student_hits = student_table[safe_flat].reshape(groups * micro, span, width)  40.5 us
    unnamed x227, local copies, waits for them, and re-layouts  39.2 us
  transfers between devices with their start and end apart: 7, of which 3 were waited for; matrix products, arithmetic and copies ran while one was open for 23% of the time, Pallas kernels for 37%

profile of v4, /device:TPU:0, one launch (start us, length us, event | category | flops | bytes accessed | tf_op | source)
XLA Modules:
  0.0 989.1 jit_solution(7594143156872956370)
XLA Ops:
  11.3 52.7 %spread_tables.2 = bf16[4,2,480,768]{3,2,1,0:T(8,128)(2,1)} custom-call(bf16[2,480,768]{2,1,0:T(8,128)(2,1)} %bitcast.263), custom_call_target="tpu_custom_call" | custom-call | tf_op jit(solution)/shard_map/spread_tables/pallas_call | solution.py:122
  66.0 8.8 share_small.2
  76.0 40.5 %gather_fusion = bf16[8192,768]{1,0:T(8,128)(2,1)} fusion(bf16[3840,768]{1,0:T(8,128)(2,1)} %bitcast.246, s32[8192]{0:T(1024)S(1)} %broadcast_clamp_fusion), kind=kCustom, calls=%fused_computation | custom fusion | bytes 25198592 | tf_op jit(solution)/shard_map/gather | solution.py:1373
  119.1 78.9 %spread_tables.3 = bf16[4,2,480,768]{3,2,1,0:T(8,128)(2,1)} custom-call(bf16[2,480,768]{2,1,0:T(8,128)(2,1)} %bitcast.264), custom_call_target="tpu_custom_call" | custom-call | tf_op jit(solution)/shard_map/spread_tables/pallas_call | solution.py:122
  198.0 40.6 %gather_fusion.1 = bf16[8192,768]{1,0:T(8,128)(2,1)} fusion(bf16[3840,768]{1,0:T(8,128)(2,1)} %bitcast.249, s32[8192]{0:T(1024)S(1)} %broadcast_clamp_fusion), kind=kCustom, calls=%fused_computation.1 | custom fusion | bytes 25198592 | tf_op jit(solution)/shard_map/gather | solution.py:1382
  243.1 105.5 %gather_weights.1 = bf16[4,8,2,160,768]{4,3,2,1,0:T(8,128)(2,1)} custom-call(bf16[2,160,768]{2,1,0:T(8,128)(2,1)} %bitcast.287), custom_call_target="tpu_custom_call" | custom-call | tf_op jit(solution)/shard_map/gather_weights/pallas_call | solution.py:332
  377.5 19.2 %attend.2 = bf16[2,512,768]{2,1,0:T(8,128)(2,1)} custom-call(s32[2]{0:T(128)} %lengths.5, bf16[2,512,2304]{2,1,0:T(8,128)(2,1)} %add_convert_fusion.1.q_ref.k_ref.v_ref, bf16[2,512,2304]{2,1,0:T(8,128)(2,1)} %add_convert_fusion.1.q_ref.k_ref.v_ref, bf16[2,512,2304]{2,1,0:T(8,128)(2,1)} %add_convert_fusion.1.q_ref.k_ref.v_ref), custom_call_target="tpu_custom_call" | custom-call | flops 1610612736 | bytes 6291456 | tf_op jit(solution)/shard_map/attend/pallas_call | solution.py:949
  404.4 11.3 %multiply_convert_fusion.1 = (bf16[2,512,3072]{2,1,0:T(8,128)(2,1)S(1)}, f32[2,512,3072]{2,1,0:T(8,128)}) fusion(f32[3072]{0:T(1024)S(1)} %add.504, bf16[2,512,768]{2,1,0:T(8,128)(2,1)S(1)} %fusion.24, bf16[768,768]{1,0:T(8,128)(2,1)S(1)} %bitcast.300, bf16[768,768]{1,0:T(8,128)(2,1)S(1)} %bitcast.302, bf16[768,768]{1,0:T(8,128)(2,1)S(1)} %bitcast.304, ...), kind=kOutput, calls=%fused_computation.10 | convolution fusion | flops 4869586944 | bytes 25178112 | tf_op jit(solution)/shard_map/bsd,df->bsf/dot_general | solution.py:1033
  425.6 12.9 %reduce-scatter.6.cloned.1.call-done = bf16[2,512,768]{2,1,0:T(8,128)(2,1)} async-done(((bf16[16,512,768]{2,1,0:T(8,128)(2,1)}), bf16[2,512,768]{2,1,0:T(8,128)(2,1)}) %reduce-scatter.6.cloned.1.call-update) | async-done | bytes 1572880 | tf_op jit(solution)/shard_map/reduce_scatter | solution.py:1386
  464.9 19.2 %attend.3 = bf16[2,512,768]{2,1,0:T(8,128)(2,1)} custom-call(s32[2]{0:T(128)} %lengths.5, bf16[2,512,2304]{2,1,0:T(8,128)(2,1)} %add_convert_fusion.q_ref.k_ref.v_ref, bf16[2,512,2304]{2,1,0:T(8,128)(2,1)} %add_convert_fusion.q_ref.k_ref.v_ref, bf16[2,512,2304]{2,1,0:T(8,128)(2,1)} %add_convert_fusion.q_ref.k_ref.v_ref), custom_call_target="tpu_custom_call" | custom-call | flops 1610612736 | bytes 6291456 | tf_op jit(solution)/shard_map/attend/pallas_call | solution.py:949
  512.4 15.2 %student_logits.1 = (f32[3840,1024]{1,0:T(8,128)}, f32[4,1024]{1,0:T(4,128)S(1)}) custom-call(bf16[1024,768]{1,0:T(8,128)(2,1)S(1)} %copy-done.3, bf16[3840,768]{1,0:T(8,128)(2,1)S(1)} %bitcast.248, s32[1,1024]{1,0:T(1,128)S(1)} %compare_select_fusion.4.target), custom_call_target="tpu_custom_call" | custom-call | flops 6039797760 | bytes 21626880 | tf_op jit(solution)/shard_map/student_logits/pallas_call | solution.py:846
  532.9 18.9 %teacher_logits.1 = (f32[3840,1024]{1,0:T(8,128)}, f32[4,1024]{1,0:T(4,128)S(1)}) custom-call(bf16[1024,768]{1,0:T(8,128)(2,1)S(1)} %copy-done.2, bf16[3840,768]{1,0:T(8,128)(2,1)S(1)} %bitcast.250, f32[3840,1024]{1,0:T(8,128)} %get-tuple-element.84.student), custom_call_target="tpu_custom_call" | custom-call | flops 6039797760 | bytes 21626880 | tf_op jit(solution)/shard_map/teacher_logits/pallas_call | solution.py:846
  552.5 9.3 share_small.3
  564.1 24.0 %logits_back.1 = (bf16[3840,1024]{1,0:T(8,128)(2,1)}, bf16[1024,768]{1,0:T(8,128)(2,1)}) custom-call(f32[3840,1024]{1,0:T(8,128)} %get-tuple-element.84.student, f32[3840,1024]{1,0:T(8,128)} %get-tuple-element.87.teacher, bf16[3840,768]{1,0:T(8,128)(2,1)} %bitcast.247, f32[4,1024]{1,0:T(4,128)S(1)} %pad_maximum_fusion.4.consts, ...), custom_call_target="tpu_custom_call" | custom-call | flops 6039797760 | bytes 45219840 | tf_op jit(solution)/shard_map/logits_back/pallas_call | solution.py:902
  592.3 12.5 %fusion.142 = f32[3840,768]{1,0:T(8,128)} fusion(bf16[3840,1024]{1,0:T(8,128)(2,1)} %get-tuple-element.91, bf16[1024,768]{1,0:T(8,128)(2,1)S(1)} %copy-done.4), kind=kOutput, calls=%fused_computation.364 | convolution fusion | flops 6039797760 | bytes 21233664 | tf_op jit(solution)/shard_map/vp,pd->vd/dot_general | solution.py:1033
  604.8 18.0 %reduce-scatter.8.cloned.1.call-done = bf16[128,768]{1,0:T(8,128)(2,1)} async-done(((bf16[1024,768]{1,0:T(8,128)(2,1)}), bf16[128,768]{1,0:T(8,128)(2,1)}) %reduce-scatter.8.cloned.1.call-update) | async-done | bytes 196624 | tf_op jit(solution)/shard_map/reduce_scatter | solution.py:1249
  628.2 14.2 %fusion.141 = (bf16[3072]{0:T(1024)(128)(2,1)S(1)}, bf16[2,512,3072]{2,1,0:T(8,128)(2,1)}) fusion(f32[2,512,3072]{2,1,0:T(8,128)} %get-tuple-element.413, f32[3072]{0:T(1024)S(1)} %add.504, bf16[2,512,768]{2,1,0:T(8,128)(2,1)S(1)} %get-tuple-element.102, bf16[3072,768,1]{1,0,2:T(8,128)(2,1)} %bitcast.275), kind=kOutput, calls=%fused_computation.363 | convolution fusion | flops 4869583872 | bytes 25184256 | tf_op jit(solution)/shard_map/bsd,fd->bsf/dot_general | solution.py:1033
  642.4 11.3 %multiply_reduce_fusion.4 = (bf16[768]{0:T(1024)(128)(2,1)S(1)}, f32[2,512]{1,0:T(2,128)S(1)}, f32[2,512]{1,0:T(2,128)S(1)}, bf16[768]{0:T(1024)(128)(2,1)S(1)}, f32[2,512,768]{2,1,0:T(8,128)S(1)}) fusion(f32[2,512,768]{2,1,0:T(8,128)S(1)} %copy-done.8, f32[2,512]{1,0:T(2,128)S(1)} %add_rsqrt_fusion.4, f32[2,512]{1,0:T(2,128)S(1)} %broadcast_multiply_fusion.10, ...), kind=kOutput, calls=%fused_computation.38 | convolution fusion | flops 4864077824 | bytes 23634944 | tf_op jit(solution)/shard_map/bsf,df->bsd/dot_general | solution.py:1033
  659.1 29.3 %attend_back.1 = bf16[3,2,512,768]{3,2,1,0:T(8,128)(2,1)} custom-call(s32[2]{0:T(128)} %lengths.5, bf16[2,512,2304]{2,1,0:T(8,128)(2,1)} %add_convert_fusion.1.q_ref.k_ref.v_ref, bf16[2,512,2304]{2,1,0:T(8,128)(2,1)} %add_convert_fusion.1.q_ref.k_ref.v_ref, bf16[2,512,2304]{2,1,0:T(8,128)(2,1)} %add_convert_fusion.1.q_ref.k_ref.v_ref, ...), custom_call_target="tpu_custom_call" | custom-call | flops 4026531840 | bytes 11010048 | tf_op jit(solution)/shard_map/attend_back/pallas_call | solution.py:1010
  693.9 8.1 multiply_reduce_fusion.2
  744.9 122.1 %reduce_weights.1 = f32[2,160,768]{2,1,0:T(8,128)} custom-call(bf16[4,8,2,160,768]{4,3,2,1,0:T(8,128)(2,1)} %bitcast.82.g), custom_call_target="tpu_custom_call" | custom-call | tf_op jit(solution)/shard_map/reduce_weights/pallas_call | solution.py:573
  869.1 75.5 %fold_table.1 = (f32[2,480,768]{2,1,0:T(8,128)}, f32[1,768]{1,0:T(1,128)}) custom-call(s32[4,1,2048]{2,1,0:T(1,128)} %reshape_reshape.3.ids, bf16[8192,768]{1,0:T(8,128)(2,1)} %bitcast.257, f32[4,2,480,768]{3,2,1,0:T(8,128)} %bitcast.258), custom_call_target="tpu_custom_call" | custom-call | tf_op jit(solution)/shard_map/fold_table/pallas_call | solution.py:683
  948.0 9.9 %total.1 = f32[8,128]{1,0:T(8,128)} custom-call(f32[8,128]{1,0:T(8,128)} %broadcast_in_dim.176.x), custom_call_target="tpu_custom_call" | custom-call | tf_op jit(solution)/shard_map/total/pallas_call | solution.py:764
  970.3 8.0 multiply_add_fusion.7
  (415 shorter events, 200.4 us)
Async XLA Ops:
  8.0 230.5 %all-gather.12.cloned.1.call-start = ((), (), s32[]{:S(2)}) async-start(), calls=%async_computation.9 | async-start | bytes 16220160 | tf_op jit(solution)/shard_map/all_gather | solution.py:1371
  11.3 52.8 %copy-start.84 = (bf16[16,24]{1,0:T(8,128)(2,1)S(1)}, bf16[16,24]{1,0:T(8,128)(2,1)}, u32[]{:S(2)}) copy-start(bf16[16,24]{1,0:T(8,128)(2,1)} %param.50) | copy-start | bytes 2308
  11.3 52.9 %copy-start.63 = (bf16[24,2304]{1,0:T(8,128)(2,1)S(1)}, bf16[24,2304]{1,0:T(8,128)(2,1)}, u32[]{:S(2)}) copy-start(bf16[24,2304]{1,0:T(8,128)(2,1)} %param.46) | copy-start | bytes 331780
  11.3 53.0 %copy-start.70 = (bf16[24,768]{1,0:T(8,128)(2,1)S(1)}, bf16[24,768]{1,0:T(8,128)(2,1)}, u32[]{:S(2)}) copy-start(bf16[24,768]{1,0:T(8,128)(2,1)} %param.47) | copy-start | bytes 110596
  11.3 53.0 %copy-start.61 = (bf16[24,3072]{1,0:T(8,128)(2,1)S(1)}, bf16[24,3072]{1,0:T(8,128)(2,1)}, u32[]{:S(2)}) copy-start(bf16[24,3072]{1,0:T(8,128)(2,1)} %param.48) | copy-start | bytes 442372
  11.3 53.0 %copy-start.62 = (bf16[96,768]{1,0:T(8,128)(2,1)S(1)}, bf16[96,768]{1,0:T(8,128)(2,1)}, u32[]{:S(2)}) copy-start(bf16[96,768]{1,0:T(8,128)(2,1)} %param.49) | copy-start | bytes 442372
  11.3 53.1 %copy-start.78 = (bf16[512,24]{0,1:T(8,128)(2,1)S(1)}, bf16[512,24]{0,1:T(8,128)(2,1)}, u32[]{:S(2)}) copy-start(bf16[512,24]{0,1:T(8,128)(2,1)} %param.51) | copy-start | bytes 73732
  11.3 54.0 %copy-start.80 = (s32[2]{0:T(128)S(1)}, s32[2]{0:T(128)}, u32[]{:S(2)}) copy-start(s32[2]{0:T(128)} %lengths.5) | copy-start | bytes 28
  11.3 54.0 %copy-start.86 = (s32[2,512]{1,0:T(2,128)S(1)}, s32[2,512]{1,0:T(2,128)}, u32[]{:S(2)}) copy-start(s32[2,512]{1,0:T(2,128)} %param.33) | copy-start | bytes 12292
  11.3 54.0 %copy-start.87 = (s32[2,64]{1,0:T(2,128)S(1)}, s32[2,64]{1,0:T(2,128)}, u32[]{:S(2)}) copy-start(s32[2,64]{1,0:T(2,128)} %param.37) | copy-start | bytes 1540
  65.2 300.5 %reduce-scatter.4.cloned.1.call-start = ((), (), s32[]{:S(2)}) async-start(), calls=%async_computation.3 | async-start | bytes 14155776 | tf_op jit(solution)/shard_map/reduce_scatter | solution.py:1376
  75.8 40.7 %copy-start.52 = (s32[16,640]{1,0:T(8,128)}, s32[16,640]{1,0:T(8,128)S(1)}, u32[]{:S(2)}) copy-start(s32[16,640]{1,0:T(8,128)S(1)} %reshape.679) | copy-start | bytes 122884
  116.5 321.9 %reduce-scatter.6.cloned.1.call-start = ((), (), s32[]{:S(2)}) async-start(), calls=%async_computation.4 | async-start | bytes 14155776 | tf_op jit(solution)/shard_map/reduce_scatter | solution.py:1386
  238.6 269.5 %all-gather.6.cloned.1.call-start = ((), (), s32[]{:S(2)}) async-start(), calls=%async_computation.5 | async-start | bytes 1769472 | tf_op jit(solution)/shard_map/all_gather | solution.py:1402
  363.2 33.5 %copy-start.5 = (f32[512,768]{1,0:T(8,128)}, f32[512,768]{1,0:T(8,128)S(1)}, u32[]{:S(2)}) copy-start(f32[512,768]{1,0:T(8,128)S(1)} %copy.209) | copy-start | bytes 4718596
  365.6 31.1 %copy-start.64 = (f32[768]{0:T(1024)}, f32[768]{0:T(1024)S(1)}, u32[]{:S(2)}) copy-start(f32[768]{0:T(1024)S(1)} %get-tuple-element.307) | copy-start | bytes 9220
  365.6 31.1 %copy-start.66 = (f32[768]{0:T(1024)}, f32[768]{0:T(1024)S(1)}, u32[]{:S(2)}) copy-start(f32[768]{0:T(1024)S(1)} %get-tuple-element.308) | copy-start | bytes 9220
  365.6 31.1 %copy-start.71 = (f32[768]{0:T(1024)}, f32[768]{0:T(1024)S(1)}, u32[]{:S(2)}) copy-start(f32[768]{0:T(1024)S(1)} %get-tuple-element.306) | copy-start | bytes 9220
  368.1 28.7 %copy-start.68 = (f32[2,512]{1,0:T(2,128)}, f32[2,512]{1,0:T(2,128)S(1)}, u32[]{:S(2)}) copy-start(f32[2,512]{1,0:T(2,128)S(1)} %broadcast_multiply_fusion.11) | copy-start | bytes 12292
  453.9 74.9 %all-gather.8.cloned.1.call-start = ((), (), s32[]{:S(2)}) async-start(), calls=%async_computation.6 | async-start | bytes 1769472 | tf_op jit(solution)/shard_map/all_gather | solution.py:1406
  504.8 118.0 %reduce-scatter.8.cloned.1.call-start = ((), (), s32[]{:S(2)}) async-start(), calls=%async_computation.7 | async-start | bytes 1769472 | tf_op jit(solution)/shard_map/reduce_scatter | solution.py:1249
  588.1 281.0 %all-gather.10.cloned.1.call-start = ((), (), s32[]{:S(2)}) async-start(), calls=%async_computation.8 | async-start | bytes 14155776 | tf_op jit(solution)/shard_map/all_gather | solution.py:1450
  869.1 99.2 %copy-start.31 = (f32[96,768]{1,0:T(8,128)S(1)}, f32[96,768]{1,0:T(8,128)}, u32[]{:S(2)}) copy-start(f32[96,768]{1,0:T(8,128)} %param.42) | copy-start | bytes 884740
  869.1 99.2 %copy-start.54 = (f32[96,768]{1,0:T(8,128)S(1)}, f32[96,768]{1,0:T(8,128)}, u32[]{:S(2)}) copy-start(f32[96,768]{1,0:T(8,128)} %param.63) | copy-start | bytes 884740
  (80 other events, 452.0 us)
Sparse Core Ops, SparseCore 0:
  65.3 163.3 all-gather.11
Sparse Core Ops, SparseCore 1:
  116.6 182.4 reduce-scatter.3
  301.2 137.2 reduce-scatter.5
  454.0 23.9 all-gather.5
  504.9 23.9 all-gather.7
  588.2 34.6 reduce-scatter.7
  705.6 120.1 all-gather.9

commit v5 on v4

--- a/solution.py
+++ b/solution.py
@@ -51,16 +51,33 @@
     return index + bit - 2 * bit * (lax.div(index, bit) % 2)
 
 
-def spread_body(dp, count, *refs):
+def spread_body(dp, count, groups, *refs):
     blocks, outs = refs[:count], refs[count : 2 * count]
-    local, send, recv = refs[2 * count :]
+    local, send, recv = refs[2 * count : 2 * count + 3]
+    extra = refs[2 * count + 3 :]
+    shared = []
+    friends = []
+    if groups:
+        spot = lax.axis_index("fsdp")
+        friends = [{"fsdp": lax.rem(spot + hop, groups)} for hop in range(1, groups)]
+
+    def share_info():
+        if groups:
+            note, notes, note_send, note_recv = extra
+            for hop, friend in enumerate(friends):
+                shared.append(
+                    push(note, notes.at[spot], note_send.at[hop], note_recv.at[hop], friend)
+                )
+            notes[spot] = note[...]
+
     me = lax.axis_index("dp")
     own = [pltpu.make_async_copy(blocks[k], outs[k].at[me], local.at[k]) for k in range(count)]
     for copy in own:
         copy.start()
     if dp == 4:
         near = [flipped(me, 1), flipped(me, 2)]
-        greet([{"dp": near[0]}, {"dp": near[1]}])
+        greet([{"dp": near[0]}, {"dp": near[1]}] + friends)
+        share_info()
         first = []
         for k in range(count):
             for step in range(2):
@@ -96,7 +113,8 @@
             copy.wait_send()
     else:
         peers = [lax.rem(me + hop, dp) for hop in range(1, dp)]
-        greet([{"dp": peer} for peer in peers])
+        greet([{"dp": peer} for peer in peers] + friends)
+        share_info()
         sent = []
         for k in range(count):
             for hop, peer in enumerate(peers):
@@ -113,26 +131,57 @@
             copy.wait()
     for copy in own:
         copy.wait()
-
-
-def spread_dp(blocks, dp, identity):
+    for copy in shared:
+        copy.wait()
+
+
+def spread_dp(blocks, dp, identity, info=None, groups=0):
     count = len(blocks)
     rows, width = blocks[0].shape
     cut = [block.reshape(2, rows // 2, width) for block in blocks]
+    anywhere = pl.BlockSpec(memory_space=pl.ANY)
+    vmem = pl.BlockSpec(memory_space=pltpu.VMEM)
+    dma = pltpu.SemaphoreType.DMA
+    out_shape = [jax.ShapeDtypeStruct((dp, 2, rows // 2, width), LOW)] * count
+    in_specs, out_specs = [anywhere] * count, [anywhere] * count
+    scratch = [
+        dma((count,)),
+        dma((count, max(3, dp - 1), 2)),
+        dma((count, max(3, dp - 1), 2)),
+    ]
+    body = functools.partial(spread_body, dp, count, 0)
+    if info is not None:
+        cut.append(info)
+        in_specs.append(vmem)
+        out_shape.append(jax.ShapeDtypeStruct((groups,) + info.shape, info.dtype))
+        out_specs.append(vmem)
+        scratch += [dma((groups - 1,)), dma((groups - 1,))]
+
+        def body(*refs):
+            size = count + 1
+            ins, outs, rest = refs[:size], refs[size : 2 * size], refs[2 * size :]
+            spread_body(
+                dp,
+                count,
+                groups,
+                *ins[:count],
+                *outs[:count],
+                *rest[:3],
+                ins[count],
+                outs[count],
+                *rest[3:],
+            )
+
     outs = pl.pallas_call(
-        functools.partial(spread_body, dp, count),
-        out_shape=[jax.ShapeDtypeStruct((dp, 2, rows // 2, width), LOW)] * count,
-        in_specs=[pl.BlockSpec(memory_space=pl.ANY)] * count,
-        out_specs=[pl.BlockSpec(memory_space=pl.ANY)] * count,
-        scratch_shapes=[
-            pltpu.SemaphoreType.DMA((count,)),
-            pltpu.SemaphoreType.DMA((count, max(3, dp - 1), 2)),
-            pltpu.SemaphoreType.DMA((count, max(3, dp - 1), 2)),
-        ],
+        body,
+        out_shape=out_shape,
+        in_specs=in_specs,
+        out_specs=out_specs,
+        scratch_shapes=scratch,
         compiler_params=pltpu.CompilerParams(collective_id=identity, has_side_effects=True),
         name="spread_tables",
     )(*cut)
-    return [out.reshape(dp * rows, width) for out in outs]
+    return [out.reshape(dp * rows, width) for out in outs[:count]] + list(outs[count:])
 
 
 def ways_of(me, dp):
@@ -324,14 +373,14 @@
 
 def gather_weights(blocks, dp, groups, identity):
     count = len(blocks)
-    rows, width = blocks[0].shape
+    width = blocks[0].shape[1]
     n = groups // 2
-    cut = [block.reshape(2, rows // 2, width) for block in blocks]
+    cut = [block.reshape(2, block.shape[0] // 2, width) for block in blocks]
     ways = 2 if dp == 4 else dp - 1
     dma = pltpu.SemaphoreType.DMA
     outs = pl.pallas_call(
         functools.partial(gather_body, dp, n, count),
-        out_shape=[jax.ShapeDtypeStruct((dp, groups, 2, rows // 2, width), LOW)] * count,
+        out_shape=[jax.ShapeDtypeStruct((dp, groups) + block.shape, LOW) for block in cut],
         in_specs=[pl.BlockSpec(memory_space=pl.ANY)] * count,
         out_specs=[pl.BlockSpec(memory_space=pl.ANY)] * count,
         scratch_shapes=[
@@ -348,7 +397,7 @@
         compiler_params=pltpu.CompilerParams(collective_id=identity, has_side_effects=True),
         name="gather_weights",
     )(*cut)
-    return [out.reshape(dp * groups, rows, width) for out in outs]
+    return [out.reshape(dp * groups, -1, width) for out in outs]
 
 
 def dot_over(left, right, left_dim, right_dim):
@@ -364,8 +413,8 @@
     return total
 
 
-def reduce_body(dp, n, g, out, core, far, near, last, right, left, core_sem, far_sem, near_sem,
-                last_sem, line_sem):
+def reduce_body(dp, n, pieces, g, out, core, far, near, last, right, left, core_sem, far_sem,
+                near_sem, last_sem, line_sem):
     me = lax.axis_index("fsdp")
     row = lax.axis_index("dp")
     p = lax.div(me, 2)
@@ -377,6 +426,7 @@
     order = []
     for k in range((n + 1) // 2):
         order += [n - 1 - k] + ([k] if k != n - 1 - k else [])
+    turns = [(i, q) for i in range(pieces) for q in order]
 
     def hello(where):
         pl.semaphore_signal(barrier, inc=1, device_id=where, device_id_type=pl.DeviceIdType.MESH)
@@ -411,104 +461,105 @@
             device_id_type=pl.DeviceIdType.MESH,
         )
 
-    def core_copy(j, q, half):
+    def core_copy(j, q, i, half):
         return remote(
-            g.at[j, 2 * q + 1 - c, half],
-            core.at[j, q, half],
+            g.at[j, 2 * q + 1 - c, i, half],
+            core.at[j, q, i, half],
             core_sem,
-            (j, q, half),
+            (j, q, i, half),
             {"fsdp": partner},
         )
 
-    def far_copy(q, w):
+    def far_copy(q, i, w):
         return remote(
-            core.at[opposite, q, w], far.at[q, w], far_sem, (q, w), {"dp": ways[w]}
+            core.at[opposite, q, i, w], far.at[q, i, w], far_sem, (q, i, w), {"dp": ways[w]}
         )
 
-    def near_copy(q, w):
+    def near_copy(q, i, w):
         return remote(
-            core.at[ways[w], q, w], near.at[q, w], near_sem, (q, w, 0), {"dp": ways[w]}
+            core.at[ways[w], q, i, w], near.at[q, i, w], near_sem, (q, i, w, 0), {"dp": ways[w]}
         )
 
-    def last_copy(q, w):
+    def last_copy(q, i, w):
         return remote(
-            far.at[q, w], last.at[q, w], last_sem, (q, w), {"dp": ways[1 - w]}
+            far.at[q, i, w], last.at[q, i, w], last_sem, (q, i, w), {"dp": ways[1 - w]}
         )
 
-    def direct_copy(hop, q, half):
+    def direct_copy(hop, q, i, half):
         return remote(
-            core.at[ways[hop], q, half],
-            near.at[hop, q, half],
+            core.at[ways[hop], q, i, half],
+            near.at[hop, q, i, half],
             near_sem,
-            (q, half, hop),
+            (q, i, half, hop),
             {"dp": ways[hop]},
         )
 
-    def line_copy(buffer, q, side):
+    def line_copy(buffer, q, i, side):
         return remote(
-            buffer.at[q], buffer.at[q], line_sem, (q, side), {"fsdp": me + 2 - 4 * side}
+            buffer.at[q, i], buffer.at[q, i], line_sem, (q, i, side), {"fsdp": me + 2 - 4 * side}
         )
 
-    for q in order:
+    for i, q in turns:
         for j in [opposite, *ways, row] if dp == 4 else range(dp):
             for half in range(2):
-                core_copy(j, q, half).start()
-
-    def pair(j, q, half):
-        core_copy(j, q, half).wait_recv()
-        core[j, q, half] = added(core[j, q, half], g[j, 2 * q + c, half]).astype(LOW)
-
-    for q in order:
+                core_copy(j, q, i, half).start()
+
+    def pair(j, q, i, half):
+        core_copy(j, q, i, half).wait_recv()
+        core[j, q, i, half] = added(core[j, q, i, half], g[j, 2 * q + c, i, half]).astype(LOW)
+
+    for i, q in turns:
         if dp == 4:
             for w in range(2):
-                pair(opposite, q, w)
-                far_copy(q, w).start()
+                pair(opposite, q, i, w)
+                far_copy(q, i, w).start()
             for w in range(2):
-                pair(ways[w], q, w)
-                near_copy(q, w).start()
+                pair(ways[w], q, i, w)
+                near_copy(q, i, w).start()
             for w in range(2):
-                pair(ways[w], q, 1 - w)
-                pair(row, q, w)
+                pair(ways[w], q, i, 1 - w)
+                pair(row, q, i, w)
         else:
             for half in range(2):
                 for j in range(dp):
-                    pair(j, q, half)
+                    pair(j, q, i, half)
                 for hop in range(dp - 1):
-                    direct_copy(hop, q, half).start()
-    if dp == 4:
-        for q in order:
+                    direct_copy(hop, q, i, half).start()
+
+    def relay(i, q):
+        if dp == 4:
             for w in range(2):
-                far_copy(q, w).wait_recv()
-                far[q, w] = added(far[q, w], core[ways[1 - w], q, w]).astype(LOW)
-                last_copy(q, w).start()
-
-    def total(q, half):
+                far_copy(q, i, w).wait_recv()
+                far[q, i, w] = added(far[q, i, w], core[ways[1 - w], q, i, w]).astype(LOW)
+                last_copy(q, i, w).start()
+
+    def total(q, i, half):
         if dp == 4:
-            near_copy(q, half).wait_recv()
-            last_copy(q, half).wait_recv()
-            return added(core[row, q, half], near[q, half], last[q, half])
-        parts = [core[row, q, half]]
+            near_copy(q, i, half).wait_recv()
+            last_copy(q, i, half).wait_recv()
+            return added(core[row, q, i, half], near[q, i, half], last[q, i, half])
+        parts = [core[row, q, i, half]]
         for hop in range(dp - 1):
-            direct_copy(hop, q, half).wait_recv()
-            parts.append(near[hop, q, half])
+            direct_copy(hop, q, i, half).wait_recv()
+            parts.append(near[hop, q, i, half])
         return added(*parts)
 
-    for q in order:
-        sums = [total(q, half) for half in range(2)]
+    def line_up(i, q):
+        sums = [total(q, i, half) for half in range(2)]
 
         def store(buffer, side, first):
             for half in range(2):
                 if first:
-                    buffer[q, half] = sums[half].astype(LOW)
+                    buffer[q, i, half] = sums[half].astype(LOW)
                 else:
-                    buffer[q, half] = added(sums[half], buffer[q, half]).astype(LOW)
-            line_copy(buffer, q, side).start()
+                    buffer[q, i, half] = added(sums[half], buffer[q, i, half]).astype(LOW)
+            line_copy(buffer, q, i, side).start()
 
         if q > 0:
 
             @pl.when((p > 0) & (p < q))
             def _():
-                line_copy(right, q, 0).wait_recv()
+                line_copy(right, q, i, 0).wait_recv()
                 store(right, 0, False)
 
             @pl.when((p == 0) & (p < q))
@@ -519,7 +570,7 @@
 
             @pl.when((p < n - 1) & (p > q))
             def _():
-                line_copy(left, q, 1).wait_recv()
+                line_copy(left, q, i, 1).wait_recv()
                 store(left, 1, False)
 
             @pl.when((p == n - 1) & (p > q))
@@ -529,64 +580,72 @@
         @pl.when(p == q)
         def _():
             for half in range(2):
-                out[half] = sums[half]
+                out[i, half] = sums[half]
+
+    for k in range(len(turns) + n):
+        if k < len(turns):
+            relay(*turns[k])
+        if k >= n:
+            line_up(*turns[k - n])
 
     @pl.when(p > 0)
     def _():
-        line_copy(right, p, 0).wait_recv()
-        out[...] = added(out[...], right[p])
+        for i in range(pieces):
+            line_copy(right, p, i, 0).wait_recv()
+            out[i] = added(out[i], right[p, i])
 
     @pl.when(p < n - 1)
     def _():
-        line_copy(left, p, 1).wait_recv()
-        out[...] = added(out[...], left[p])
-
-    for q in order:
+        for i in range(pieces):
+            line_copy(left, p, i, 1).wait_recv()
+            out[i] = added(out[i], left[p, i])
+
+    for i, q in turns:
         for half in range(2):
             for j in range(dp):
-                core_copy(j, q, half).wait_send()
+                core_copy(j, q, i, half).wait_send()
             if dp == 4:
-                far_copy(q, half).wait_send()
-                near_copy(q, half).wait_send()
-                last_copy(q, half).wait_send()
+                far_copy(q, i, half).wait_send()
+                near_copy(q, i, half).wait_send()
+                last_copy(q, i, half).wait_send()
             else:
                 for hop in range(dp - 1):
-                    direct_copy(hop, q, half).wait_send()
+                    direct_copy(hop, q, i, half).wait_send()
 
         @pl.when(p < q)
         def _():
-            line_copy(right, q, 0).wait_send()
+            line_copy(right, q, i, 0).wait_send()
 
         @pl.when(p > q)
         def _():
-            line_copy(left, q, 1).wait_send()
-
-
-def reduce_weights(g, dp, groups, identity):
+            line_copy(left, q, i, 1).wait_send()
+
+
+def reduce_weights(g, dp, groups, pieces, identity):
     devices, rows, width = g.shape
     n = groups // 2
-    half = rows // 2
-    g = g.reshape(dp, groups, 2, half, width)
+    half = rows // (2 * pieces)
+    g = g.reshape(dp, groups, pieces, 2, half, width)
     dma = pltpu.SemaphoreType.DMA
-    block = pltpu.VMEM((n, 2, half, width), LOW)
-    near = block if dp == 4 else pltpu.VMEM((dp - 1, n, 2, half, width), LOW)
+    block = pltpu.VMEM((n, pieces, 2, half, width), LOW)
+    near = block if dp == 4 else pltpu.VMEM((dp - 1, n, pieces, 2, half, width), LOW)
     out = pl.pallas_call(
-        functools.partial(reduce_body, dp, n),
-        out_shape=jax.ShapeDtypeStruct((2, half, width), jnp.float32),
+        functools.partial(reduce_body, dp, n, pieces),
+        out_shape=jax.ShapeDtypeStruct((pieces, 2, half, width), jnp.float32),
         in_specs=[pl.BlockSpec(memory_space=pltpu.VMEM)],
         out_specs=pl.BlockSpec(memory_space=pltpu.VMEM),
         scratch_shapes=[
-            pltpu.VMEM((dp, n, 2, half, width), LOW),
+            pltpu.VMEM((dp, n, pieces, 2, half, width), LOW),
             block,
             near,
             block,
             block,
             block,
-            dma((2, dp, n, 2)),
-            dma((2, n, 2)),
-            dma((2, n, 2, max(1, dp - 1))),
-            dma((2, n, 2)),
-            dma((2, n, 2)),
+            dma((2, dp, n, pieces, 2)),
+            dma((2, n, pieces, 2)),
+            dma((2, n, pieces, 2, max(1, dp - 1))),
+            dma((2, n, pieces, 2)),
+            dma((2, n, pieces, 2)),
         ],
         compiler_params=pltpu.CompilerParams(
             collective_id=identity, has_side_effects=True, vmem_limit_bytes=56 * MIB
@@ -930,8 +989,8 @@
         parts = []
         for head in range(2):
             mine = low_lane if head == 0 else jnp.logical_not(low_lane)
-            scores = dot_over(k, jnp.where(mine, q, jnp.zeros_like(q)), 1, 1)
-            scores = jnp.where(keep, scores * 0.125, NEGATIVE)
+            scores = dot_over(k, jnp.where(mine, q * 0.125, jnp.zeros_like(q)), 1, 1)
+            scores = jnp.where(keep, scores, NEGATIVE)
             exponent = jnp.exp(scores - jnp.max(scores, axis=0, keepdims=True))
             scale = 1.0 / jnp.sum(exponent, axis=0, keepdims=True)
             parts.append(dot_over((exponent * scale).astype(LOW), v, 0, 0))
@@ -977,8 +1036,8 @@
         parts = []
         for head in range(2):
             mine = low_lane if head == 0 else jnp.logical_not(low_lane)
-            scores = dot_over(k, jnp.where(mine, q, jnp.zeros_like(q)), 1, 1)
-            scores = jnp.where(keep, scores * 0.125, NEGATIVE)
+            scores = dot_over(k, jnp.where(mine, q * 0.125, jnp.zeros_like(q)), 1, 1)
+            scores = jnp.where(keep, scores, NEGATIVE)
             exponent = jnp.exp(scores - jnp.max(scores, axis=0, keepdims=True))
             probs = exponent * (1.0 / jnp.sum(exponent, axis=0, keepdims=True))
             d_probs = dot_over(v, jnp.where(mine, d, jnp.zeros_like(d)), 1, 1)
@@ -1072,36 +1131,63 @@
     return (jnp.arange(labels)[None, :] < needed[:, None]).astype(jnp.float32)
 
 
-def pack_layer(weights, extra):
-    w_qkv, w_out, w_up, w_down, small, position = (w.astype(LOW) for w in weights)
-    rows, width = w_out.shape
-    pieces = [w_qkv[:, k * width : (k + 1) * width] for k in range(3)]
-    pieces += [w_out]
-    pieces += [w_up[:, k * width : (k + 1) * width] for k in range(w_up.shape[1] // width)]
-    pieces += [w_down]
-    rest = [position.T, small.T] + ([] if extra is None else [extra])
-    rest = jnp.concatenate(rest, axis=1)
-    pieces += [jnp.pad(rest, ((0, 0), (0, width - rest.shape[1])))]
-    packed = jnp.concatenate(pieces, axis=0)
-    return jnp.pad(packed, ((0, -packed.shape[0] % 32), (0, 0)))
-
-
-def unpack_layer(packed, span, slots):
+def pack_body(*refs):
+    out = refs[-1]
+    width = out.shape[1]
+    first = 0
+    for ref in refs[:-1]:
+        rows = ref.shape[0]
+        for k in range(ref.shape[1] // width):
+            piece = ref[:, k * width : (k + 1) * width]
+            out[first : first + rows, :] = piece.astype(LOW)
+            first += rows
+    if first < out.shape[0]:
+        out[first:, :] = jnp.zeros((out.shape[0] - first, width), LOW)
+
+
+def pack_rows(arrays, width):
+    filled = sum(array.size // width for array in arrays)
+    padded = filled + -filled % 32
+    if any(array.shape[0] % 16 for array in arrays) and arrays[0].shape[0] % 8:
+        pieces = []
+        for array in arrays:
+            for k in range(array.shape[1] // width):
+                pieces.append(array[:, k * width : (k + 1) * width].astype(LOW))
+        return jnp.pad(jnp.concatenate(pieces, axis=0), ((0, padded - filled), (0, 0)))
+    vmem = pl.BlockSpec(memory_space=pltpu.VMEM)
+    return pl.pallas_call(
+        pack_body,
+        in_specs=[vmem] * len(arrays),
+        out_specs=vmem,
+        out_shape=jax.ShapeDtypeStruct((padded, width), LOW),
+        name="pack_rows",
+    )(*arrays)
+
+
+def pack_rest(small, position, extra, width):
+    rest = [position.astype(LOW).T, small.astype(LOW).T]
+    rest = jnp.concatenate(rest + ([] if extra is None else [extra]), axis=1)
+    return jnp.pad(rest, ((0, 0), (0, width - rest.shape[1])))
+
+
+def unpack_rows(packed, layout):
     devices, _, width = packed.shape
-    rows = width // devices
-    ff = 4 * width
-
-    def part(first, count):
-        return packed[:, first : first + count].reshape(devices * count, width)
-
-    w_qkv = jnp.concatenate([part(k * rows, rows) for k in range(3)], axis=1)
-    w_out = part(3 * rows, rows)
-    w_up = jnp.concatenate([part((4 + k) * rows, rows) for k in range(4)], axis=1)
-    w_down = part(8 * rows, ff // devices)
-    rest = part(8 * rows + ff // devices, rows)
+    parts = []
+    first = 0
+    for rows, count in layout:
+        pieces = []
+        for k in range(count):
+            piece = packed[:, first : first + rows].reshape(devices * rows, width)
+            pieces.append(piece)
+            first += rows
+        parts.append(pieces[0] if count == 1 else jnp.concatenate(pieces, axis=1))
+    return parts
+
+
+def unpack_rest(rest, span, slots):
     position = rest[:, :span].T.astype(jnp.float32)
     small = rest[:, span : span + slots].T.astype(jnp.float32)
-    return (w_qkv, w_out, w_up, w_down, small, position), rest[:, span + slots :]
+    return small, position, rest[:, span + slots :]
 
 
 def embed_forward(token_rows, weights, segment_ids):
@@ -1122,6 +1208,7 @@
     first_low = first.astype(LOW)
     upward = product_of("bsd,df->bsf", first_low, w_up) + small[3:7].reshape(-1)
     act, slope = gelu_parts(upward)
+    slope = slope.astype(LOW)
     act_low = act.astype(LOW)
     down = product_of("bsf,fd->bsd", act_low, w_down) + small[7]
     out, normed_second, inverse_second = layer_norm_keep(first + down, small[10], small[11])
@@ -1160,7 +1247,7 @@
     d_second, gain_second, shift_second = layer_norm_back(
         grad, normed_second, inverse_second, small[10]
     )
-    d_down = d_second.astype(LOW)
+    d_second, d_down = lax.optimization_barrier((d_second, d_second.astype(LOW)))
     d_up = (product_of("bsd,fd->bsf", d_down, w_down) * slope).astype(LOW)
     d_first = d_second + product_of("bsf,df->bsd", d_up, w_up)
     d_sum, gain_first, shift_first = layer_norm_back(d_first, normed_first, inverse_first, small[8])
@@ -1273,7 +1360,7 @@
     rest = jnp.pad(rest, ((0, width - rest.shape[0]), (0, 0))).T
     pieces += [shards(rest)]
     filled = 8 * rows + g_down.shape[0] // devices + rows
-    pad = -filled % 32
+    pad = -filled % 64
     if pad:
         pieces += [jnp.zeros((devices, pad, width), LOW)]
     return jnp.concatenate(pieces, axis=1)
@@ -1354,20 +1441,21 @@
         [tok_ids, label_ids, jnp.broadcast_to(seq_len[:, None], (micro, labels))], axis=1
     )
     info = jnp.pad(info, ((0, -micro % 8), (0, 0)))
-    info = share_small(info, groups, 7)[:, :micro].reshape(groups * micro, span + 2 * labels)
+    student_table, info = spread_dp(
+        [jnp.pad(table.astype(LOW), ((0, pad), (0, 0)))], dp, 1, info, groups
+    )
+    info = info[:, :micro].reshape(groups * micro, span + 2 * labels)
     ids_all = info[:, :span]
     targets_all = info[:, span : span + labels].reshape(-1)
     lengths_all = info[:, span + labels]
-    student_table = spread_dp([jnp.pad(table.astype(LOW), ((0, pad), (0, 0)))], dp, 1)[0]
     valid_local = label_valid(seq_len, labels, span)
     counts = jnp.stack([jnp.sum(valid_local), jnp.sum((seq_len > 0).astype(jnp.float32))])
     extra = jnp.broadcast_to(counts.astype(LOW)[None, :], (rows_own, 2))
 
     safe_ids = owned(ids_all, share, padded, groups, own)[1]
-    t_weights, student_table = lax.optimization_barrier(
-        ((t_qkv, t_out, t_up, t_down, t_small, t_position), student_table)
-    )
-    packed_teacher = pack_layer(t_weights, None)
+    packed_teacher = pack_rows(
+        (t_qkv, t_out, t_up, t_down, pack_rest(t_small, t_position, None, width)), width
+    )
     packed_teacher = lax.all_gather(packed_teacher, BOTH)
     safe_flat = safe_ids.reshape(-1)
     student_hits = student_table[safe_flat].reshape(groups * micro, span, width)
@@ -1384,8 +1472,27 @@
         ((w_qkv, w_out, w_up, w_down, small, position), teacher_hits, packed_teacher)
     )
     tokens_teacher = lax.psum_scatter(teacher_hits, "fsdp", scatter_dimension=0, tiled=True)
-    packed_student = gather_weights([pack_layer(s_weights, extra)], dp, groups, 5)[0]
-    weights, rest = unpack_layer(packed_student, span, slots)
+    packed_student = pack_rows(
+        s_weights[:2] + (pack_rest(s_weights[4], s_weights[5], extra, width),), width
+    )
+    packed_student, up_student, down_student = gather_weights(
+        [packed_student, pack_rows((s_weights[2],), width), pack_rows((s_weights[3],), width)],
+        dp,
+        groups,
+        5,
+    )
+    layout = (
+        (rows_own, 3),
+        (rows_own, 1),
+        (rows_own, 4),
+        (w_down.shape[0], 1),
+        (rows_own, 1),
+    )
+    full_qkv, full_out, rest = unpack_rows(packed_student, layout[:2] + layout[4:])
+    full_small, full_position, rest = unpack_rest(rest, span, slots)
+    full_up = unpack_rows(up_student, layout[2:3])[0]
+    full_down = down_student[:, : w_down.shape[0]].reshape(-1, width)
+    weights = (full_qkv, full_out, full_up, full_down, full_small, full_position)
     counted = jnp.sum(rest[::rows_own, :2].astype(jnp.float32), axis=0)
     label_count, count_seq = counted[0], counted[1]
 
@@ -1395,10 +1502,12 @@
     student_out, kept = layer_forward(start, weights, seq_len)
     pick = (label_pos[..., None] == jnp.arange(span)).astype(LOW)
     student_rows = label_rows(pick, student_out)
-    student_rows, tokens_teacher, packed_teacher = lax.optimization_barrier(
-        (student_rows, tokens_teacher, packed_teacher)
-    )
-    teacher, _ = unpack_layer(packed_teacher, span, slots)
+    student_rows, packed_teacher = lax.optimization_barrier((student_rows, packed_teacher))
+    *teacher, teacher_rest = unpack_rows(packed_teacher, layout)
+    teacher = tuple(teacher) + unpack_rest(teacher_rest, span, slots)[:2]
+    student_rows, teacher, tokens_teacher = lax.optimization_barrier(
+        (student_rows, teacher, tokens_teacher)
+    )
     student_rows = lax.all_gather(student_rows, "fsdp", axis=0, tiled=True)
     teacher_start = embed_forward(tokens_teacher.astype(jnp.float32), teacher, segments)[0]
     teacher_out = layer_forward(teacher_start, teacher, seq_len)[0]
@@ -1452,7 +1561,7 @@
         product_of("bsd,bsf->df", left, right) for left, right in factors
     ]
     packed_grads = pack_grads(*matrices, small_grad, position_grad, devices)
-    packed_grads = reduce_weights(packed_grads, dp, groups, 6)
+    packed_grads = reduce_weights(packed_grads, dp, groups, 2, 6)
     layer_squares = jnp.sum(packed_grads * packed_grads)
     table_grad, embed_grads, packed_grads, layer_squares = lax.optimization_barrier(
         (table_grad, embed_grads, packed_grads, layer_squares)

time: 995 us -> 945 us (0.950)
  Pallas kernels: 589 us -> 547 us
  local copies, waits for them, and re-layouts: 170 us -> 158 us
    pallas_call x1, Pallas kernels: 106 us -> 81.8 us  [gather_weights(): pl.pallas_call(functools.partial(gather_body, dp, n, count), out_shape=[j...]
    pallas_call x3 -> x7, Pallas kernels: 254 us -> 246 us  [the longest x2 124 us: spread_dp(): pl.pallas_call(body, out_shape=out_shape, in_specs=in_specs, out_specs=ou...]
    unnamed x227 -> x198, local copies, waits for them, and re-layouts: 39.2 us -> 34.9 us
  transfers between devices with their start and end apart: 7 -> 7, of which waited for: 3 -> 3; matrix products, arithmetic and copies ran while one was open for 23% -> 26% of each run, Pallas kernels for 37% -> 40%
where the time goes in v5:
time: 945 us; the launch traced here: 938 us
  Pallas kernels  547 us (58%)
  local copies, waits for them, and re-layouts  158 us (17%)
  matrix products  122 us (13%)
  other arithmetic  57.4 us (6%)
  waiting for transfers between devices  30.7 us (3%)
  between operations  22.5 us (2%)
    pallas_call x2, Pallas kernels, spread_dp(): pl.pallas_call(body, out_shape=out_shape, in_specs=in_specs, out_specs=ou...  124 us
    dot_general x20, matrix products, product_of(): return jnp.einsum(form, left, right, preferred_element_type=jnp.float32)  122 us
    pallas_call x1, Pallas kernels, reduce_weights(): pl.pallas_call(functools.partial(reduce_body, dp, n, pieces), out_shape=j...  115 us
    pallas_call x1, Pallas kernels, gather_weights(): pl.pallas_call(functools.partial(gather_body, dp, n, count), out_shape=[j...  81.8 us
    pallas_call x1, Pallas kernels, fold_dp(): pl.pallas_call(functools.partial(fold_body, dp, step, share), out_shape=[...  74.9 us
    gather x1, local copies, waits for them, and re-layouts, on_device(): student_hits = student_table[safe_flat].reshape(groups * micro, span, width)  42.2 us
    gather x1, local copies, waits for them, and re-layouts, on_device(): teacher_hits = teacher_table[safe_flat].reshape(groups * micro, span, width)  40.5 us
    pallas_call x2, Pallas kernels, attend(): pl.pallas_call(attend_body, grid_spec=pltpu.PrefetchScalarGridSpec(num_sc...  37.2 us
  transfers between devices with their start and end apart: 7, of which 3 were waited for; matrix products, arithmetic and copies ran while one was open for 26% of the time, Pallas kernels for 40%

profile of v5, /device:TPU:0, one launch (start us, length us, event | category | flops | bytes accessed | tf_op | source)
XLA Modules:
  0.0 937.6 jit_solution(3900510993826543826)
XLA Ops:
  16.1 74.5 %spread_tables.2 = (bf16[4,2,480,768]{3,2,1,0:T(8,128)(2,1)}, s32[8,8,640]{2,1,0:T(8,128)}) custom-call(bf16[2,480,768]{2,1,0:T(8,128)(2,1)} %bitcast.257, s32[8,640]{1,0:T(8,128)} %pad.25.refs_1_), custom_call_target="tpu_custom_call" | custom-call | tf_op jit(solution)/shard_map/spread_tables/pallas_call | solution.py:175
  91.8 42.2 %gather_fusion = bf16[8192,768]{1,0:T(8,128)(2,1)} fusion(bf16[3840,768]{1,0:T(8,128)(2,1)} %bitcast.243, s32[8192]{0:T(1024)S(1)} %broadcast_clamp_fusion), kind=kCustom, calls=%fused_computation | custom fusion | bytes 25198592 | tf_op jit(solution)/shard_map/gather | solution.py:1461
  136.6 49.8 %spread_tables.3 = bf16[4,2,480,768]{3,2,1,0:T(8,128)(2,1)} custom-call(bf16[2,480,768]{2,1,0:T(8,128)(2,1)} %bitcast.256), custom_call_target="tpu_custom_call" | custom-call | tf_op jit(solution)/shard_map/spread_tables/pallas_call | solution.py:175
  186.3 40.5 %gather_fusion.1 = bf16[8192,768]{1,0:T(8,128)(2,1)} fusion(bf16[3840,768]{1,0:T(8,128)(2,1)} %bitcast.241, s32[8192]{0:T(1024)S(1)} %broadcast_clamp_fusion), kind=kCustom, calls=%fused_computation.1 | custom fusion | bytes 25198592 | tf_op jit(solution)/shard_map/gather | solution.py:1470
  235.9 81.8 %gather_weights.1 = (bf16[4,8,2,64,768]{4,3,2,1,0:T(8,128)(2,1)}, bf16[4,8,2,48,768]{4,3,2,1,0:T(8,128)(2,1)}, bf16[4,8,2,48,768]{4,3,2,1,0:T(8,128)(2,1)}) custom-call(bf16[2,64,768]{2,1,0:T(8,128)(2,1)} %bitcast.309, bf16[2,48,768]{2,1,0:T(8,128)(2,1)} %bitcast.310, bf16[2,48,768]{2,1,0:T(8,128)(2,1)} %bitcast.311), custom_call_target="tpu_custom_call" | custom-call | tf_op jit(solution)/shard_map/gather_weights/pallas_call | solution.py:381
  338.6 18.6 %attend.2 = bf16[2,512,768]{2,1,0:T(8,128)(2,1)} custom-call(s32[2]{0:T(128)} %lengths.5, bf16[2,512,2304]{2,1,0:T(8,128)(2,1)} %add_convert_fusion.1.q_ref.k_ref.v_ref, bf16[2,512,2304]{2,1,0:T(8,128)(2,1)} %add_convert_fusion.1.q_ref.k_ref.v_ref, bf16[2,512,2304]{2,1,0:T(8,128)(2,1)} %add_convert_fusion.1.q_ref.k_ref.v_ref), custom_call_target="tpu_custom_call" | custom-call | flops 1610612736 | bytes 6291456 | tf_op jit(solution)/shard_map/attend/pallas_call | solution.py:1008
  363.3 11.2 %multiply_convert_fusion.2 = (bf16[2,512,3072]{2,1,0:T(8,128)(2,1)S(1)}, f32[2,512,3072]{2,1,0:T(8,128)}) fusion(f32[3072]{0:T(1024)S(1)} %add.500, bf16[2,512,768]{2,1,0:T(8,128)(2,1)S(1)} %fusion.16, bf16[768,768]{1,0:T(8,128)(2,1)S(1)} %bitcast.299, bf16[768,768]{1,0:T(8,128)(2,1)S(1)} %bitcast.301, bf16[768,768]{1,0:T(8,128)(2,1)S(1)} %bitcast.303, ...), kind=kOutput, calls=%fused_computation.10 | convolution fusion | flops 4869586944 | bytes 25178112 | tf_op jit(solution)/shard_map/bsd,df->bsf/dot_general | solution.py:1092
  415.0 18.6 %attend.3 = bf16[2,512,768]{2,1,0:T(8,128)(2,1)} custom-call(s32[2]{0:T(128)} %lengths.5, bf16[2,512,2304]{2,1,0:T(8,128)(2,1)} %add_convert_fusion.q_ref.k_ref.v_ref, bf16[2,512,2304]{2,1,0:T(8,128)(2,1)} %add_convert_fusion.q_ref.k_ref.v_ref, bf16[2,512,2304]{2,1,0:T(8,128)(2,1)} %add_convert_fusion.q_ref.k_ref.v_ref), custom_call_target="tpu_custom_call" | custom-call | flops 1610612736 | bytes 6291456 | tf_op jit(solution)/shard_map/attend/pallas_call | solution.py:1008
  461.2 15.2 %student_logits.1 = (f32[3840,1024]{1,0:T(8,128)}, f32[4,1024]{1,0:T(4,128)S(1)}) custom-call(bf16[1024,768]{1,0:T(8,128)(2,1)S(1)} %copy-done.3, bf16[3840,768]{1,0:T(8,128)(2,1)S(1)} %bitcast.245, s32[1,1024]{1,0:T(1,128)S(1)} %compare_select_fusion.4.target), custom_call_target="tpu_custom_call" | custom-call | flops 6039797760 | bytes 21626880 | tf_op jit(solution)/shard_map/student_logits/pallas_call | solution.py:905
  476.4 9.1 all-gather.8.cloned.1.call-done.rows
  489.6 18.9 %teacher_logits.1 = (f32[3840,1024]{1,0:T(8,128)}, f32[4,1024]{1,0:T(4,128)S(1)}) custom-call(bf16[1024,768]{1,0:T(8,128)(2,1)S(1)} %copy-done.2, bf16[3840,768]{1,0:T(8,128)(2,1)S(1)} %bitcast.242, f32[3840,1024]{1,0:T(8,128)} %get-tuple-element.91.student), custom_call_target="tpu_custom_call" | custom-call | flops 6039797760 | bytes 21626880 | tf_op jit(solution)/shard_map/teacher_logits/pallas_call | solution.py:905
  509.1 9.3 share_small.1
  520.5 24.0 %logits_back.1 = (bf16[3840,1024]{1,0:T(8,128)(2,1)}, bf16[1024,768]{1,0:T(8,128)(2,1)}) custom-call(f32[3840,1024]{1,0:T(8,128)} %get-tuple-element.91.student, f32[3840,1024]{1,0:T(8,128)} %get-tuple-element.99.teacher, bf16[3840,768]{1,0:T(8,128)(2,1)} %bitcast.244, f32[4,1024]{1,0:T(4,128)S(1)} %pad_maximum_fusion.6.consts, ...), custom_call_target="tpu_custom_call" | custom-call | flops 6039797760 | bytes 45219840 | tf_op jit(solution)/shard_map/logits_back/pallas_call | solution.py:961
  548.7 12.5 %fusion.124 = f32[3840,768]{1,0:T(8,128)} fusion(bf16[3840,1024]{1,0:T(8,128)(2,1)} %get-tuple-element.103, bf16[1024,768]{1,0:T(8,128)(2,1)S(1)} %copy-done.4), kind=kOutput, calls=%fused_computation.335 | convolution fusion | flops 6039797760 | bytes 21233664 | tf_op jit(solution)/shard_map/vp,pd->vd/dot_general | solution.py:1092
  561.2 18.0 %reduce-scatter.8.cloned.1.call-done = bf16[128,768]{1,0:T(8,128)(2,1)} async-done(((bf16[1024,768]{1,0:T(8,128)(2,1)}), bf16[128,768]{1,0:T(8,128)(2,1)}) %reduce-scatter.8.cloned.1.call-update) | async-done | bytes 196624 | tf_op jit(solution)/shard_map/reduce_scatter | solution.py:1336
  584.1 14.2 %fusion.123 = (bf16[3072]{0:T(1024)(128)(2,1)S(1)}, bf16[2,512,3072]{2,1,0:T(8,128)(2,1)}) fusion(f32[2,512,3072]{2,1,0:T(8,128)} %get-tuple-element.427, f32[3072]{0:T(1024)S(1)} %add.500, bf16[2,512,768]{2,1,0:T(8,128)(2,1)S(1)} %get-tuple-element.116, bf16[3072,768,1]{1,0,2:T(8,128)(2,1)S(1)} %bitcast.326), kind=kOutput, calls=%fused_computation.334 | convolution fusion | flops 4875875328 | bytes 25184256 | tf_op jit(solution)/shard_map/bsd,fd->bsf/dot_general | solution.py:1092
  598.3 8.8 multiply_reduce_fusion.4
  612.6 29.5 %attend_back.1 = bf16[3,2,512,768]{3,2,1,0:T(8,128)(2,1)} custom-call(s32[2]{0:T(128)} %lengths.5, bf16[2,512,2304]{2,1,0:T(8,128)(2,1)} %add_convert_fusion.1.q_ref.k_ref.v_ref, bf16[2,512,2304]{2,1,0:T(8,128)(2,1)} %add_convert_fusion.1.q_ref.k_ref.v_ref, bf16[2,512,2304]{2,1,0:T(8,128)(2,1)} %add_convert_fusion.1.q_ref.k_ref.v_ref, ...), custom_call_target="tpu_custom_call" | custom-call | flops 4026531840 | bytes 11010048 | tf_op jit(solution)/shard_map/attend_back/pallas_call | solution.py:1069
  647.5 8.1 multiply_reduce_fusion.2
  666.3 7.8 bitcast_convert_fusion.2
  701.0 115.1 %reduce_weights.1 = f32[2,2,80,768]{3,2,1,0:T(8,128)} custom-call(bf16[4,8,2,2,80,768]{5,4,3,2,1,0:T(8,128)(2,1)} %bitcast.85.g), custom_call_target="tpu_custom_call" | custom-call | tf_op jit(solution)/shard_map/reduce_weights/pallas_call | solution.py:632
  818.2 74.9 %fold_table.1 = (f32[2,480,768]{2,1,0:T(8,128)}, f32[1,768]{1,0:T(1,128)}) custom-call(s32[4,1,2048]{2,1,0:T(1,128)} %reshape_reshape.6.ids, bf16[8192,768]{1,0:T(8,128)(2,1)} %bitcast.250, f32[4,2,480,768]{3,2,1,0:T(8,128)} %bitcast.251), custom_call_target="tpu_custom_call" | custom-call | tf_op jit(solution)/shard_map/fold_table/pallas_call | solution.py:742
  896.4 9.9 %total.1 = f32[8,128]{1,0:T(8,128)} custom-call(f32[8,128]{1,0:T(8,128)} %broadcast_in_dim.176.x), custom_call_target="tpu_custom_call" | custom-call | tf_op jit(solution)/shard_map/total/pallas_call | solution.py:823
  918.8 8.0 multiply_add_fusion.7
  (388 shorter events, 194.7 us)
Async XLA Ops:
  8.1 218.8 %all-gather.12.cloned.1.call-start = ((), (), s32[]{:S(2)}) async-start(), calls=%async_computation.9 | async-start | bytes 16220160 | tf_op jit(solution)/shard_map/all_gather | solution.py:1459
  12.1 314.8 %reduce-scatter.4.cloned.1.call-start = ((), (), s32[]{:S(2)}) async-start(), calls=%async_computation.3 | async-start | bytes 14155776 | tf_op jit(solution)/shard_map/reduce_scatter | solution.py:1464
  91.6 42.4 %copy-start.46 = (s32[16,640]{1,0:T(8,128)}, s32[16,640]{1,0:T(8,128)S(1)}, u32[]{:S(2)}) copy-start(s32[16,640]{1,0:T(8,128)S(1)} %reshape.686) | copy-start | bytes 122884
  134.0 268.0 %reduce-scatter.6.cloned.1.call-start = ((), (), s32[]{:S(2)}) async-start(), calls=%async_computation.4 | async-start | bytes 14155776 | tf_op jit(solution)/shard_map/reduce_scatter | solution.py:1474
  226.9 230.2 %all-gather.6.cloned.1.call-start = ((), (), s32[]{:S(2)}) async-start(), calls=%async_computation.5 | async-start | bytes 1769472 | tf_op jit(solution)/shard_map/all_gather | solution.py:1511
  324.4 32.8 %copy-start.5 = (f32[512,768]{1,0:T(8,128)}, f32[512,768]{1,0:T(8,128)S(1)}, u32[]{:S(2)}) copy-start(f32[512,768]{1,0:T(8,128)S(1)} %copy.209) | copy-start | bytes 4718596
  326.9 30.4 %copy-start.54 = (f32[768]{0:T(1024)}, f32[768]{0:T(1024)S(1)}, u32[]{:S(2)}) copy-start(f32[768]{0:T(1024)S(1)} %get-tuple-element.321) | copy-start | bytes 9220
  326.9 30.4 %copy-start.56 = (f32[768]{0:T(1024)}, f32[768]{0:T(1024)S(1)}, u32[]{:S(2)}) copy-start(f32[768]{0:T(1024)S(1)} %get-tuple-element.322) | copy-start | bytes 9220
  326.9 30.4 %copy-start.60 = (f32[768]{0:T(1024)}, f32[768]{0:T(1024)S(1)}, u32[]{:S(2)}) copy-start(f32[768]{0:T(1024)S(1)} %get-tuple-element.320) | copy-start | bytes 9220
  329.3 28.0 %copy-start.58 = (f32[2,512]{1,0:T(2,128)}, f32[2,512]{1,0:T(2,128)S(1)}, u32[]{:S(2)}) copy-start(f32[2,512]{1,0:T(2,128)S(1)} %broadcast_multiply_fusion.11) | copy-start | bytes 12292
  330.3 26.9 %copy-start.62 = (f32[2,512]{1,0:T(2,128)}, f32[2,512]{1,0:T(2,128)S(1)}, u32[]{:S(2)}) copy-start(f32[2,512]{1,0:T(2,128)S(1)} %add_rsqrt_fusion.5) | copy-start | bytes 12292
  404.7 80.8 %all-gather.8.cloned.1.call-start = ((), (), s32[]{:S(2)}) async-start(), calls=%async_computation.6 | async-start | bytes 1769472 | tf_op jit(solution)/shard_map/all_gather | solution.py:1515
  453.8 125.5 %reduce-scatter.8.cloned.1.call-start = ((), (), s32[]{:S(2)}) async-start(), calls=%async_computation.7 | async-start | bytes 1769472 | tf_op jit(solution)/shard_map/reduce_scatter | solution.py:1336
  520.5 25.0 %copy-start.69 = (s32[2]{0:T(128)S(1)}, s32[2]{0:T(128)}, u32[]{:S(2)}) copy-start(s32[2]{0:T(128)} %lengths.5) | copy-start | bytes 28
  520.5 28.2 %copy-start.4 = (bf16[1024,768]{1,0:T(8,128)(2,1)S(1)}, bf16[1024,768]{1,0:T(8,128)(2,1)}, u32[]{:S(2)}) copy-start(bf16[1024,768]{1,0:T(8,128)(2,1)} %all-gather.6.cloned.1.call-done.rows) | copy-start | bytes 4718596
  544.5 273.7 %all-gather.10.cloned.1.call-start = ((), (), s32[]{:S(2)}) async-start(), calls=%async_computation.8 | async-start | bytes 14155776 | tf_op jit(solution)/shard_map/all_gather | solution.py:1559
  584.0 14.3 %copy-start.16 = (bf16[2,512,768]{2,1,0:T(8,128)(2,1)}, bf16[2,512,768]{2,1,0:T(8,128)(2,1)S(1)}, u32[]{:S(2)}) copy-start(bf16[2,512,768]{2,1,0:T(8,128)(2,1)S(1)} %get-tuple-element.116) | copy-start | bytes 4718596
  584.1 14.2 %copy-start.38 = (bf16[32,24,768]{2,1,0:T(8,128)(2,1)S(1)}, bf16[32,24,768]{2,1,0:T(8,128)(2,1)}, u32[]{:S(2)}) copy-start(bf16[32,24,768]{2,1,0:T(8,128)(2,1)} %copy-done.37) | copy-start | bytes 3538948
  584.1 14.2 %copy-start.40 = (bf16[32,24,768]{2,1,0:T(8,128)(2,1)S(1)}, bf16[32,24,768]{2,1,0:T(8,128)(2,1)}, u32[]{:S(2)}) copy-start(bf16[32,24,768]{2,1,0:T(8,128)(2,1)} %copy-done.39) | copy-start | bytes 3538948
  584.1 14.2 %copy-start.42 = (bf16[32,24,768]{2,1,0:T(8,128)(2,1)S(1)}, bf16[32,24,768]{2,1,0:T(8,128)(2,1)}, u32[]{:S(2)}) copy-start(bf16[32,24,768]{2,1,0:T(8,128)(2,1)} %copy-done.41) | copy-start | bytes 3538948
  818.2 98.5 %copy-start.43 = (f32[96,768]{1,0:T(8,128)S(1)}, f32[96,768]{1,0:T(8,128)}, u32[]{:S(2)}) copy-start(f32[96,768]{1,0:T(8,128)} %refs_0_.4) | copy-start | bytes 884740
  818.2 98.5 %copy-start.48 = (f32[96,768]{1,0:T(8,128)S(1)}, f32[96,768]{1,0:T(8,128)}, u32[]{:S(2)}) copy-start(f32[96,768]{1,0:T(8,128)} %param.63) | copy-start | bytes 884740
  893.1 25.7 %copy-start.15 = (f32[956,768]{1,0:T(8,128)S(1)}, f32[956,768]{1,0:T(8,128)}, u32[]{:S(2)}) copy-start(f32[956,768]{1,0:T(8,128)} %param.38) | copy-start | bytes 8810500
  910.6 16.3 %copy-start.64 = (f32[16,24]{1,0:T(8,128)}, f32[16,24]{1,0:T(8,128)S(1)}, u32[]{:S(2)}) copy-start(f32[16,24]{1,0:T(8,128)S(1)} %copy.227) | copy-start | bytes 4612
  (73 other events, 356.3 us)
Sparse Core Ops, SparseCore 0:
  12.5 130.2 all-gather.11
Sparse Core Ops, SparseCore 1:
  134.1 136.8 reduce-scatter.3
  273.2 128.8 reduce-scatter.5
  404.7 31.6 all-gather.5
  453.8 31.6 all-gather.7
  544.6 34.6 reduce-scatter.7
  659.2 120.6 all-gather.9

commit v6 on v5

--- a/solution.py
+++ b/solution.py
@@ -840,8 +840,7 @@
 def block_rows(ref_rows, share):
     block = pl.program_id(0)
     index = lax.broadcasted_iota(jnp.int32, (ref_rows, 1), 0)
-    real = index + lax.rem(block, 2) * ref_rows < share
-    return index + block * ref_rows, real
+    return index + block * ref_rows, index < share
 
 
 def student_logits_body(share, rows, table, target, logits, stats):
@@ -1298,13 +1297,12 @@
     mine = micro * labels
     inside, local_target = owned(targets, share, padded, groups, own)
     target = jnp.where(inside, local_target, -1)[None, :]
-    block = padded // 2
     student, student_stats = logits_call(
         functools.partial(student_logits_body, share),
         all_student,
         table_student,
         target,
-        block,
+        padded,
         "student_logits",
     )
     teacher, teacher_stats = logits_call(
@@ -1312,7 +1310,7 @@
         all_teacher,
         table_teacher,
         student,
-        block,
+        padded,
         "teacher_logits",
     )
     stats = share_small(jnp.concatenate([student_stats, teacher_stats]), groups, 8)
@@ -1332,7 +1330,7 @@
     divergence_loss = cross / sum_teacher - lse_teacher + lse_soft
     share_lab = valid_mask / count
     consts = jnp.stack([lse_plain, lse_soft, lse_teacher, share_lab])
-    d_logits, d_rows = logits_back(student, teacher, table_student, consts, target, block)
+    d_logits, d_rows = logits_back(student, teacher, table_student, consts, target, padded)
     d_rows = lax.psum_scatter(d_rows, "fsdp", scatter_dimension=0, tiled=True)
     table_term = product_of("vp,pd->vd", d_logits, all_student)
     d_rows, table_term = lax.optimization_barrier((d_rows, table_term))

time: 945 us -> 943 us (level)
  no operation moved by 1% of the time
where the time goes in v6:
time: 943 us; the launch traced here: 935 us
  Pallas kernels  543 us (58%)
  local copies, waits for them, and re-layouts  158 us (17%)
  matrix products  122 us (13%)
  other arithmetic  57.4 us (6%)
  waiting for transfers between devices  31.8 us (3%)
  between operations  22.5 us (2%)
    pallas_call x2, Pallas kernels, spread_dp(): pl.pallas_call(body, out_shape=out_shape, in_specs=in_specs, out_specs=ou...  124 us
    dot_general x20, matrix products, product_of(): return jnp.einsum(form, left, right, preferred_element_type=jnp.float32)  122 us
    pallas_call x1, Pallas kernels, reduce_weights(): pl.pallas_call(functools.partial(reduce_body, dp, n, pieces), out_shape=j...  115 us
    pallas_call x1, Pallas kernels, gather_weights(): pl.pallas_call(functools.partial(gather_body, dp, n, count), out_shape=[j...  81.8 us
    pallas_call x1, Pallas kernels, fold_dp(): pl.pallas_call(functools.partial(fold_body, dp, step, share), out_shape=[...  74.9 us
    gather x1, local copies, waits for them, and re-layouts, on_device(): student_hits = student_table[safe_flat].reshape(groups * micro, span, width)  42.2 us
    gather x1, local copies, waits for them, and re-layouts, on_device(): teacher_hits = teacher_table[safe_flat].reshape(groups * micro, span, width)  40.5 us
    pallas_call x2, Pallas kernels, attend(): pl.pallas_call(attend_body, grid_spec=pltpu.PrefetchScalarGridSpec(num_sc...  37.2 us
  transfers between devices with their start and end apart: 7, of which 3 were waited for; matrix products, arithmetic and copies ran while one was open for 26% of the time, Pallas kernels for 40%

profile of v6, /device:TPU:0, one launch (start us, length us, event | category | flops | bytes accessed | tf_op | source)
XLA Modules:
  0.0 934.9 jit_solution(6086654555232565620)
XLA Ops:
  16.1 74.5 %spread_tables.2 = (bf16[4,2,480,768]{3,2,1,0:T(8,128)(2,1)}, s32[8,8,640]{2,1,0:T(8,128)}) custom-call(bf16[2,480,768]{2,1,0:T(8,128)(2,1)} %bitcast.257, s32[8,640]{1,0:T(8,128)} %pad.25.refs_1_), custom_call_target="tpu_custom_call" | custom-call | tf_op jit(solution)/shard_map/spread_tables/pallas_call | solution.py:175
  91.8 42.2 %gather_fusion = bf16[8192,768]{1,0:T(8,128)(2,1)} fusion(bf16[3840,768]{1,0:T(8,128)(2,1)} %bitcast.243, s32[8192]{0:T(1024)S(1)} %broadcast_clamp_fusion), kind=kCustom, calls=%fused_computation | custom fusion | bytes 25198592 | tf_op jit(solution)/shard_map/gather | solution.py:1459
  136.6 49.8 %spread_tables.3 = bf16[4,2,480,768]{3,2,1,0:T(8,128)(2,1)} custom-call(bf16[2,480,768]{2,1,0:T(8,128)(2,1)} %bitcast.256), custom_call_target="tpu_custom_call" | custom-call | tf_op jit(solution)/shard_map/spread_tables/pallas_call | solution.py:175
  186.3 40.5 %gather_fusion.1 = bf16[8192,768]{1,0:T(8,128)(2,1)} fusion(bf16[3840,768]{1,0:T(8,128)(2,1)} %bitcast.241, s32[8192]{0:T(1024)S(1)} %broadcast_clamp_fusion), kind=kCustom, calls=%fused_computation.1 | custom fusion | bytes 25198592 | tf_op jit(solution)/shard_map/gather | solution.py:1468
  235.9 81.8 %gather_weights.1 = (bf16[4,8,2,64,768]{4,3,2,1,0:T(8,128)(2,1)}, bf16[4,8,2,48,768]{4,3,2,1,0:T(8,128)(2,1)}, bf16[4,8,2,48,768]{4,3,2,1,0:T(8,128)(2,1)}) custom-call(bf16[2,64,768]{2,1,0:T(8,128)(2,1)} %bitcast.309, bf16[2,48,768]{2,1,0:T(8,128)(2,1)} %bitcast.310, bf16[2,48,768]{2,1,0:T(8,128)(2,1)} %bitcast.311), custom_call_target="tpu_custom_call" | custom-call | tf_op jit(solution)/shard_map/gather_weights/pallas_call | solution.py:381
  338.6 18.6 %attend.2 = bf16[2,512,768]{2,1,0:T(8,128)(2,1)} custom-call(s32[2]{0:T(128)} %lengths.5, bf16[2,512,2304]{2,1,0:T(8,128)(2,1)} %add_convert_fusion.1.q_ref.k_ref.v_ref, bf16[2,512,2304]{2,1,0:T(8,128)(2,1)} %add_convert_fusion.1.q_ref.k_ref.v_ref, bf16[2,512,2304]{2,1,0:T(8,128)(2,1)} %add_convert_fusion.1.q_ref.k_ref.v_ref), custom_call_target="tpu_custom_call" | custom-call | flops 1610612736 | bytes 6291456 | tf_op jit(solution)/shard_map/attend/pallas_call | solution.py:1007
  363.3 11.3 %multiply_convert_fusion.2 = (bf16[2,512,3072]{2,1,0:T(8,128)(2,1)S(1)}, f32[2,512,3072]{2,1,0:T(8,128)}) fusion(f32[3072]{0:T(1024)S(1)} %add.500, bf16[2,512,768]{2,1,0:T(8,128)(2,1)S(1)} %fusion.16, bf16[768,768]{1,0:T(8,128)(2,1)S(1)} %bitcast.299, bf16[768,768]{1,0:T(8,128)(2,1)S(1)} %bitcast.301, bf16[768,768]{1,0:T(8,128)(2,1)S(1)} %bitcast.303, ...), kind=kOutput, calls=%fused_computation.10 | convolution fusion | flops 4869586944 | bytes 25178112 | tf_op jit(solution)/shard_map/bsd,df->bsf/dot_general | solution.py:1091
  415.0 18.6 %attend.3 = bf16[2,512,768]{2,1,0:T(8,128)(2,1)} custom-call(s32[2]{0:T(128)} %lengths.5, bf16[2,512,2304]{2,1,0:T(8,128)(2,1)} %add_convert_fusion.q_ref.k_ref.v_ref, bf16[2,512,2304]{2,1,0:T(8,128)(2,1)} %add_convert_fusion.q_ref.k_ref.v_ref, bf16[2,512,2304]{2,1,0:T(8,128)(2,1)} %add_convert_fusion.q_ref.k_ref.v_ref), custom_call_target="tpu_custom_call" | custom-call | flops 1610612736 | bytes 6291456 | tf_op jit(solution)/shard_map/attend/pallas_call | solution.py:1007
  461.2 14.1 %student_logits.1 = (f32[3840,1024]{1,0:T(8,128)}, f32[4,1024]{1,0:T(4,128)S(1)}) custom-call(bf16[1024,768]{1,0:T(8,128)(2,1)S(1)} %copy-done.3, bf16[3840,768]{1,0:T(8,128)(2,1)S(1)} %bitcast.245, s32[1,1024]{1,0:T(1,128)S(1)} %compare_select_fusion.4.target), custom_call_target="tpu_custom_call" | custom-call | flops 6039797760 | bytes 21626880 | tf_op jit(solution)/shard_map/student_logits/pallas_call | solution.py:904
  475.3 10.2 %all-gather.8.cloned.1.call-done.rows = bf16[1024,768]{1,0:T(8,128)(2,1)} async-done(((bf16[128,768]{1,0:T(8,128)(2,1)}), bf16[1024,768]{1,0:T(8,128)(2,1)}) %all-gather.8.cloned.1.call-update) | async-done | bytes 1572880 | tf_op jit(solution)/shard_map/all_gather | solution.py:1513
  489.6 17.6 %teacher_logits.1 = (f32[3840,1024]{1,0:T(8,128)}, f32[4,1024]{1,0:T(4,128)S(1)}) custom-call(bf16[1024,768]{1,0:T(8,128)(2,1)S(1)} %copy-done.2, bf16[3840,768]{1,0:T(8,128)(2,1)S(1)} %bitcast.242, f32[3840,1024]{1,0:T(8,128)} %get-tuple-element.91.student), custom_call_target="tpu_custom_call" | custom-call | flops 6039797760 | bytes 21626880 | tf_op jit(solution)/shard_map/teacher_logits/pallas_call | solution.py:904
  507.8 9.3 share_small.1
  519.2 22.7 %logits_back.1 = (bf16[3840,1024]{1,0:T(8,128)(2,1)}, bf16[1024,768]{1,0:T(8,128)(2,1)}) custom-call(f32[3840,1024]{1,0:T(8,128)} %get-tuple-element.91.student, f32[3840,1024]{1,0:T(8,128)} %get-tuple-element.99.teacher, bf16[3840,768]{1,0:T(8,128)(2,1)} %bitcast.244, f32[4,1024]{1,0:T(4,128)S(1)} %pad_maximum_fusion.6.consts, ...), custom_call_target="tpu_custom_call" | custom-call | flops 6039797760 | bytes 45219840 | tf_op jit(solution)/shard_map/logits_back/pallas_call | solution.py:960
  546.2 12.5 %fusion.124 = f32[3840,768]{1,0:T(8,128)} fusion(bf16[3840,1024]{1,0:T(8,128)(2,1)} %get-tuple-element.103, bf16[1024,768]{1,0:T(8,128)(2,1)S(1)} %copy-done.4), kind=kOutput, calls=%fused_computation.335 | convolution fusion | flops 6039797760 | bytes 21233664 | tf_op jit(solution)/shard_map/vp,pd->vd/dot_general | solution.py:1091
  558.6 18.1 %reduce-scatter.8.cloned.1.call-done = bf16[128,768]{1,0:T(8,128)(2,1)} async-done(((bf16[1024,768]{1,0:T(8,128)(2,1)}), bf16[128,768]{1,0:T(8,128)(2,1)}) %reduce-scatter.8.cloned.1.call-update) | async-done | bytes 196624 | tf_op jit(solution)/shard_map/reduce_scatter | solution.py:1334
  581.6 14.2 %fusion.123 = (bf16[3072]{0:T(1024)(128)(2,1)S(1)}, bf16[2,512,3072]{2,1,0:T(8,128)(2,1)}) fusion(f32[2,512,3072]{2,1,0:T(8,128)} %get-tuple-element.427, f32[3072]{0:T(1024)S(1)} %add.500, bf16[2,512,768]{2,1,0:T(8,128)(2,1)S(1)} %get-tuple-element.116, bf16[3072,768,1]{1,0,2:T(8,128)(2,1)S(1)} %bitcast.326), kind=kOutput, calls=%fused_computation.334 | convolution fusion | flops 4875875328 | bytes 25184256 | tf_op jit(solution)/shard_map/bsd,fd->bsf/dot_general | solution.py:1091
  595.8 8.8 multiply_reduce_fusion.4
  610.1 29.5 %attend_back.1 = bf16[3,2,512,768]{3,2,1,0:T(8,128)(2,1)} custom-call(s32[2]{0:T(128)} %lengths.5, bf16[2,512,2304]{2,1,0:T(8,128)(2,1)} %add_convert_fusion.1.q_ref.k_ref.v_ref, bf16[2,512,2304]{2,1,0:T(8,128)(2,1)} %add_convert_fusion.1.q_ref.k_ref.v_ref, bf16[2,512,2304]{2,1,0:T(8,128)(2,1)} %add_convert_fusion.1.q_ref.k_ref.v_ref, ...), custom_call_target="tpu_custom_call" | custom-call | flops 4026531840 | bytes 11010048 | tf_op jit(solution)/shard_map/attend_back/pallas_call | solution.py:1068
  645.0 8.1 multiply_reduce_fusion.2
  663.8 7.8 bitcast_convert_fusion.2
  698.5 115.0 %reduce_weights.1 = f32[2,2,80,768]{3,2,1,0:T(8,128)} custom-call(bf16[4,8,2,2,80,768]{5,4,3,2,1,0:T(8,128)(2,1)} %bitcast.85.g), custom_call_target="tpu_custom_call" | custom-call | tf_op jit(solution)/shard_map/reduce_weights/pallas_call | solution.py:632
  815.5 74.9 %fold_table.1 = (f32[2,480,768]{2,1,0:T(8,128)}, f32[1,768]{1,0:T(1,128)}) custom-call(s32[4,1,2048]{2,1,0:T(1,128)} %reshape_reshape.6.ids, bf16[8192,768]{1,0:T(8,128)(2,1)} %bitcast.250, f32[4,2,480,768]{3,2,1,0:T(8,128)} %bitcast.251), custom_call_target="tpu_custom_call" | custom-call | tf_op jit(solution)/shard_map/fold_table/pallas_call | solution.py:742
  893.8 9.9 %total.1 = f32[8,128]{1,0:T(8,128)} custom-call(f32[8,128]{1,0:T(8,128)} %broadcast_in_dim.176.x), custom_call_target="tpu_custom_call" | custom-call | tf_op jit(solution)/shard_map/total/pallas_call | solution.py:823
  916.1 8.0 multiply_add_fusion.7
  (388 shorter events, 194.6 us)
Async XLA Ops:
  8.1 218.8 %all-gather.12.cloned.1.call-start = ((), (), s32[]{:S(2)}) async-start(), calls=%async_computation.9 | async-start | bytes 16220160 | tf_op jit(solution)/shard_map/all_gather | solution.py:1457
  12.1 314.8 %reduce-scatter.4.cloned.1.call-start = ((), (), s32[]{:S(2)}) async-start(), calls=%async_computation.3 | async-start | bytes 14155776 | tf_op jit(solution)/shard_map/reduce_scatter | solution.py:1462
  91.6 42.4 %copy-start.46 = (s32[16,640]{1,0:T(8,128)}, s32[16,640]{1,0:T(8,128)S(1)}, u32[]{:S(2)}) copy-start(s32[16,640]{1,0:T(8,128)S(1)} %reshape.686) | copy-start | bytes 122884
  134.0 268.0 %reduce-scatter.6.cloned.1.call-start = ((), (), s32[]{:S(2)}) async-start(), calls=%async_computation.4 | async-start | bytes 14155776 | tf_op jit(solution)/shard_map/reduce_scatter | solution.py:1472
  226.9 230.2 %all-gather.6.cloned.1.call-start = ((), (), s32[]{:S(2)}) async-start(), calls=%async_computation.5 | async-start | bytes 1769472 | tf_op jit(solution)/shard_map/all_gather | solution.py:1509
  324.4 32.8 %copy-start.5 = (f32[512,768]{1,0:T(8,128)}, f32[512,768]{1,0:T(8,128)S(1)}, u32[]{:S(2)}) copy-start(f32[512,768]{1,0:T(8,128)S(1)} %copy.209) | copy-start | bytes 4718596
  326.9 30.4 %copy-start.54 = (f32[768]{0:T(1024)}, f32[768]{0:T(1024)S(1)}, u32[]{:S(2)}) copy-start(f32[768]{0:T(1024)S(1)} %get-tuple-element.321) | copy-start | bytes 9220
  326.9 30.4 %copy-start.56 = (f32[768]{0:T(1024)}, f32[768]{0:T(1024)S(1)}, u32[]{:S(2)}) copy-start(f32[768]{0:T(1024)S(1)} %get-tuple-element.322) | copy-start | bytes 9220
  326.9 30.4 %copy-start.60 = (f32[768]{0:T(1024)}, f32[768]{0:T(1024)S(1)}, u32[]{:S(2)}) copy-start(f32[768]{0:T(1024)S(1)} %get-tuple-element.320) | copy-start | bytes 9220
  329.3 28.0 %copy-start.58 = (f32[2,512]{1,0:T(2,128)}, f32[2,512]{1,0:T(2,128)S(1)}, u32[]{:S(2)}) copy-start(f32[2,512]{1,0:T(2,128)S(1)} %broadcast_multiply_fusion.11) | copy-start | bytes 12292
  330.3 26.9 %copy-start.62 = (f32[2,512]{1,0:T(2,128)}, f32[2,512]{1,0:T(2,128)S(1)}, u32[]{:S(2)}) copy-start(f32[2,512]{1,0:T(2,128)S(1)} %add_rsqrt_fusion.5) | copy-start | bytes 12292
  404.7 80.8 %all-gather.8.cloned.1.call-start = ((), (), s32[]{:S(2)}) async-start(), calls=%async_computation.6 | async-start | bytes 1769472 | tf_op jit(solution)/shard_map/all_gather | solution.py:1513
  453.8 122.9 %reduce-scatter.8.cloned.1.call-start = ((), (), s32[]{:S(2)}) async-start(), calls=%async_computation.7 | async-start | bytes 1769472 | tf_op jit(solution)/shard_map/reduce_scatter | solution.py:1334
  519.2 23.8 %copy-start.69 = (s32[2]{0:T(128)S(1)}, s32[2]{0:T(128)}, u32[]{:S(2)}) copy-start(s32[2]{0:T(128)} %lengths.5) | copy-start | bytes 28
  519.2 27.0 %copy-start.4 = (bf16[1024,768]{1,0:T(8,128)(2,1)S(1)}, bf16[1024,768]{1,0:T(8,128)(2,1)}, u32[]{:S(2)}) copy-start(bf16[1024,768]{1,0:T(8,128)(2,1)} %all-gather.6.cloned.1.call-done.rows) | copy-start | bytes 4718596
  541.9 273.6 %all-gather.10.cloned.1.call-start = ((), (), s32[]{:S(2)}) async-start(), calls=%async_computation.8 | async-start | bytes 14155776 | tf_op jit(solution)/shard_map/all_gather | solution.py:1557
  581.5 14.3 %copy-start.16 = (bf16[2,512,768]{2,1,0:T(8,128)(2,1)}, bf16[2,512,768]{2,1,0:T(8,128)(2,1)S(1)}, u32[]{:S(2)}) copy-start(bf16[2,512,768]{2,1,0:T(8,128)(2,1)S(1)} %get-tuple-element.116) | copy-start | bytes 4718596
  581.6 14.2 %copy-start.38 = (bf16[32,24,768]{2,1,0:T(8,128)(2,1)S(1)}, bf16[32,24,768]{2,1,0:T(8,128)(2,1)}, u32[]{:S(2)}) copy-start(bf16[32,24,768]{2,1,0:T(8,128)(2,1)} %copy-done.37) | copy-start | bytes 3538948
  581.6 14.2 %copy-start.40 = (bf16[32,24,768]{2,1,0:T(8,128)(2,1)S(1)}, bf16[32,24,768]{2,1,0:T(8,128)(2,1)}, u32[]{:S(2)}) copy-start(bf16[32,24,768]{2,1,0:T(8,128)(2,1)} %copy-done.39) | copy-start | bytes 3538948
  581.6 14.2 %copy-start.42 = (bf16[32,24,768]{2,1,0:T(8,128)(2,1)S(1)}, bf16[32,24,768]{2,1,0:T(8,128)(2,1)}, u32[]{:S(2)}) copy-start(bf16[32,24,768]{2,1,0:T(8,128)(2,1)} %copy-done.41) | copy-start | bytes 3538948
  815.5 98.5 %copy-start.43 = (f32[96,768]{1,0:T(8,128)S(1)}, f32[96,768]{1,0:T(8,128)}, u32[]{:S(2)}) copy-start(f32[96,768]{1,0:T(8,128)} %refs_0_.4) | copy-start | bytes 884740
  815.5 98.5 %copy-start.48 = (f32[96,768]{1,0:T(8,128)S(1)}, f32[96,768]{1,0:T(8,128)}, u32[]{:S(2)}) copy-start(f32[96,768]{1,0:T(8,128)} %param.63) | copy-start | bytes 884740
  890.4 25.7 %copy-start.15 = (f32[956,768]{1,0:T(8,128)S(1)}, f32[956,768]{1,0:T(8,128)}, u32[]{:S(2)}) copy-start(f32[956,768]{1,0:T(8,128)} %param.38) | copy-start | bytes 8810500
  907.9 16.3 %copy-start.64 = (f32[16,24]{1,0:T(8,128)}, f32[16,24]{1,0:T(8,128)S(1)}, u32[]{:S(2)}) copy-start(f32[16,24]{1,0:T(8,128)S(1)} %copy.227) | copy-start | bytes 4612
  (73 other events, 356.6 us)
Sparse Core Ops, SparseCore 0:
  12.5 130.2 all-gather.11
Sparse Core Ops, SparseCore 1:
  134.1 136.8 reduce-scatter.3
  273.2 128.8 reduce-scatter.5
  404.7 31.6 all-gather.5
  453.8 31.6 all-gather.7
  542.0 34.6 reduce-scatter.7
  656.6 120.4 all-gather.9
